TPU v7x, 512 devices: a whole 4x8x8 slice. The times are simulated.
512 devices in a mesh: st: 64 (over z, x, core), tile: 8 (over y).
Axes of the slice: x: 4, y: 8, z: 8, core: 2. Of those that a mesh axis runs over, the one named last changes fastest.
Arguments:
- grid: bfloat16 [8, 2048, 128], P(None, 'tile'), may hold values from -6 to 6
- a_terms: float32 [512, 2, 4, 1024], P('st'), may hold values from -5 to 5
- stations: int32 [4096, 2], P(('st', 'tile')), may hold values from 0 to 511, as said below
- intervals: int32 [4096], P(('st', 'tile')), may hold values from 0 to 1
- offsets: int32 [4096, 2], P(('st', 'tile')), may hold values from 0 to 2016, as said below
- uv: float32 [4096, 2, 512], P(('st', 'tile')), may hold values from -12 to 12
- observed: float32 [4096, 8, 512], P(('st', 'tile')), may hold values from -6 to 6
- flags: int32 [4096, 512], P(('st', 'tile')), may hold values 0 or 1
Outputs:
- residual: float32 [4096, 8, 512], P(('st', 'tile'))
- a_grad: float32 [512, 2, 4, 1024], P('st')
Inputs may be any that keep to these rules, and one draw needn't show every extreme that they name: Among the 8 subgrids of one device, at most 2 station ends (first and second stations together) lie in one block of 8 consecutive stations starting at a multiple of 8, and some such block gets exactly 2; the two stations of a subgrid differ. `offsets`: column 0 is the grid row, column 1 the grid column of the corner. A subgrid's 32 rows lie inside one block of 256 consecutive rows starting at a multiple of 256, and its columns inside the strip. Among the 8 subgrids of one device at most 2 lie in one such block, and some block gets exactly 2.
All inputs are finite; a program needn't handle non-finite values. No bound on the sum of `flags` on one device may be relied on, other than what follows from the above.
Results may differ from a plain program's by a relative error of at most 0.0003.
Values may be sent and summed in bfloat16 or wider, within the bound.
No kernel may reach another device: no remote copies, remote signals or barrier semaphores. Data moves between devices by JAX's collectives and lax.ppermute only.
A program may use at most 64 MiB of HBM per device.

v0:
```python
import jax
import jax.numpy as jnp
from jax import lax
from jax.sharding import PartitionSpec as P

SUBSIZE = 32


HIGH = lax.Precision.HIGHEST


def tables(side):
    index = jnp.arange(side, dtype=jnp.float32)
    angle = 2.0 * jnp.pi * index[:, None] * index[None, :] / side
    f_real = jnp.cos(angle) / side
    f_imag = jnp.sin(angle) / side
    edge = jnp.cos(jnp.pi * (index - (side - 1) / 2.0) / side)
    return (f_real, f_imag, edge[:, None] * edge[None, :])


def predict_residual(patches, a_p, a_q, coords, observed, flags):
    side = SUBSIZE
    count = patches.shape[0]
    f_real, f_imag, taper = tables(side)
    g_re = patches[:, :4].reshape(count, 4, side, side)
    g_im = patches[:, 4:].reshape(count, 4, side, side)
    x_re = jnp.einsum("la,bpam->bplm", f_real, g_re, precision=HIGH) - jnp.einsum(
        "la,bpam->bplm", f_imag, g_im, precision=HIGH
    )
    x_im = jnp.einsum("la,bpam->bplm", f_real, g_im, precision=HIGH) + jnp.einsum(
        "la,bpam->bplm", f_imag, g_re, precision=HIGH
    )
    i_re = jnp.einsum("bplk,mk->bplm", x_re, f_real, precision=HIGH) - jnp.einsum(
        "bplk,mk->bplm", x_im, f_imag, precision=HIGH
    )
    i_im = jnp.einsum("bplk,mk->bplm", x_re, f_imag, precision=HIGH) + jnp.einsum(
        "bplk,mk->bplm", x_im, f_real, precision=HIGH
    )
    i_re = i_re.reshape(count, 2, 2, side, side)
    i_im = i_im.reshape(count, 2, 2, side, side)
    p_re = a_p[:, 0:2].reshape(count, 2, 1, side, side)
    p_im = a_p[:, 2:4].reshape(count, 2, 1, side, side)
    q_re = a_q[:, 0:2].reshape(count, 1, 2, side, side)
    q_im = a_q[:, 2:4].reshape(count, 1, 2, side, side)
    y_re = i_re * q_re + i_im * q_im
    y_im = i_im * q_re - i_re * q_im
    z_re = ((p_re * y_re - p_im * y_im) * taper).reshape(count, 4, side, side)
    z_im = ((p_re * y_im + p_im * y_re) * taper).reshape(count, 4, side, side)
    zt_re = z_re.transpose(0, 3, 1, 2).reshape(count, side, 4 * side)
    zt_im = z_im.transpose(0, 3, 1, 2).reshape(count, side, 4 * side)
    centre = jnp.arange(side, dtype=jnp.float32) - side / 2.0
    phase_u = 2.0 * jnp.pi * coords[:, 0, :, None] * centre / side
    phase_v = 2.0 * jnp.pi * coords[:, 1, :, None] * centre / side
    eu_re, eu_im = (jnp.cos(phase_u), jnp.sin(phase_u))
    ev_re, ev_im = (jnp.cos(phase_v), jnp.sin(phase_v))
    w_re = jnp.einsum("bvm,bmq->bvq", ev_re, zt_re, precision=HIGH) - jnp.einsum(
        "bvm,bmq->bvq", ev_im, zt_im, precision=HIGH
    )
    w_im = jnp.einsum("bvm,bmq->bvq", ev_re, zt_im, precision=HIGH) + jnp.einsum(
        "bvm,bmq->bvq", ev_im, zt_re, precision=HIGH
    )
    vcount = coords.shape[2]
    w_re = w_re.reshape(count, vcount, 4, side)
    w_im = w_im.reshape(count, vcount, 4, side)
    eu_re = eu_re[:, :, None, :]
    eu_im = eu_im[:, :, None, :]
    v_re = jnp.sum(eu_re * w_re - eu_im * w_im, axis=-1)
    v_im = jnp.sum(eu_re * w_im + eu_im * w_re, axis=-1)
    model = jnp.concatenate([v_re, v_im], axis=-1).transpose(0, 2, 1)
    return flags[:, None, :].astype(jnp.float32) * (observed - model)


def cut_patch(source, row, column):
    start = jnp.zeros((), jnp.int32)
    piece = lax.dynamic_slice(source, (start, row, column), (8, SUBSIZE, SUBSIZE))
    return piece.reshape(8, SUBSIZE * SUBSIZE)


def earlier_same(owner):
    count = owner.shape[0]
    positions = jnp.arange(count, dtype=jnp.int32)
    same = owner[:, None] == owner[None, :]
    before = positions[:, None] > positions[None, :]
    return jnp.sum((same & before).astype(jnp.int32), axis=1)


def body(grid, a_terms, stations, intervals, offsets, uv, observed, flags):
    subs = stations.shape[0]
    pixels = SUBSIZE * SUBSIZE
    n_st = lax.axis_size("st")
    sta_dev = a_terms.shape[0]
    n_int = a_terms.shape[1]
    cap = 2 * max(1, 2 * subs // n_st)
    strip = lax.all_gather(grid, "tile", axis=1, tiled=True)
    patches = jax.vmap(cut_patch, in_axes=(None, 0, 0))(strip, offsets[:, 0], offsets[:, 1])
    end_station = jnp.concatenate([stations[:, 0], stations[:, 1]])
    end_interval = jnp.concatenate([intervals, intervals])
    st_owner = end_station // sta_dev
    local_screen = end_station % sta_dev * n_int + end_interval
    st_slot = st_owner * cap + earlier_same(st_owner)
    asked = jnp.zeros((n_st * cap,), jnp.int32).at[st_slot].set(local_screen).reshape(n_st, cap)
    screens = a_terms.reshape(sta_dev * n_int, 4, pixels)
    screen_ids = lax.all_to_all(asked, "st", split_axis=0, concat_axis=0, tiled=True)
    found = screens[screen_ids]
    got = lax.all_to_all(found, "st", split_axis=0, concat_axis=0, tiled=True)
    end_screens = got.reshape(n_st * cap, 4, pixels)[st_slot]
    a_first = end_screens[:subs]
    a_second = end_screens[subs:]
    block = min(subs, 8)
    blocks = subs // block

    def as_blocks(array):
        return array.reshape((blocks, block) + array.shape[1:])

    def run_block(item):
        patch_block, first, second, coords, seen, usable = item
        patch_block = patch_block.astype(jnp.float32)

        def forward(left, right):
            return predict_residual(patch_block, left, right, coords, seen, usable)

        result, pullback = jax.vjp(forward, first, second)
        grad_first, grad_second = pullback(result)
        return (result, grad_first, grad_second)

    result, grad_first, grad_second = lax.map(
        run_block, tuple((as_blocks(a) for a in (patches, a_first, a_second, uv, observed, flags)))
    )
    result = result.reshape(subs, 8, uv.shape[2])
    end_grads = jnp.concatenate(
        [grad_first.reshape(subs, 4, pixels), grad_second.reshape(subs, 4, pixels)]
    )
    outgoing = jnp.zeros((n_st * cap, 4, pixels), jnp.float32).at[st_slot].set(end_grads)
    outgoing = outgoing.reshape(n_st, cap, 4, pixels)
    incoming = lax.all_to_all(outgoing, "st", split_axis=0, concat_axis=0, tiled=True)
    selector = (
        screen_ids.reshape(-1)[:, None] == jnp.arange(sta_dev * n_int, dtype=jnp.int32)[None, :]
    ).astype(jnp.float32)
    partial_grad = jnp.einsum(
        "rs,rkn->skn", selector, incoming.reshape(n_st * cap, 4, pixels), precision=HIGH
    )
    total = lax.psum(partial_grad, "tile")
    return (result, total.reshape(sta_dev, n_int, 4, pixels))


def solution(mesh):
    placed = (
        P(None, "tile", None),
        P("st", None, None, None),
        P(("st", "tile"), None),
        P(("st", "tile")),
        P(("st", "tile"), None),
        P(("st", "tile"), None, None),
        P(("st", "tile"), None, None),
        P(("st", "tile"), None),
    )
    return jax.shard_map(
        body,
        mesh=mesh,
        in_specs=placed,
        out_specs=(P(("st", "tile"), None, None), P("st", None, None, None)),
        check_vma=False,
    )
```

profile of v0, /device:TPU:2, one launch (start us, length us, event | category | flops | bytes accessed | tf_op | source)
XLA Modules:
  0.0 327.0 jit_solution(524868472120936685)
XLA Ops:
  10.6 22.3 %all_to_all.22 = s32[64,1,2]{2,1,0:T(1,128)S(1)} all-to-all(s32[64,1,2]{2,1,0:T(1,128)S(1)} %bitcast.151), channel_id=1, replica_groups=mesh['st'=64,'tile'=8] {'st'}, dimensions={0} | all-to-all | bytes 1024 | tf_op jit(solution)/shard_map/all_to_all | solution.py:103
  33.6 3.0 gather_fusion
  36.7 7.2 %all-to-all-start.1 = ((f32[64,2,4,1024]{3,2,1,0:T(4,128)}), f32[64,2,4,1024]{3,2,1,0:T(4,128)}, u32[]{:S(2)}, u32[]{:S(2)}) async-start(f32[64,2,4,1024]{3,2,1,0:T(4,128)} %bitcast.9), calls=%async_computation.1 | async-start | bytes 4194304 | tf_op jit(solution)/shard_map/all_to_all | solution.py:105
  44.2 1.9 fusion.22
  46.1 48.9 %all-to-all-done.1 = f32[64,2,4,1024]{3,2,1,0:T(4,128)} async-done(((f32[64,2,4,1024]{3,2,1,0:T(4,128)}), f32[64,2,4,1024]{3,2,1,0:T(4,128)}, u32[]{:S(2)}, u32[]{:S(2)}) %all-to-all-start.1) | async-done | bytes 2097184 | tf_op jit(solution)/shard_map/all_to_all | solution.py:105
  95.0 2.3 gather_fusion.1
  98.1 23.6 %while.1 = (s32[]{:T(128)}, bf16[8,2048,128]{2,1,0:T(8,128)(2,1)}, s32[8,3]{0,1:T(4,128)S(1)}, bf16[8,8,32,32]{3,2,1,0:T(8,128)(2,1)S(1)}, s32[]{:T(128)}) while((s32[]{:T(128)}, bf16[8,2048,128]{2,1,0:T(8,128)(2,1)}, s32[8,3]{0,1:T(4,128)S(1)}, bf16[8,8,32,32]{3,2,1,0:T(8,128)(2,1)S(1)}, s32[]{:T(128)}) %tuple.54), condition=%wide.while_cond, body=%wide.while_body.sunk | while | flops 2 | bytes 82037 | solution.py:75
  98.8 2.3 bitcast_dynamic-update-slice_fusion.2
  101.7 2.3 bitcast_dynamic-update-slice_fusion.2
  104.7 2.3 bitcast_dynamic-update-slice_fusion.2
  107.6 2.3 bitcast_dynamic-update-slice_fusion.2
  110.6 2.3 bitcast_dynamic-update-slice_fusion.2
  113.5 2.3 bitcast_dynamic-update-slice_fusion.2
  116.5 2.3 bitcast_dynamic-update-slice_fusion.2
  119.4 2.3 bitcast_dynamic-update-slice_fusion.2
  128.2 1.9 subtract_multiply_fusion
  130.3 4.0 %fusion.12 = f32[8,512,128]{1,2,0:T(8,128)S(1)} fusion(f32[8,32,128]{1,2,0:T(8,128)S(1)} %bitcast.138, f32[8,512]{1,0:T(8,128)S(1)} %get-tuple-element.93, f32[32]{0:T(128)S(1)} %iota_add_fusion), kind=kOutput, calls=%fused_computation.42 | convolution fusion | flops 201588736 | bytes 2244736 | tf_op jit(solution)/shard_map/while/body/eval_jaxpr/jvp(bvm,bmq->bvq)/dot_general | solution.py:59
  134.3 3.8 %fusion.14 = f32[8,512,128]{1,2,0:T(8,128)S(1)} fusion(f32[8,32,128]{1,2,0:T(8,128)S(1)} %bitcast.136, f32[8,512]{1,0:T(8,128)S(1)} %get-tuple-element.93, f32[32]{0:T(128)S(1)} %iota_add_fusion), kind=kOutput, calls=%fused_computation.43 | convolution fusion | flops 201588736 | bytes 2244736 | tf_op jit(solution)/shard_map/while/body/eval_jaxpr/jvp(bvm,bmq->bvq)/dot_general | solution.py:56
  138.1 3.8 %convolution_subtract_fusion = f32[8,512,128]{1,2,0:T(8,128)S(1)} fusion(f32[8,512,128]{1,2,0:T(8,128)S(1)} %fusion.14, f32[8,32,128]{1,2,0:T(8,128)S(1)} %bitcast.139, f32[8,512]{1,0:T(8,128)S(1)} %get-tuple-element.93, f32[32]{0:T(128)S(1)} %iota_add_fusion), kind=kOutput, calls=%fused_computation.13 | convolution fusion | flops 202113024 | bytes 4341888 | tf_op jit(solution)/shard_map/while/body/eval_jaxpr/jvp(bvm,bmq->bvq)/dot_general | solution.py:56
  142.0 5.0 %subtract_reduce_fusion = (f32[8,512,4]{1,2,0:T(4,128)S(1)}, f32[8,512,4]{1,2,0:T(4,128)S(1)}) fusion(f32[8,512,32]{1,2,0:T(8,128)S(1)} %get-tuple-element.85, f32[8,512,32]{1,2,0:T(8,128)S(1)} %get-tuple-element.84, f32[8,512,128]{1,2,0:T(8,128)S(1)} %convolution_subtract_fusion, f32[8,512,128]{1,2,0:T(8,128)S(1)} %fusion.12, ...), kind=kOutput, calls=%fused_computation.11 | convolution fusion | flops 206274560 | bytes 5521536 | tf_op jit(solution)/shard_map/while/body/eval_jaxpr/jvp(bvm,bmq->bvq)/dot_general | solution.py:59
  149.3 3.8 %fusion.10 = f32[8,32,128]{2,1,0:T(8,128)S(1)} fusion(f32[8,512,128]{1,2,0:T(8,128)S(1)} %bitcast.129, f32[8,512]{1,0:T(8,128)S(1)} %get-tuple-element.93, f32[32]{0:T(128)S(1)} %iota_add_fusion), kind=kOutput, calls=%fused_computation.41 | convolution fusion | flops 201588736 | bytes 2244736 | tf_op jit(solution)/shard_map/while/body/eval_jaxpr/transpose(jvp(bvm,bmq->bvq))/dot_general | solution.py:59
  153.1 4.5 %fusion.16 = f32[8,32,128]{2,1,0:T(8,128)S(1)} fusion(f32[8,512,128]{1,2,0:T(8,128)S(1)} %bitcast.130, f32[8,512]{1,0:T(8,128)S(1)} %get-tuple-element.93, f32[32]{0:T(128)} %copy-done.18), kind=kOutput, calls=%fused_computation.44 | convolution fusion | flops 201588736 | bytes 2244736 | tf_op jit(solution)/shard_map/while/body/eval_jaxpr/transpose(jvp(bvm,bmq->bvq))/dot_general | solution.py:59
  157.6 3.9 %fusion.4 = f32[8,32,128]{2,1,0:T(8,128)S(1)} fusion(f32[8,32,128]{2,1,0:T(8,128)S(1)} %fusion.10, f32[8,512,128]{1,2,0:T(8,128)S(1)} %bitcast.127, f32[8,512]{1,0:T(8,128)S(1)} %get-tuple-element.93, f32[32]{0:T(128)S(1)} %copy-done.19), kind=kOutput, calls=%fused_computation.20 | convolution fusion | flops 202145792 | bytes 2375808 | tf_op jit(solution)/shard_map/while/body/eval_jaxpr/transpose(jvp(bvm,bmq->bvq))/dot_general | solution.py:56
  163.8 5.4 %convolution_add_fusion.3 = f32[8,32,128]{2,1,0:T(8,128)} fusion(f32[8,32,128]{2,1,0:T(8,128)S(1)} %fusion.16, f32[8,512,128]{1,2,0:T(8,128)S(1)} %bitcast.128, f32[8,512]{1,0:T(8,128)S(1)} %get-tuple-element.93, f32[32]{0:T(128)} %copy-done.18), kind=kOutput, calls=%fused_computation.21 | convolution fusion | flops 201621504 | bytes 2375808 | tf_op jit(solution)/shard_map/while/body/eval_jaxpr/transpose(jvp(bvm,bmq->bvq))/dot_general | solution.py:56
  172.0 1.8 multiply_reduce_fusion.6
  177.5 3.2 copy.104
  180.8 5.6 %all-to-all-start.2 = ((f32[64,2,4,1024]{3,1,2,0:T(2,128)}), f32[64,2,4,1024]{3,1,2,0:T(2,128)S(1)}, u32[]{:S(2)}, u32[]{:S(2)}) async-start(f32[64,2,4,1024]{3,1,2,0:T(2,128)} %copy.104), calls=%async_computation.2 | async-start | bytes 4194304 | tf_op jit(solution)/shard_map/all_to_all | solution.py:135
  187.8 49.8 %all-to-all-done.2 = f32[64,2,4,1024]{3,1,2,0:T(2,128)S(1)} async-done(((f32[64,2,4,1024]{3,1,2,0:T(2,128)}), f32[64,2,4,1024]{3,1,2,0:T(2,128)S(1)}, u32[]{:S(2)}, u32[]{:S(2)}) %all-to-all-start.2) | async-done | bytes 2097184 | tf_op jit(solution)/shard_map/all_to_all | solution.py:135
  237.6 2.1 copy.105
  239.8 2.7 reshape.549
  244.2 74.0 %all-reduce.6.cloned.1.call-done = f32[8,2,4,1024]{3,2,1,0:T(4,128)} async-done(((f32[8,2,4,1024]{3,2,1,0:T(4,128)}), f32[8,2,4,1024]{3,2,1,0:T(4,128)}) %all-reduce.6.cloned.1.call-update) | async-done | bytes 262160 | tf_op jit(solution)/shard_map/psum | solution.py:142
  318.2 1.7 copy.151
  (142 shorter events, 31.0 us)
Async XLA Ops:
  7.2 26.5 %copy-start = (f32[8,2,4,1024]{3,2,1,0:T(4,128)S(1)}, f32[8,2,4,1024]{3,2,1,0:T(4,128)}, u32[]{:S(2)}) copy-start(f32[8,2,4,1024]{3,2,1,0:T(4,128)} %param.9) | copy-start | bytes 786436
  7.2 90.9 %all-gather.2.cloned.1.call-start = ((), (), s32[]{:S(2)}) async-start(), calls=%async_computation.3 | async-start | bytes 4718592 | tf_op jit(solution)/shard_map/all_gather | solution.py:94
  9.8 34.2 %copy-start.22 = (s32[16]{0:T(128)}, s32[16]{0:T(128)S(1)}, u32[]{:S(2)}) copy-start(s32[16]{0:T(128)S(1)} %fusion.86) | copy-start | bytes 196
  32.9 0.6 copy-start.15
  36.7 7.2 %copy-start.21 = (s32[8,512]{1,0:T(8,128)S(1)}, s32[8,512]{1,0:T(8,128)}, u32[]{:S(2)}) copy-start(s32[8,512]{1,0:T(8,128)} %param.15) | copy-start | bytes 49156
  36.7 7.3 %copy-start.24 = (s32[8,2]{0,1:T(2,128)S(1)}, s32[8,2]{0,1:T(2,128)}, u32[]{:S(2)}) copy-start(s32[8,2]{0,1:T(2,128)} %param.12) | copy-start | bytes 196
  36.7 7.5 %copy-start.20 = (f32[8,2,512]{2,1,0:T(2,128)S(1)}, f32[8,2,512]{2,1,0:T(2,128)}, u32[]{:S(2)}) copy-start(f32[8,2,512]{2,1,0:T(2,128)} %param.13) | copy-start | bytes 98308
  36.7 58.3 %all-to-all-start.1 = ((f32[64,2,4,1024]{3,2,1,0:T(4,128)}), f32[64,2,4,1024]{3,2,1,0:T(4,128)}, u32[]{:S(2)}, u32[]{:S(2)}) async-start(f32[64,2,4,1024]{3,2,1,0:T(4,128)} %bitcast.9), calls=%async_computation.1 | async-start | bytes 4194304 | tf_op jit(solution)/shard_map/all_to_all | solution.py:105
  44.0 105.2 %copy-start.18 = (f32[32]{0:T(128)}, f32[32]{0:T(128)S(1)}, u32[]{:S(2)}) copy-start(f32[32]{0:T(128)S(1)} %iota_add_fusion) | copy-start | bytes 388
  44.2 85.9 %copy-start.13 = (f32[32,32]{1,0:T(8,128)}, f32[32,32]{1,0:T(8,128)S(1)}, u32[]{:S(2)}) copy-start(f32[32,32]{1,0:T(8,128)S(1)} %broadcast_multiply_fusion) | copy-start | bytes 12292
  46.1 95.8 %copy-start.1 = (f32[8,512,32]{1,2,0:T(8,128)}, f32[8,512,32]{1,2,0:T(8,128)S(1)}, u32[]{:S(2)}) copy-start(f32[8,512,32]{1,2,0:T(8,128)S(1)} %get-tuple-element.85) | copy-start | bytes 1572868
  97.5 30.5 %copy-start.6 = (f32[8,2,32,32]{3,2,1,0:T(8,128)}, f32[8,2,32,32]{3,2,1,0:T(8,128)S(1)}, u32[]{:S(2)}) copy-start(f32[8,2,32,32]{3,2,1,0:T(8,128)S(1)} %mul.531) | copy-start | bytes 196612
  97.7 30.2 %copy-start.7 = (f32[8,2,32,32]{3,2,1,0:T(8,128)}, f32[8,2,32,32]{3,2,1,0:T(8,128)S(1)}, u32[]{:S(2)}) copy-start(f32[8,2,32,32]{3,2,1,0:T(8,128)S(1)} %mul.547) | copy-start | bytes 196612
  97.9 30.1 %copy-start.2 = (f32[8,2,32,32]{3,2,1,0:T(8,128)}, f32[8,2,32,32]{3,2,1,0:T(8,128)S(1)}, u32[]{:S(2)}) copy-start(f32[8,2,32,32]{3,2,1,0:T(8,128)S(1)} %mul.538) | copy-start | bytes 196612
  98.1 30.0 %copy-start.4 = (f32[8,2,32,32]{3,2,1,0:T(8,128)}, f32[8,2,32,32]{3,2,1,0:T(8,128)S(1)}, u32[]{:S(2)}) copy-start(f32[8,2,32,32]{3,2,1,0:T(8,128)S(1)} %mul.542) | copy-start | bytes 196612
  141.9 5.0 %copy-start.17 = (f32[8,8,512]{2,1,0:T(8,128)S(1)}, f32[8,8,512]{2,1,0:T(8,128)}, u32[]{:S(2)}) copy-start(f32[8,8,512]{2,1,0:T(8,128)} %param.14) | copy-start | bytes 393220
  153.1 4.5 %copy-start.19 = (f32[32]{0:T(128)S(1)}, f32[32]{0:T(128)}, u32[]{:S(2)}) copy-start(f32[32]{0:T(128)} %copy-done.18) | copy-start | bytes 388
  169.2 2.7 copy-start.3
  169.2 2.7 copy-start.5
  169.2 2.8 copy-start.8
  169.2 2.8 copy-start.14
  173.7 1.5 copy-start.11
  173.7 1.6 copy-start.12
  173.7 1.8 copy-start.9
  173.7 1.8 copy-start.10
  175.5 0.9 copy-start.23
  180.8 6.2 %copy-start.16 = (s32[64,1,2]{2,1,0:T(1,128)S(1)}, s32[64,1,2]{2,1,0:T(1,128)}, u32[]{:S(2)}) copy-start(s32[64,1,2]{2,1,0:T(1,128)} %copy-done.15) | copy-start | bytes 1540
  180.8 56.9 %all-to-all-start.2 = ((f32[64,2,4,1024]{3,1,2,0:T(2,128)}), f32[64,2,4,1024]{3,1,2,0:T(2,128)S(1)}, u32[]{:S(2)}, u32[]{:S(2)}) async-start(f32[64,2,4,1024]{3,1,2,0:T(2,128)} %copy.104), calls=%async_computation.2 | async-start | bytes 4194304 | tf_op jit(solution)/shard_map/all_to_all | solution.py:135
  186.3 131.8 %all-reduce.6.cloned.1.call-start = ((), (), s32[]{:S(2)}) async-start(), calls=%async_computation.4 | async-start | bytes 524288 | tf_op jit(solution)/shard_map/psum | solution.py:142
Sparse Core Ops, SparseCore 0:
  10.1 61.7 all-gather.1
  244.3 73.8 all-reduce.5
where the time goes:
time: 331 us; the launch traced here: 327 us
  waiting for transfers between devices  173 us (52%)
  local copies, waits for them, and re-layouts  50.3 us (15%)
  matrix products  42 us (13%)
  blocking collectives  22.3 us (7%)
  between operations  15 us (5%)
  starting transfers between devices  12.9 us (4%)
  other arithmetic  11 us (3%)
    psum x1, waiting for transfers between devices, body(): total = lax.psum(partial_grad, 'tile')  74 us
    all_to_all x1, waiting for transfers between devices, body(): lax.all_to_all(outgoing, 'st', split_axis=0, concat_axis=0, tiled=True)  49.8 us
    all_to_all x1, waiting for transfers between devices, body(): got = lax.all_to_all(found, 'st', split_axis=0, concat_axis=0, tiled=True)  48.9 us
    gather x24, local copies, waits for them, and re-layouts  23.5 us
    all_to_all x1, blocking collectives, body(): lax.all_to_all(asked, 'st', split_axis=0, concat_axis=0, tiled=True)  22.3 us
    dot_general x2, matrix products, predict_residual(): jnp.einsum('bvm,bmq->bvq', ev_im, zt_re, precision=HIGH)  9.42 us
    dot_general x2, matrix products, predict_residual(): jnp.einsum('bvm,bmq->bvq', ev_re, zt_re, precision=HIGH)  9.26 us
    dot_general x2, matrix products, predict_residual(): jnp.einsum('bvm,bmq->bvq', ev_re, zt_im, precision=HIGH)  7.81 us
  transfers between devices with their start and end apart: 4, of which 3 were waited for; matrix products, arithmetic and copies ran while one was open for 4% of the time, Pallas kernels for 0%

commit v1 on v0

v1 whole, which is shorter than its diff:
```python
import math

import jax
import jax.numpy as jnp
import numpy as np
from jax import lax
from jax.experimental import pallas as pl
from jax.experimental.pallas import tpu as pltpu
from jax.sharding import Mesh
from jax.sharding import PartitionSpec as P

SIDE = 32
SUBS = 8
ENDS = 2 * SUBS
VIS = 512
PEERS = 32
BLOCKS = 16
ROWS = 64
SCREENS = BLOCKS * ROWS
LANES = 128
SLOTS = 16

F32 = jnp.float32
BF16 = jnp.bfloat16
S32 = jnp.int32


def bf16_parts(array, count):
    rest = np.asarray(array, np.float64)
    parts = []
    for _ in range(count):
        part = rest.astype(np.float32).astype(jnp.bfloat16)
        parts.append(part)
        rest = rest - part.astype(np.float64)
    return parts


def dft_tables():
    index = np.arange(SIDE)
    angle = 2.0 * np.pi * (index[:, None] * index[None, :] % SIDE) / SIDE
    f_real = np.cos(angle) / SIDE
    f_imag = np.sin(angle) / SIDE
    rows = np.concatenate([f_real, f_imag], axis=0)
    rows_parts = np.concatenate(bf16_parts(rows, 3), axis=1)
    eye = np.eye(4)
    cols = np.concatenate([np.kron(eye, f_real.T), np.kron(eye, f_imag.T)], axis=1)
    hi, lo = bf16_parts(cols, 2)
    cols_parts = np.concatenate([hi, hi, lo], axis=0)
    edge = np.cos(np.pi * (index - (SIDE - 1) / 2.0) / SIDE)
    taper = np.tile(edge[:, None] * edge[None, :], (1, 4)).astype(np.float32)
    return rows_parts, cols_parts, taper


def turn_polynomials():
    nodes = 0.25 * np.cos(np.pi * (np.arange(400) + 0.5) / 400) ** 2
    r = np.sqrt(nodes)
    scaled = nodes * 4.0
    sine = np.polynomial.polynomial.polyfit(scaled, np.sin(2 * np.pi * r) / r, 7)
    cosine = np.polynomial.polynomial.polyfit(scaled, np.cos(2 * np.pi * r), 8)
    power = 4.0 ** np.arange(9)
    return [float(a) for a in sine * power[:8]], [float(a) for a in cosine * power]


SINE, COSINE = turn_polynomials()


def unit_circle(turns):
    r = turns - jnp.floor(turns + 0.5)
    r2 = r * r
    s = jnp.full_like(r, SINE[-1])
    for a in SINE[-2::-1]:
        s = s * r2 + a
    c = jnp.full_like(r, COSINE[-1])
    for a in COSINE[-2::-1]:
        c = c * r2 + a
    return c, s * r


def split(x):
    hi = x.astype(BF16)
    return hi, (x - hi.astype(F32)).astype(BF16)


def dot(a, b, contract):
    return lax.dot_general(a, b, ((contract[:1], contract[1:]), ((), ())), preferred_element_type=F32)


def cut_kernel(place_ref, wanted_ref, strip_ref, out_ref, wide_ref):
    wide_ref[...] = strip_ref[...].astype(F32)
    tile = place_ref[0]
    lane = lax.broadcasted_iota(S32, (SIDE, LANES), 1) // SIDE

    def one(i, carry):
        total = jnp.zeros((SIDE, LANES), F32)
        for slot in range(2):
            code = wanted_ref[i, 2 * tile + slot]
            row = code // LANES
            column = code - row * LANES
            for part in range(2):
                piece = wide_ref[part, pl.ds(row, SIDE), :]
                spot = 2 * slot + part
                piece = pltpu.roll(piece, (spot * SIDE + LANES - column) % LANES, 1)
                total = jnp.where(lane == spot, piece, total)
        out_ref[i] = total.astype(BF16)
        return carry

    lax.fori_loop(0, PEERS, one, 0)


def gather_kernel(table_ref, row_ref, patch_ref, out_ref):
    hi, lo = split(table_ref[...])
    table = jnp.concatenate([hi, lo], axis=1)
    ids = lax.broadcasted_iota(S32, (PEERS * ENDS, SCREENS), 1)
    chosen = jnp.where(ids == row_ref[...], 1.0, 0.0).astype(BF16)
    found = dot(chosen, table, (1, 0))
    out_ref[:, 0:16, :] = found[:, :LANES].reshape(PEERS, ENDS, LANES).astype(BF16)
    out_ref[:, 16:32, :] = found[:, LANES:].reshape(PEERS, ENDS, LANES).astype(BF16)
    out_ref[:, 32:64, :] = patch_ref[...]


def scatter_kernel(grads_ref, row_ref, out_ref):
    hi, lo = split(grads_ref[...])
    grads = jnp.concatenate([hi, lo], axis=1)
    ids = lax.broadcasted_iota(S32, (SCREENS, PEERS * ENDS), 0)
    chosen = jnp.where(ids == row_ref[...], 1.0, 0.0).astype(BF16)
    total = dot(chosen, grads, (1, 0))
    out_ref[...] = total[:, :LANES] + total[:, LANES:]


def add_kernel(parts_ref, out_ref):
    total = parts_ref[0]
    for i in range(1, BLOCKS):
        total = total + parts_ref[i]
    for i in range(PEERS):
        part = i // 8
        out_ref[i] = total[part * ENDS : (part + 1) * ENDS, :]


def place_kernel(parts_ref, out_ref):
    lane = lax.broadcasted_iota(S32, (ENDS, LANES), 1) // SIDE
    for block in range(8):
        rows = [parts_ref[4 * block + i] for i in range(4)]
        turned = [[rows[i] if d == 0 else pltpu.roll(rows[i], d * SIDE, 1) for d in range(4)] for i in range(4)]
        for comp in range(4):
            total = turned[0][(0 - comp) % 4]
            for i in range(1, 4):
                total = jnp.where(lane == i, turned[i][(i - comp) % 4], total)
            out_ref[:, comp, block * LANES : (block + 1) * LANES] = total


def main_kernel(slot_ref, got_ref, uv_ref, seen_ref, flag_ref, rows_ref, cols_ref, taper_ref, res_ref, grad_ref, beam_ref):
    got = got_ref[:, 0:16, :].astype(F32) + got_ref[:, 16:32, :].astype(F32)
    beam_ref[...] = got.reshape(PEERS * ENDS, LANES)
    lane = lax.broadcasted_iota(S32, (SIDE, LANES), 1) // SIDE
    centre = (lax.broadcasted_iota(S32, (SIDE, VIS), 0).astype(F32) - SIDE / 2.0) * (1.0 / SIDE)
    taper = taper_ref[...]

    def turn(x, blocks):
        return pltpu.roll(x, blocks * SIDE, 1)

    def one(k, carry):
        slot = slot_ref[k]
        tile = slot // 2
        second = (slot - 2 * tile) > 0
        pieces = [got_ref[8 * i + tile, 32:64, :].astype(F32) for i in range(4)]
        spun = [turn(p, 2) for p in pieces]
        halves = []
        for a, b in ((0, 1), (2, 3)):
            left = jnp.where(second, spun[a], pieces[a])
            right = jnp.where(second, pieces[b], spun[b])
            halves.append(jnp.where(lane < 2, left, right))
        patch = jnp.concatenate(halves, axis=1).astype(BF16)
        patch3 = jnp.concatenate([patch, patch, patch], axis=0)
        a = dot(rows_ref[...], patch3, (1, 0))
        x_re = a[:SIDE, :LANES] - a[SIDE:, LANES:]
        x_im = a[:SIDE, LANES:] + a[SIDE:, :LANES]
        hi, lo = split(jnp.concatenate([x_re, x_im], axis=0))
        b = dot(jnp.concatenate([hi, lo, hi], axis=1), cols_ref[...], (1, 0))
        i_re = b[:SIDE, :LANES] - b[SIDE:, LANES:]
        i_im = b[:SIDE, LANES:] + b[SIDE:, :LANES]

        g = beam_ref[pl.ds(k, SIDE, stride=ENDS), :]
        g1, g2, g3 = turn(g, 1), turn(g, 2), turn(g, 3)
        p_re = jnp.where(lane == 0, g, jnp.where(lane == 3, g2, g1))
        p_im = jnp.where(lane == 0, g2, jnp.where(lane == 3, g, g3))
        g = beam_ref[pl.ds(k + SUBS, SIDE, stride=ENDS), :]
        g2 = turn(g, 2)
        q_re = jnp.where(lane < 2, g, g2)
        q_im = jnp.where(lane < 2, g2, g)

        y_re = i_re * q_re + i_im * q_im
        y_im = i_im * q_re - i_re * q_im
        z_re = (p_re * y_re - p_im * y_im) * taper
        z_im = (p_re * y_im + p_im * y_re) * taper

        eu_re, eu_im = unit_circle(uv_ref[k, 0:1, :] * centre)
        ev_re, ev_im = unit_circle(uv_ref[k, 1:2, :] * centre)
        eu_hi, eu_lo = split(jnp.concatenate([eu_re, eu_im], axis=0))

        z = jnp.concatenate(
            [jnp.concatenate([z_re, z_im], axis=1), jnp.concatenate([-z_im, z_re], axis=1)], axis=0
        )
        z_hi, z_lo = split(z)
        w = dot(
            jnp.concatenate([z_hi, z_lo, z_hi], axis=0),
            jnp.concatenate([eu_hi, eu_hi, eu_lo], axis=0),
            (0, 0),
        )
        reals, imags = [], []
        for pol in range(4):
            w_re = w[pol * SIDE : (pol + 1) * SIDE]
            w_im = w[LANES + pol * SIDE : LANES + (pol + 1) * SIDE]
            reals.append(jnp.sum(w_re * ev_re - w_im * ev_im, axis=0, keepdims=True))
            imags.append(jnp.sum(w_re * ev_im + w_im * ev_re, axis=0, keepdims=True))
        model = jnp.concatenate(reals + imags, axis=0)
        used = flag_ref[pl.ds(k, 1), :].astype(F32)
        res = used * (seen_ref[k] - model)
        res_ref[k] = res
        back = -used * res

        t_re, t_im = [], []
        for pol in range(4):
            d_re = back[pol : pol + 1]
            d_im = back[4 + pol : 5 + pol]
            t_re.append(ev_re * d_re + ev_im * d_im)
            t_im.append(ev_re * d_im - ev_im * d_re)
        t_hi, t_lo = split(jnp.concatenate(t_re + t_im, axis=0))
        both = dot(jnp.concatenate([eu_hi, eu_lo], axis=0), t_hi, (1, 1))
        d = both[: 2 * SIDE] + both[2 * SIDE :] + dot(eu_hi, t_lo, (1, 1))
        dz_re = (d[:SIDE, :LANES] + d[SIDE:, LANES:]) * taper
        dz_im = (d[:SIDE, LANES:] - d[SIDE:, :LANES]) * taper

        dp_re = dz_re * y_re + dz_im * y_im
        dp_im = dz_im * y_re - dz_re * y_im
        dp_re = dp_re + turn(dp_re, 3)
        dp_im = dp_im + turn(dp_im, 3)
        grad_p = jnp.where(
            lane == 0, dp_re, jnp.where(lane == 1, turn(dp_re, 3), jnp.where(lane == 2, turn(dp_im, 2), turn(dp_im, 1)))
        )
        dy_re = dz_re * p_re + dz_im * p_im
        dy_im = dz_im * p_re - dz_re * p_im
        dq_re = dy_re * i_re + dy_im * i_im
        dq_im = dy_re * i_im - dy_im * i_re
        dq_re = dq_re + turn(dq_re, 2)
        dq_im = dq_im + turn(dq_im, 2)
        grad_q = jnp.where(lane < 2, dq_re, dq_im)
        grad_ref[pl.ds(k, SIDE, stride=ENDS), :] = grad_p
        grad_ref[pl.ds(k + SUBS, SIDE, stride=ENDS), :] = grad_q
        return carry

    lax.fori_loop(0, SUBS, one, 0)


SMEM = pl.BlockSpec(memory_space=pltpu.SMEM)
VMEM = pl.BlockSpec(memory_space=pltpu.VMEM)
PARAMS = pltpu.CompilerParams(vmem_limit_bytes=40 * 1024 * 1024)


def call(kernel, shapes, specs, out_specs, scratch=()):
    return pl.pallas_call(
        kernel,
        out_shape=shapes,
        in_specs=specs,
        out_specs=out_specs,
        scratch_shapes=list(scratch),
        compiler_params=PARAMS,
    )


def shape(dims, dtype=F32):
    return jax.ShapeDtypeStruct(dims, dtype)


def cut(place, wanted, grid):
    return pl.pallas_call(
        cut_kernel,
        out_shape=shape((PEERS, SIDE, LANES), BF16),
        grid_spec=pltpu.PrefetchScalarGridSpec(
            num_scalar_prefetch=2,
            grid=(1,),
            in_specs=[pl.BlockSpec((2, grid.shape[1], LANES), lambda i, place, wanted: (place[1], 0, 0))],
            out_specs=pl.BlockSpec((PEERS, SIDE, LANES), lambda i, place, wanted: (0, 0, 0)),
            scratch_shapes=[pltpu.VMEM((2, grid.shape[1], LANES), F32)],
        ),
        compiler_params=PARAMS,
    )(place, wanted, grid)


def exchange(x, axes):
    return lax.all_to_all(x, axes, split_axis=0, concat_axis=0, tiled=True)


ACROSS = ("x", "tile")
DEPTH = ("z", "core")


def body(grid, a_terms, stations, intervals, offsets, uv, observed, flags):
    tile = lax.axis_index("tile").astype(S32)
    mine = lax.dynamic_index_in_dim(a_terms, tile, 0, keepdims=False)
    mine = mine.reshape(2, 4, SIDE, SIDE).transpose(2, 0, 1, 3).reshape(SIDE, 2, LANES)

    ends = jnp.concatenate([stations[:, 0], stations[:, 1]])
    depth = (ends >> 6) * 2 + ((ends >> 3) & 1)
    row = (depth * PEERS + ((ends >> 4) & 3) * 8 + (ends & 7)) * 2 + jnp.concatenate([intervals, intervals])
    owner = offsets[:, 0] >> 8
    same = owner[:, None] == owner[None, :]
    earlier = jnp.arange(SUBS)[:, None] > jnp.arange(SUBS)[None, :]
    slot = owner * 2 + jnp.sum((same & earlier).astype(S32), axis=1)
    code = (offsets[:, 0] & 255) * LANES + offsets[:, 1]
    placed = slot[:, None] == jnp.arange(SLOTS, dtype=S32)[None, :]
    codes = jnp.sum(jnp.where(placed, code[:, None], 0), axis=0)
    asked = jnp.concatenate([row, codes, jnp.zeros((LANES - ENDS - SLOTS,), S32)]).astype(F32)
    asked = jnp.broadcast_to(asked[None, None, :], (PEERS, 1, LANES))

    got_a = exchange(jnp.concatenate([mine, asked, jnp.zeros_like(asked)], axis=1), ACROSS)
    part = got_a[:, :2, :].reshape(1, ROWS, LANES)
    table = exchange(jnp.broadcast_to(part, (BLOCKS, ROWS, LANES)), DEPTH)

    wanted = got_a[:, 2, :].astype(S32)
    rows = wanted[:, :ENDS].reshape(PEERS * ENDS)
    place = jnp.stack([tile, lax.axis_index("x").astype(S32)])
    patches = cut(place, wanted[:, ENDS : ENDS + SLOTS], grid)

    found = call(
        gather_kernel, shape((PEERS, 64, LANES), BF16), [VMEM] * 3, VMEM
    )(table.reshape(SCREENS, LANES), rows[:, None], patches)
    got_c = exchange(found, ACROSS)

    tables = [jnp.asarray(t) for t in dft_tables()]
    result, grads = call(
        main_kernel,
        (shape((SUBS, 8, VIS)), shape((PEERS * ENDS, LANES))),
        [SMEM] + [VMEM] * 7,
        (VMEM, VMEM),
        [pltpu.VMEM((PEERS * ENDS, LANES), F32)],
    )(slot, got_c, uv, observed, flags, *tables)

    back_c = exchange(grads.reshape(PEERS, ENDS, LANES), ACROSS)
    dense = call(
        scatter_kernel, shape((SCREENS, LANES)), [VMEM] * 2, VMEM
    )(back_c.reshape(PEERS * ENDS, LANES), rows[None, :])
    back_b = exchange(dense.reshape(BLOCKS, ROWS, LANES), DEPTH)
    summed = call(add_kernel, shape((PEERS, ENDS, LANES)), [VMEM], VMEM)(back_b)
    back_a = exchange(summed, ACROSS)
    total = call(place_kernel, shape((ENDS, 4, SIDE * SIDE)), [VMEM], VMEM)(back_a)
    return (result, total.reshape(8, 2, 4, SIDE * SIDE))


def solution(mesh):
    fine = Mesh(mesh.devices.reshape(8, 4, 2, 8), ("z", "x", "core", "tile"))
    st = ("z", "x", "core")
    every = ("z", "x", "core", "tile")
    placed = (
        P(None, "tile", None),
        P(st, None, None, None),
        P(every, None),
        P(every),
        P(every, None),
        P(every, None, None),
        P(every, None, None),
        P(every, None),
    )
    return jax.shard_map(
        body,
        mesh=fine,
        in_specs=placed,
        out_specs=(P(every, None, None), P(st, None, None, None)),
        check_vma=False,
    )
```

time: 331 us -> 142 us (0.43)
  the two profiles are of different devices: /device:TPU:2 before, /device:TPU:8 now
where the time goes in v1:
time: 142 us; the launch traced here: 141 us
  blocking collectives  55.6 us (39%)
  waiting for transfers between devices  43 us (30%)
  starting transfers between devices  20.8 us (15%)
  Pallas kernels  17 us (12%)
  local copies, waits for them, and re-layouts  3.7 us (3%)
    all_to_all x3, blocking collectives, exchange(): return lax.all_to_all(x, axes, split_axis=0, concat_axis=0, tiled=True)  55.6 us
    all_to_all x3, waiting for transfers between devices, exchange(): return lax.all_to_all(x, axes, split_axis=0, concat_axis=0, tiled=True)  43 us
    all_to_all x3, starting transfers between devices, exchange(): return lax.all_to_all(x, axes, split_axis=0, concat_axis=0, tiled=True)  20.8 us
    pallas_call x1, Pallas kernels, body(): call(main_kernel, (shape((SUBS, 8, VIS)), shape((PEERS * ENDS, LANES))),...  10.6 us
    pallas_call x1, Pallas kernels, cut(): pl.pallas_call(cut_kernel, out_shape=shape((PEERS, SIDE, LANES), BF16), g...  3.48 us
  transfers between devices with their start and end apart: 3, of which 3 were waited for; matrix products, arithmetic and copies ran while one was open for 0% of the time, Pallas kernels for 2%

profile of v1, /device:TPU:8, one launch (start us, length us, event | category | flops | bytes accessed | tf_op | source)
XLA Modules:
  0.0 141.4 jit_solution(7988489102688037917)
XLA Ops:
  0.6 0.0 copy-start
  0.7 0.7 copy-done.9
  1.4 0.2 convert_reduce_fusion
  1.6 0.7 copy-done.8
  2.3 0.1 reshape.70
  2.4 0.1 copy.22
  2.4 0.1 reshape.71
  2.6 0.1 pad.4.clone
  2.6 0.1 select_reduce_fusion
  2.7 0.7 copy-done.10
  3.4 0.1 add_add_fusion
  3.5 0.1 add_convert_fusion
  3.6 0.1 maximum_maximum_fusion
  3.7 19.1 %all_to_all.30 = f32[32,4,128]{2,1,0:T(4,128)S(1)} all-to-all(f32[32,4,128]{2,1,0:T(4,128)S(1)} %copy.23), channel_id=1, replica_groups=mesh['z'=8,'x'=4,'core'=2,'tile'=8] {'x','tile'}, dimensions={0} | all-to-all | bytes 131072 | tf_op jit(solution)/shard_map/all_to_all | solution.py:290
  22.8 0.8 broadcast_in_dim.47
  23.6 10.6 %all-to-all-start.1 = ((f32[16,64,128]{2,1,0:T(8,128)}), f32[16,64,128]{2,1,0:T(8,128)S(1)}, u32[]{:S(2)}, u32[]{:S(2)}) async-start(f32[16,64,128]{2,1,0:T(8,128)} %broadcast_in_dim.47), calls=%async_computation.1 | async-start | bytes 1048576 | tf_op jit(solution)/shard_map/all_to_all | solution.py:290
  34.2 0.1 pad_add_fusion.1.place_ref
  34.3 0.1 fusion.2
  34.4 0.2 broadcast_in_dim_reshape.8.row_ref
  34.5 3.5 %shard_map.122.patch_ref = bf16[32,32,128]{2,1,0:T(8,128)(2,1)S(1)} custom-call(s32[2]{0:T(128)S(1)} %pad_add_fusion.1.place_ref, s32[32,16]{1,0:T(8,128)S(1)} %get-tuple-element.6.wanted_ref, bf16[8,256,128]{2,1,0:T(8,128)(2,1)S(1)} %copy-done.1), custom_call_target="tpu_custom_call" | custom-call | tf_op jit(solution)/shard_map/pallas_call | solution.py:275
  38.0 12.2 %all-to-all-done.1 = f32[16,64,128]{2,1,0:T(8,128)S(1)} async-done(((f32[16,64,128]{2,1,0:T(8,128)}), f32[16,64,128]{2,1,0:T(8,128)S(1)}, u32[]{:S(2)}, u32[]{:S(2)}) %all-to-all-start.1) | async-done | bytes 524320 | tf_op jit(solution)/shard_map/all_to_all | solution.py:290
  50.2 1.4 shard_map.123
  51.6 4.8 %all-to-all-start.2 = ((bf16[32,64,128]{2,1,0:T(8,128)(2,1)}), bf16[32,64,128]{2,1,0:T(8,128)(2,1)S(1)}, u32[]{:S(2)}, u32[]{:S(2)}) async-start(bf16[32,64,128]{2,1,0:T(8,128)(2,1)} %shard_map.123), calls=%async_computation.2 | async-start | bytes 1048576 | tf_op jit(solution)/shard_map/all_to_all | solution.py:290
  56.5 18.1 %all-to-all-done.2.got_ref = bf16[32,64,128]{2,1,0:T(8,128)(2,1)S(1)} async-done(((bf16[32,64,128]{2,1,0:T(8,128)(2,1)}), bf16[32,64,128]{2,1,0:T(8,128)(2,1)S(1)}, u32[]{:S(2)}, u32[]{:S(2)}) %all-to-all-start.2) | async-done | bytes 524320 | tf_op jit(solution)/shard_map/all_to_all | solution.py:290
  74.6 10.6 %shard_map.124 = (f32[8,8,512]{2,1,0:T(8,128)}, f32[512,128]{1,0:T(8,128)}) custom-call(s32[8]{0:T(128)S(1)} %multiply_add_fusion.slot_ref, bf16[32,64,128]{2,1,0:T(8,128)(2,1)S(1)} %all-to-all-done.2.got_ref, f32[8,2,512]{2,1,0:T(2,128)S(1)} %copy-done.4, f32[8,8,512]{2,1,0:T(8,128)S(1)} %copy-done.3, s32[8,512]{1,0:T(8,128)S(1)} %copy-done.5, ...), custom_call_target="tpu_custom_call" | custom-call | tf_op jit(solution)/shard_map/pallas_call | solution.py:330
  85.2 5.4 %all-to-all-start.3 = ((f32[32,16,128]{2,1,0:T(8,128)}), f32[32,16,128]{2,1,0:T(8,128)S(1)}, u32[]{:S(2)}, u32[]{:S(2)}) async-start(f32[32,16,128]{2,1,0:T(8,128)} %bitcast.12), calls=%async_computation.3 | async-start | bytes 524288 | tf_op jit(solution)/shard_map/all_to_all | solution.py:290
  90.6 0.1 broadcast_in_dim_reshape.7.row_ref
  90.7 12.7 %all-to-all-done.3 = f32[32,16,128]{2,1,0:T(8,128)S(1)} async-done(((f32[32,16,128]{2,1,0:T(8,128)}), f32[32,16,128]{2,1,0:T(8,128)S(1)}, u32[]{:S(2)}, u32[]{:S(2)}) %all-to-all-start.3) | async-done | bytes 262176 | tf_op jit(solution)/shard_map/all_to_all | solution.py:290
  103.4 0.4 shard_map.125
  103.8 19.0 %all_to_all.31.parts_ref = f32[16,64,128]{2,1,0:T(8,128)S(1)} all-to-all(f32[16,64,128]{2,1,0:T(8,128)S(1)} %bitcast.32), channel_id=1, replica_groups=mesh['z'=8,'x'=4,'core'=2,'tile'=8] {'z','core'}, dimensions={0} | all-to-all | bytes 1048576 | tf_op jit(solution)/shard_map/all_to_all | solution.py:290
  122.8 17.5 %all_to_all.32.parts_ref = f32[32,16,128]{2,1,0:T(8,128)S(1)} all-to-all(f32[32,16,128]{2,1,0:T(8,128)S(1)} %shard_map.126), channel_id=1, replica_groups=mesh['z'=8,'x'=4,'core'=2,'tile'=8] {'x','tile'}, dimensions={0} | all-to-all | bytes 524288 | tf_op jit(solution)/shard_map/all_to_all | solution.py:290
  140.4 1.1 shard_map.127
  (30 shorter events, 0.2 us)
Async XLA Ops:
  0.6 1.6 %copy-start = (f32[8,2,4,1024]{3,2,1,0:T(4,128)S(1)}, f32[8,2,4,1024]{3,2,1,0:T(4,128)}, u32[]{:S(2)}) copy-start(f32[8,2,4,1024]{3,2,1,0:T(4,128)} %param.12) | copy-start | bytes 786436
  0.6 0.7 copy-start.9
  1.6 0.7 copy-start.8
  2.7 0.7 copy-start.10
  23.6 10.9 %copy-start.1 = (bf16[8,256,128]{2,1,0:T(8,128)(2,1)S(1)}, bf16[8,256,128]{2,1,0:T(8,128)(2,1)}, u32[]{:S(2)}) copy-start(bf16[8,256,128]{2,1,0:T(8,128)(2,1)} %strip_ref.1) | copy-start | bytes 1572868
  23.6 26.6 %all-to-all-start.1 = ((f32[16,64,128]{2,1,0:T(8,128)}), f32[16,64,128]{2,1,0:T(8,128)S(1)}, u32[]{:S(2)}, u32[]{:S(2)}) async-start(f32[16,64,128]{2,1,0:T(8,128)} %broadcast_in_dim.47), calls=%async_computation.1 | async-start | bytes 1048576 | tf_op jit(solution)/shard_map/all_to_all | solution.py:290
  51.6 23.0 %copy-start.2 = (bf16[384,256]{1,0:T(8,128)(2,1)S(1)}, bf16[384,256]{1,0:T(8,128)(2,1)}, u32[]{:S(2)}) copy-start(bf16[384,256]{1,0:T(8,128)(2,1)} %constant.48.clone.cols_ref) | copy-start | bytes 589828
  51.6 23.0 %copy-start.3 = (f32[8,8,512]{2,1,0:T(8,128)S(1)}, f32[8,8,512]{2,1,0:T(8,128)}, u32[]{:S(2)}) copy-start(f32[8,8,512]{2,1,0:T(8,128)} %seen_ref.1) | copy-start | bytes 393220
  51.6 23.0 %copy-start.4 = (f32[8,2,512]{2,1,0:T(2,128)S(1)}, f32[8,2,512]{2,1,0:T(2,128)}, u32[]{:S(2)}) copy-start(f32[8,2,512]{2,1,0:T(2,128)} %uv_ref.1) | copy-start | bytes 98308
  51.6 23.0 %copy-start.5 = (s32[8,512]{1,0:T(8,128)S(1)}, s32[8,512]{1,0:T(8,128)}, u32[]{:S(2)}) copy-start(s32[8,512]{1,0:T(8,128)} %flag_ref.1) | copy-start | bytes 49156
  51.6 23.0 %copy-start.6 = (f32[32,128]{1,0:T(8,128)S(1)}, f32[32,128]{1,0:T(8,128)}, u32[]{:S(2)}) copy-start(f32[32,128]{1,0:T(8,128)} %constant.49.clone.taper_ref) | copy-start | bytes 49156
  51.6 23.0 %copy-start.7 = (bf16[64,96]{1,0:T(8,128)(2,1)S(1)}, bf16[64,96]{1,0:T(8,128)(2,1)}, u32[]{:S(2)}) copy-start(bf16[64,96]{1,0:T(8,128)(2,1)} %constant.17.clone.rows_ref) | copy-start | bytes 36868
  51.6 22.9 %all-to-all-start.2 = ((bf16[32,64,128]{2,1,0:T(8,128)(2,1)}), bf16[32,64,128]{2,1,0:T(8,128)(2,1)S(1)}, u32[]{:S(2)}, u32[]{:S(2)}) async-start(bf16[32,64,128]{2,1,0:T(8,128)(2,1)} %shard_map.123), calls=%async_computation.2 | async-start | bytes 1048576 | tf_op jit(solution)/shard_map/all_to_all | solution.py:290
  85.2 18.2 %all-to-all-start.3 = ((f32[32,16,128]{2,1,0:T(8,128)}), f32[32,16,128]{2,1,0:T(8,128)S(1)}, u32[]{:S(2)}, u32[]{:S(2)}) async-start(f32[32,16,128]{2,1,0:T(8,128)} %bitcast.12), calls=%async_computation.3 | async-start | bytes 524288 | tf_op jit(solution)/shard_map/all_to_all | solution.py:290

commit v2 on v1

--- a/solution.py
+++ b/solution.py
@@ -1,5 +1,3 @@
-import math
-
 import jax
 import jax.numpy as jnp
 import numpy as np
@@ -14,9 +12,10 @@
 ENDS = 2 * SUBS
 VIS = 512
 PEERS = 32
-BLOCKS = 16
+LAYERS = 8
 ROWS = 64
-SCREENS = BLOCKS * ROWS
+HALF = LAYERS * ROWS
+UNROLL = 8
 LANES = 128
 SLOTS = 16
 
@@ -85,6 +84,69 @@
     return lax.dot_general(a, b, ((contract[:1], contract[1:]), ((), ())), preferred_element_type=F32)
 
 
+def slots(offsets_ref):
+    tiles = [offsets_ref[0, k] >> 8 for k in range(SUBS)]
+    seconds = []
+    for k in range(SUBS):
+        second = jnp.zeros((), S32)
+        for j in range(k):
+            second = jnp.where(tiles[j] == tiles[k], 1, second)
+        seconds.append(second)
+    return tiles, seconds
+
+
+def prep_kernel(
+    stations_in, intervals_in, offsets_in, terms_in, out_ref, stations_ref, intervals_ref, offsets_ref, terms_ref, sems
+):
+    own = lax.axis_index("tile")
+    copies = [
+        pltpu.make_async_copy(stations_in, stations_ref, sems.at[0]),
+        pltpu.make_async_copy(intervals_in, intervals_ref, sems.at[1]),
+        pltpu.make_async_copy(offsets_in, offsets_ref, sems.at[2]),
+        pltpu.make_async_copy(terms_in.at[own], terms_ref, sems.at[3]),
+    ]
+    for copy in copies:
+        copy.start()
+    for copy in copies[:3]:
+        copy.wait()
+    spot = lax.broadcasted_iota(S32, (1, LANES), 1)
+    asked = jnp.zeros((1, LANES), S32)
+    tiles, seconds = slots(offsets_ref)
+    for k in range(SUBS):
+        for end in range(2):
+            station = stations_ref[end, k]
+            depth = ((station >> 3) & 1) * LAYERS + (station >> 6)
+            row = depth * ROWS + (((station >> 4) & 3) * 8 + (station & 7)) * 2 + intervals_ref[k]
+            asked = jnp.where(spot == end * SUBS + k, row, asked)
+        code = (offsets_ref[0, k] & 255) * LANES + offsets_ref[1, k]
+        asked = jnp.where(spot == ENDS + 2 * tiles[k] + seconds[k], code, asked)
+    out_ref[:, 2:4, :] = jnp.broadcast_to(asked.astype(F32).reshape(1, 1, LANES), (PEERS, 2, LANES))
+    copies[3].wait()
+    lane = lax.broadcasted_iota(S32, (2, LANES), 1) // SIDE
+    for block in range(8):
+        comps = [terms_ref[:, comp, block * LANES : (block + 1) * LANES] for comp in range(4)]
+        for i in range(4):
+            total = comps[i]
+            for comp in range(4):
+                if comp != i:
+                    total = jnp.where(lane == comp, pltpu.roll(comps[comp], (comp - i) % 4 * SIDE, 1), total)
+            out_ref[4 * block + i, 0:2, :] = total
+
+
+def wave_kernel(uv_ref, row_wave_ref, column_wave_ref):
+    centre = (lax.broadcasted_iota(S32, (SIDE, VIS), 0).astype(F32) - SIDE / 2.0) * (1.0 / SIDE)
+
+    def one(k, carry):
+        real, imag = unit_circle(uv_ref[k, 0:1, :] * centre)
+        hi, lo = split(jnp.concatenate([real, imag], axis=0))
+        row_wave_ref[k] = jnp.concatenate([hi, hi, lo], axis=0)
+        real, imag = unit_circle(uv_ref[k, 1:2, :] * centre)
+        column_wave_ref[k] = jnp.concatenate([real, imag], axis=0)
+        return carry
+
+    lax.fori_loop(0, SUBS, one, 0)
+
+
 def cut_kernel(place_ref, wanted_ref, strip_ref, out_ref, wide_ref):
     wide_ref[...] = strip_ref[...].astype(F32)
     tile = place_ref[0]
@@ -94,42 +156,59 @@
         total = jnp.zeros((SIDE, LANES), F32)
         for slot in range(2):
             code = wanted_ref[i, 2 * tile + slot]
-            row = code // LANES
-            column = code - row * LANES
+            row = code >> 7
+            column = code & (LANES - 1)
             for part in range(2):
+                spot = 2 * slot + part
                 piece = wide_ref[part, pl.ds(row, SIDE), :]
-                spot = 2 * slot + part
-                piece = pltpu.roll(piece, (spot * SIDE + LANES - column) % LANES, 1)
+                piece = pltpu.roll(piece, (spot * SIDE + LANES - column) & (LANES - 1), 1)
                 total = jnp.where(lane == spot, piece, total)
         out_ref[i] = total.astype(BF16)
         return carry
 
-    lax.fori_loop(0, PEERS, one, 0)
-
-
-def gather_kernel(table_ref, row_ref, patch_ref, out_ref):
-    hi, lo = split(table_ref[...])
-    table = jnp.concatenate([hi, lo], axis=1)
-    ids = lax.broadcasted_iota(S32, (PEERS * ENDS, SCREENS), 1)
-    chosen = jnp.where(ids == row_ref[...], 1.0, 0.0).astype(BF16)
-    found = dot(chosen, table, (1, 0))
+    lax.fori_loop(0, PEERS, one, 0, unroll=4)
+
+
+def spread_kernel(got_ref, out_ref):
+    part = got_ref[:, 0:2, :].reshape(ROWS, LANES)
+    for i in range(LAYERS):
+        out_ref[i] = part
+
+
+def pick(table, rows, first):
+    hi, lo = split(table)
+    ids = lax.broadcasted_iota(S32, (PEERS * ENDS, HALF), 1) + first
+    chosen = jnp.where(ids == rows, 1.0, 0.0).astype(BF16)
+    return dot(chosen, jnp.concatenate([hi, lo], axis=1), (1, 0))
+
+
+def near_kernel(place_ref, table_ref, row_ref, out_ref):
+    out_ref[...] = pick(table_ref[...], row_ref[...], HALF * place_ref[2]).astype(BF16)
+
+
+def gather_kernel(place_ref, table_ref, row_ref, near_ref, patch_ref, out_ref):
+    found = pick(table_ref[...], row_ref[...], HALF * (1 - place_ref[2])) + near_ref[...].astype(F32)
     out_ref[:, 0:16, :] = found[:, :LANES].reshape(PEERS, ENDS, LANES).astype(BF16)
     out_ref[:, 16:32, :] = found[:, LANES:].reshape(PEERS, ENDS, LANES).astype(BF16)
     out_ref[:, 32:64, :] = patch_ref[...]
 
 
-def scatter_kernel(grads_ref, row_ref, out_ref):
+def scatter_kernel(first_ref, grads_ref, row_ref, out_ref):
     hi, lo = split(grads_ref[...])
     grads = jnp.concatenate([hi, lo], axis=1)
-    ids = lax.broadcasted_iota(S32, (SCREENS, PEERS * ENDS), 0)
+    ids = lax.broadcasted_iota(S32, (HALF, PEERS * ENDS), 0) + first_ref[0]
     chosen = jnp.where(ids == row_ref[...], 1.0, 0.0).astype(BF16)
     total = dot(chosen, grads, (1, 0))
     out_ref[...] = total[:, :LANES] + total[:, LANES:]
 
 
+def pair_kernel(keep_ref, other_ref, out_ref):
+    out_ref[...] = keep_ref[...] + other_ref[...]
+
+
 def add_kernel(parts_ref, out_ref):
     total = parts_ref[0]
-    for i in range(1, BLOCKS):
+    for i in range(1, LAYERS):
         total = total + parts_ref[i]
     for i in range(PEERS):
         part = i // 8
@@ -148,34 +227,48 @@
             out_ref[:, comp, block * LANES : (block + 1) * LANES] = total
 
 
-def main_kernel(slot_ref, got_ref, uv_ref, seen_ref, flag_ref, rows_ref, cols_ref, taper_ref, res_ref, grad_ref, beam_ref):
+def main_kernel(
+    slot_ref, got_ref, row_wave_in, column_wave_in, seen_in, flag_in, rows_ref, cols_ref, taper_ref,
+    res_ref, grad_ref, beam_ref, row_wave_ref, column_wave_ref, seen_ref, flag_ref, side_ref, z_ref, dz_ref, sems,
+):
+    copies = [
+        pltpu.make_async_copy(a, b, sems.at[i])
+        for i, (a, b) in enumerate(
+            ((row_wave_in, row_wave_ref), (column_wave_in, column_wave_ref), (seen_in, seen_ref), (flag_in, flag_ref))
+        )
+    ]
+    for copy in copies:
+        copy.start()
     got = got_ref[:, 0:16, :].astype(F32) + got_ref[:, 16:32, :].astype(F32)
     beam_ref[...] = got.reshape(PEERS * ENDS, LANES)
     lane = lax.broadcasted_iota(S32, (SIDE, LANES), 1) // SIDE
-    centre = (lax.broadcasted_iota(S32, (SIDE, VIS), 0).astype(F32) - SIDE / 2.0) * (1.0 / SIDE)
     taper = taper_ref[...]
 
     def turn(x, blocks):
         return pltpu.roll(x, blocks * SIDE, 1)
 
-    def one(k, carry):
+    patches = []
+    for k in range(SUBS):
         slot = slot_ref[k]
-        tile = slot // 2
-        second = (slot - 2 * tile) > 0
+        tile = slot >> 1
+        second = (slot & 1) > 0
         pieces = [got_ref[8 * i + tile, 32:64, :].astype(F32) for i in range(4)]
-        spun = [turn(p, 2) for p in pieces]
-        halves = []
         for a, b in ((0, 1), (2, 3)):
-            left = jnp.where(second, spun[a], pieces[a])
-            right = jnp.where(second, pieces[b], spun[b])
-            halves.append(jnp.where(lane < 2, left, right))
-        patch = jnp.concatenate(halves, axis=1).astype(BF16)
-        patch3 = jnp.concatenate([patch, patch, patch], axis=0)
-        a = dot(rows_ref[...], patch3, (1, 0))
-        x_re = a[:SIDE, :LANES] - a[SIDE:, LANES:]
-        x_im = a[:SIDE, LANES:] + a[SIDE:, :LANES]
-        hi, lo = split(jnp.concatenate([x_re, x_im], axis=0))
-        b = dot(jnp.concatenate([hi, lo, hi], axis=1), cols_ref[...], (1, 0))
+            left = jnp.where(second, turn(pieces[a], 2), pieces[a])
+            right = jnp.where(second, pieces[b], turn(pieces[b], 2))
+            patches.append(jnp.where(lane < 2, left, right).astype(BF16))
+    patch = jnp.concatenate(patches, axis=1)
+    a = dot(rows_ref[...], jnp.concatenate([patch, patch, patch], axis=0), (1, 0))
+    mixed = []
+    for k in range(SUBS):
+        re = a[:, 2 * k * LANES : (2 * k + 1) * LANES]
+        im = a[:, (2 * k + 1) * LANES : (2 * k + 2) * LANES]
+        mixed += [re[:SIDE] - im[SIDE:], im[:SIDE] + re[SIDE:]]
+    hi, lo = split(jnp.concatenate(mixed, axis=0))
+    images = dot(jnp.concatenate([hi, lo, hi], axis=1), cols_ref[...], (1, 0))
+
+    for k in range(SUBS):
+        b = images[2 * k * SIDE : 2 * (k + 1) * SIDE]
         i_re = b[:SIDE, :LANES] - b[SIDE:, LANES:]
         i_im = b[:SIDE, LANES:] + b[SIDE:, :LANES]
 
@@ -192,20 +285,22 @@
         y_im = i_im * q_re - i_re * q_im
         z_re = (p_re * y_re - p_im * y_im) * taper
         z_im = (p_re * y_im + p_im * y_re) * taper
-
-        eu_re, eu_im = unit_circle(uv_ref[k, 0:1, :] * centre)
-        ev_re, ev_im = unit_circle(uv_ref[k, 1:2, :] * centre)
-        eu_hi, eu_lo = split(jnp.concatenate([eu_re, eu_im], axis=0))
-
+        for i, part in enumerate((i_re, i_im, p_re, p_im, y_re, y_im)):
+            side_ref[k, i] = part * taper if i > 3 else part
         z = jnp.concatenate(
             [jnp.concatenate([z_re, z_im], axis=1), jnp.concatenate([-z_im, z_re], axis=1)], axis=0
         )
         z_hi, z_lo = split(z)
-        w = dot(
-            jnp.concatenate([z_hi, z_lo, z_hi], axis=0),
-            jnp.concatenate([eu_hi, eu_hi, eu_lo], axis=0),
-            (0, 0),
-        )
+        z_ref[k] = jnp.concatenate([z_hi, z_lo, z_hi], axis=0)
+
+    for copy in copies:
+        copy.wait()
+
+    def one(k, carry):
+        row_wave = row_wave_ref[k]
+        ev_re = column_wave_ref[k, :SIDE, :]
+        ev_im = column_wave_ref[k, SIDE:, :]
+        w = dot(z_ref[k], row_wave, (0, 0))
         reals, imags = [], []
         for pol in range(4):
             w_re = w[pol * SIDE : (pol + 1) * SIDE]
@@ -225,10 +320,17 @@
             t_re.append(ev_re * d_re + ev_im * d_im)
             t_im.append(ev_re * d_im - ev_im * d_re)
         t_hi, t_lo = split(jnp.concatenate(t_re + t_im, axis=0))
-        both = dot(jnp.concatenate([eu_hi, eu_lo], axis=0), t_hi, (1, 1))
-        d = both[: 2 * SIDE] + both[2 * SIDE :] + dot(eu_hi, t_lo, (1, 1))
-        dz_re = (d[:SIDE, :LANES] + d[SIDE:, LANES:]) * taper
-        dz_im = (d[:SIDE, LANES:] - d[SIDE:, :LANES]) * taper
+        both = dot(row_wave[2 * SIDE :], t_hi, (1, 1))
+        dz_ref[k] = both[: 2 * SIDE] + both[2 * SIDE :] + dot(row_wave[: 2 * SIDE], t_lo, (1, 1))
+        return carry
+
+    lax.fori_loop(0, SUBS, one, 0, unroll=UNROLL)
+
+    for k in range(SUBS):
+        d = dz_ref[k]
+        i_re, i_im, p_re, p_im, y_re, y_im = (side_ref[k, i] for i in range(6))
+        dz_re = d[:SIDE, :LANES] + d[SIDE:, LANES:]
+        dz_im = d[:SIDE, LANES:] - d[SIDE:, :LANES]
 
         dp_re = dz_re * y_re + dz_im * y_im
         dp_im = dz_im * y_re - dz_re * y_im
@@ -237,22 +339,22 @@
         grad_p = jnp.where(
             lane == 0, dp_re, jnp.where(lane == 1, turn(dp_re, 3), jnp.where(lane == 2, turn(dp_im, 2), turn(dp_im, 1)))
         )
+        i_re = i_re * taper
+        i_im = i_im * taper
         dy_re = dz_re * p_re + dz_im * p_im
         dy_im = dz_im * p_re - dz_re * p_im
         dq_re = dy_re * i_re + dy_im * i_im
         dq_im = dy_re * i_im - dy_im * i_re
         dq_re = dq_re + turn(dq_re, 2)
         dq_im = dq_im + turn(dq_im, 2)
-        grad_q = jnp.where(lane < 2, dq_re, dq_im)
         grad_ref[pl.ds(k, SIDE, stride=ENDS), :] = grad_p
-        grad_ref[pl.ds(k + SUBS, SIDE, stride=ENDS), :] = grad_q
-        return carry
-
-    lax.fori_loop(0, SUBS, one, 0)
+        grad_ref[pl.ds(k + SUBS, SIDE, stride=ENDS), :] = jnp.where(lane < 2, dq_re, dq_im)
 
 
 SMEM = pl.BlockSpec(memory_space=pltpu.SMEM)
 VMEM = pl.BlockSpec(memory_space=pltpu.VMEM)
+HBM = pl.BlockSpec(memory_space=pltpu.HBM)
+WAVES = pl.BlockSpec(memory_space=pl.ANY)
 PARAMS = pltpu.CompilerParams(vmem_limit_bytes=40 * 1024 * 1024)
 
 
@@ -286,60 +388,91 @@
     )(place, wanted, grid)
 
 
+def in_hbm(x):
+    return pltpu.with_memory_space_constraint(x, pltpu.HBM)
+
+
 def exchange(x, axes):
     return lax.all_to_all(x, axes, split_axis=0, concat_axis=0, tiled=True)
 
 
+def main(*args):
+    tables = [jnp.asarray(t) for t in dft_tables()]
+    return call(
+        main_kernel,
+        (shape((SUBS, 8, VIS)), shape((PEERS * ENDS, LANES))),
+        [SMEM, VMEM] + [WAVES] * 2 + [HBM] * 2 + [VMEM] * 3,
+        (VMEM, VMEM),
+        [
+            pltpu.VMEM((PEERS * ENDS, LANES), F32),
+            pltpu.VMEM((SUBS, 6 * SIDE, VIS), BF16),
+            pltpu.VMEM((SUBS, 2 * SIDE, VIS), F32),
+            pltpu.VMEM((SUBS, 8, VIS), F32),
+            pltpu.VMEM((SUBS, VIS), S32),
+            pltpu.VMEM((SUBS, 6, SIDE, LANES), F32),
+            pltpu.VMEM((SUBS, 6 * SIDE, 2 * LANES), BF16),
+            pltpu.VMEM((SUBS, 2 * SIDE, 2 * LANES), F32),
+            pltpu.SemaphoreType.DMA((4,)),
+        ],
+    )(*args, *tables)
+
+
 ACROSS = ("x", "tile")
-DEPTH = ("z", "core")
+SWAP = ((0, 1), (1, 0))
 
 
 def body(grid, a_terms, stations, intervals, offsets, uv, observed, flags):
-    tile = lax.axis_index("tile").astype(S32)
-    mine = lax.dynamic_index_in_dim(a_terms, tile, 0, keepdims=False)
-    mine = mine.reshape(2, 4, SIDE, SIDE).transpose(2, 0, 1, 3).reshape(SIDE, 2, LANES)
-
-    ends = jnp.concatenate([stations[:, 0], stations[:, 1]])
-    depth = (ends >> 6) * 2 + ((ends >> 3) & 1)
-    row = (depth * PEERS + ((ends >> 4) & 3) * 8 + (ends & 7)) * 2 + jnp.concatenate([intervals, intervals])
-    owner = offsets[:, 0] >> 8
+    place = jnp.stack([lax.axis_index(name).astype(S32) for name in ("tile", "x", "core")])
+    offsets = offsets.T
+    sent = call(
+        prep_kernel,
+        shape((PEERS, 4, LANES)),
+        [HBM] * 4,
+        VMEM,
+        [
+            pltpu.SMEM((2, SUBS), S32),
+            pltpu.SMEM((SUBS,), S32),
+            pltpu.SMEM((2, SUBS), S32),
+            pltpu.VMEM((2, 4, SIDE * SIDE), F32),
+            pltpu.SemaphoreType.DMA((4,)),
+        ],
+    )(*(in_hbm(x) for x in (stations.T, intervals, offsets, a_terms)))
+    got_a = exchange(sent, ACROSS)
+    spread = call(spread_kernel, shape((LAYERS, ROWS, LANES)), [VMEM], VMEM)(got_a)
+    own = exchange(spread, "z").reshape(HALF, LANES)
+
+    wanted = got_a[:, 2, :].astype(S32)
+    rows = wanted[:, :ENDS].reshape(PEERS * ENDS)
+    patches = cut(place, wanted[:, ENDS : ENDS + SLOTS], grid)
+    own, patches = lax.optimization_barrier((own, patches))
+    other = lax.ppermute(own, "core", SWAP)
+    waves = call(
+        wave_kernel, (shape((SUBS, 6 * SIDE, VIS), BF16), shape((SUBS, 2 * SIDE, VIS))), [VMEM], (VMEM, VMEM)
+    )(uv)
+
+    column = rows[:, None]
+    near = call(near_kernel, shape((PEERS * ENDS, 2 * LANES), BF16), [SMEM] + [VMEM] * 2, VMEM)(place, own, column)
+    found = call(
+        gather_kernel, shape((PEERS, 64, LANES), BF16), [SMEM] + [VMEM] * 4, VMEM
+    )(place, other, column, near, patches)
+    got_c = exchange(found, ACROSS)
+
+    owner = offsets[0] >> 8
     same = owner[:, None] == owner[None, :]
     earlier = jnp.arange(SUBS)[:, None] > jnp.arange(SUBS)[None, :]
     slot = owner * 2 + jnp.sum((same & earlier).astype(S32), axis=1)
-    code = (offsets[:, 0] & 255) * LANES + offsets[:, 1]
-    placed = slot[:, None] == jnp.arange(SLOTS, dtype=S32)[None, :]
-    codes = jnp.sum(jnp.where(placed, code[:, None], 0), axis=0)
-    asked = jnp.concatenate([row, codes, jnp.zeros((LANES - ENDS - SLOTS,), S32)]).astype(F32)
-    asked = jnp.broadcast_to(asked[None, None, :], (PEERS, 1, LANES))
-
-    got_a = exchange(jnp.concatenate([mine, asked, jnp.zeros_like(asked)], axis=1), ACROSS)
-    part = got_a[:, :2, :].reshape(1, ROWS, LANES)
-    table = exchange(jnp.broadcast_to(part, (BLOCKS, ROWS, LANES)), DEPTH)
-
-    wanted = got_a[:, 2, :].astype(S32)
-    rows = wanted[:, :ENDS].reshape(PEERS * ENDS)
-    place = jnp.stack([tile, lax.axis_index("x").astype(S32)])
-    patches = cut(place, wanted[:, ENDS : ENDS + SLOTS], grid)
-
-    found = call(
-        gather_kernel, shape((PEERS, 64, LANES), BF16), [VMEM] * 3, VMEM
-    )(table.reshape(SCREENS, LANES), rows[:, None], patches)
-    got_c = exchange(found, ACROSS)
-
-    tables = [jnp.asarray(t) for t in dft_tables()]
-    result, grads = call(
-        main_kernel,
-        (shape((SUBS, 8, VIS)), shape((PEERS * ENDS, LANES))),
-        [SMEM] + [VMEM] * 7,
-        (VMEM, VMEM),
-        [pltpu.VMEM((PEERS * ENDS, LANES), F32)],
-    )(slot, got_c, uv, observed, flags, *tables)
+    result, grads = main(slot, got_c, *waves, observed, flags)
 
     back_c = exchange(grads.reshape(PEERS, ENDS, LANES), ACROSS)
-    dense = call(
-        scatter_kernel, shape((SCREENS, LANES)), [VMEM] * 2, VMEM
-    )(back_c.reshape(PEERS * ENDS, LANES), rows[None, :])
-    back_b = exchange(dense.reshape(BLOCKS, ROWS, LANES), DEPTH)
+    half = shape((HALF, LANES))
+    back_c = back_c.reshape(PEERS * ENDS, LANES)
+    first = HALF * place[2:3]
+    scatter = call(scatter_kernel, half, [SMEM, VMEM, VMEM], VMEM)
+    lend = scatter(HALF - first, back_c, rows[None, :])
+    other = lax.ppermute(lend, "core", SWAP)
+    keep = scatter(first, back_c, rows[None, :])
+    dense = call(pair_kernel, half, [VMEM] * 2, VMEM)(keep, other)
+    back_b = exchange(dense.reshape(LAYERS, ROWS, LANES), "z")
     summed = call(add_kernel, shape((PEERS, ENDS, LANES)), [VMEM], VMEM)(back_b)
     back_a = exchange(summed, ACROSS)
     total = call(place_kernel, shape((ENDS, 4, SIDE * SIDE)), [VMEM], VMEM)(back_a)

time: 142 us -> 131 us (0.923)
  blocking collectives: 55.6 us -> 31.7 us
  starting transfers between devices: 20.8 us -> 33.6 us
  waiting for transfers between devices: 43 us -> 46.8 us
  local copies, waits for them, and re-layouts: 3.7 us -> 0.38 us
  Pallas kernels: 17 us -> 15.5 us
    all_to_all x3 -> x2, blocking collectives: 55.6 us -> 31.7 us  [exchange(): return lax.all_to_all(x, axes, split_axis=0, concat_axis=0, tiled=True)]
    all_to_all x3 -> x4, starting transfers between devices: 20.8 us -> 29.8 us  [exchange(): return lax.all_to_all(x, axes, split_axis=0, concat_axis=0, tiled=True)]
    ppermute x0 -> x2, starting transfers between devices: none -> 3.83 us  [the longest x1 1.92 us: body(): other = lax.ppermute(lend, 'core', SWAP)]
    all_to_all x3 -> x4, waiting for transfers between devices: 43 us -> 45.2 us  [exchange(): return lax.all_to_all(x, axes, split_axis=0, concat_axis=0, tiled=True)]
    unnamed x22 -> x18, local copies, waits for them, and re-layouts: 2.08 us -> 0.05 us
    pallas_call x1, Pallas kernels: 3.48 us -> 1.68 us  [cut(): pl.pallas_call(cut_kernel, out_shape=shape((PEERS, SIDE, LANES), BF16), g...]
    ppermute x0 -> x2, waiting for transfers between devices: none -> 1.57 us  [the longest x1 1.19 us: body(): other = lax.ppermute(lend, 'core', SWAP)]
    pallas_call x3 -> x9, Pallas kernels: 12.4 us -> 12.7 us  [the longest x1 5.51 us: main(): call(main_kernel, (shape((SUBS, 8, VIS)), shape((PEERS * ENDS, LANES))),...]
  transfers between devices with their start and end apart: 3 -> 6, of which waited for: 3 -> 6; matrix products, arithmetic and copies ran while one was open for 0% -> 2% of each run, Pallas kernels for 2% -> 3%
where the time goes in v2:
time: 131 us; the launch traced here: 130 us
  waiting for transfers between devices  46.8 us (36%)
  starting transfers between devices  33.6 us (26%)
  blocking collectives  31.7 us (24%)
  Pallas kernels  15.5 us (12%)
  other arithmetic  1.63 us (1%)
    all_to_all x4, waiting for transfers between devices, exchange(): return lax.all_to_all(x, axes, split_axis=0, concat_axis=0, tiled=True)  45.2 us
    all_to_all x2, blocking collectives, exchange(): return lax.all_to_all(x, axes, split_axis=0, concat_axis=0, tiled=True)  31.7 us
    all_to_all x4, starting transfers between devices, exchange(): return lax.all_to_all(x, axes, split_axis=0, concat_axis=0, tiled=True)  29.8 us
    pallas_call x1, Pallas kernels, main(): call(main_kernel, (shape((SUBS, 8, VIS)), shape((PEERS * ENDS, LANES))),...  5.51 us
  transfers between devices with their start and end apart: 6, of which 6 were waited for; matrix products, arithmetic and copies ran while one was open for 2% of the time, Pallas kernels for 3%

profile of v2, /device:TPU:8, one launch (start us, length us, event | category | flops | bytes accessed | tf_op | source)
XLA Modules:
  0.0 130.5 jit_solution(2849439232181921699)
XLA Ops:
  0.6 1.8 %shard_map.122 = f32[32,4,128]{2,1,0:T(4,128)} custom-call(s32[2,8]{1,0:T(2,128)} %bitcast.24, s32[8]{0:T(128)} %intervals_in.1, s32[2,8]{1,0:T(2,128)} %bitcast.25, f32[8,2,4,1024]{3,2,1,0:T(4,128)} %terms_in.1), custom_call_target="tpu_custom_call" | custom-call | tf_op jit(solution)/shard_map/pallas_call | solution.py:427
  2.5 10.2 %all-to-all-start = ((f32[32,4,128]{2,1,0:T(4,128)}), f32[32,4,128]{2,1,0:T(4,128)S(1)}, u32[]{:S(2)}, u32[]{:S(2)}) async-start(f32[32,4,128]{2,1,0:T(4,128)} %shard_map.122), calls=%async_computation | async-start | bytes 131072 | tf_op jit(solution)/shard_map/all_to_all | solution.py:396
  12.6 9.1 %all-to-all-done.got_ref = f32[32,4,128]{2,1,0:T(4,128)S(1)} async-done(((f32[32,4,128]{2,1,0:T(4,128)}), f32[32,4,128]{2,1,0:T(4,128)S(1)}, u32[]{:S(2)}, u32[]{:S(2)}) %all-to-all-start) | async-done | bytes 65568 | tf_op jit(solution)/shard_map/all_to_all | solution.py:396
  21.7 0.7 shard_map.123
  22.5 10.3 %all-to-all-start.1 = ((f32[8,64,128]{2,1,0:T(8,128)}), f32[8,64,128]{2,1,0:T(8,128)S(1)}, u32[]{:S(2)}, u32[]{:S(2)}) async-start(f32[8,64,128]{2,1,0:T(8,128)} %shard_map.123), calls=%async_computation.1 | async-start | bytes 524288 | tf_op jit(solution)/shard_map/all_to_all | solution.py:396
  32.8 0.1 pad_add_fusion.place_ref
  32.9 0.1 fusion.1
  33.0 1.7 %shard_map.124.patch_ref = bf16[32,32,128]{2,1,0:T(8,128)(2,1)S(1)} custom-call(s32[3]{0:T(128)S(1)} %pad_add_fusion.place_ref, s32[32,16]{1,0:T(8,128)S(1)} %get-tuple-element.15.wanted_ref, bf16[8,256,128]{2,1,0:T(8,128)(2,1)S(1)} %copy-done), custom_call_target="tpu_custom_call" | custom-call | tf_op jit(solution)/shard_map/pallas_call | solution.py:377
  34.7 8.8 %all-to-all-done.1 = f32[8,64,128]{2,1,0:T(8,128)S(1)} async-done(((f32[8,64,128]{2,1,0:T(8,128)}), f32[8,64,128]{2,1,0:T(8,128)S(1)}, u32[]{:S(2)}, u32[]{:S(2)}) %all-to-all-start.1) | async-done | bytes 262176 | tf_op jit(solution)/shard_map/all_to_all | solution.py:396
  43.5 1.9 %collective-permute-start = (f32[512,128]{1,0:T(8,128)S(1)}, f32[512,128]{1,0:T(8,128)S(1)}, u32[]{:S(2)}, u32[]{:S(2)}) collective-permute-start(f32[512,128]{1,0:T(8,128)S(1)} %bitcast.20), channel_id=1, source_target_pairs={{0,8},{8,0},{1,9},{9,1},{2,10},{10,2},{3,11},{11,3},{4,12},{12,4},... | collective-permute-start | bytes 786440 | tf_op jit(solution)/shard_map/ppermute | solution.py:448
  45.4 0.2 broadcast_in_dim_reshape.9.row_ref
  45.6 0.0 copy-start.1
  45.7 0.9 shard_map.125.near_ref
  46.5 0.4 collective-permute-done.table_ref
  46.9 1.7 %shard_map.126 = bf16[32,64,128]{2,1,0:T(8,128)(2,1)} custom-call(s32[3]{0:T(128)S(1)} %pad_add_fusion.place_ref, f32[512,128]{1,0:T(8,128)S(1)} %collective-permute-done.table_ref, s32[512,1]{1,0:T(8,128)S(1)} %broadcast_in_dim_reshape.9.row_ref, bf16[512,256]{1,0:T(8,128)(2,1)S(1)} %shard_map.125.near_ref, bf16[32,32,128]{2,1,0:T(8,128)(2,1)S(1)} %shard_map.124.patch_ref), custom_call_target="tpu_custom_call" | custom-call | tf_op jit(solution)/shard_map/pallas_call | solution.py:455
  48.6 4.5 %all-to-all-start.2 = ((bf16[32,64,128]{2,1,0:T(8,128)(2,1)}), bf16[32,64,128]{2,1,0:T(8,128)(2,1)S(1)}, u32[]{:S(2)}, u32[]{:S(2)}) async-start(bf16[32,64,128]{2,1,0:T(8,128)(2,1)} %shard_map.126), calls=%async_computation.2 | async-start | bytes 1048576 | tf_op jit(solution)/shard_map/all_to_all | solution.py:396
  53.1 1.5 %shard_map.127 = (bf16[8,192,512]{2,1,0:T(8,128)(2,1)S(1)}, f32[8,64,512]{2,1,0:T(8,128)S(1)}) custom-call(f32[8,2,512]{2,1,0:T(2,128)S(1)} %copy-done.3), custom_call_target="tpu_custom_call" | custom-call | tf_op jit(solution)/shard_map/pallas_call | solution.py:449
  54.5 0.7 shift-right-arithmetic_bitcast_fusion
  55.2 0.2 convert_reduce_fusion
  55.4 0.7 multiply_add_fusion.slot_ref
  56.1 15.3 %all-to-all-done.2.got_ref = bf16[32,64,128]{2,1,0:T(8,128)(2,1)S(1)} async-done(((bf16[32,64,128]{2,1,0:T(8,128)(2,1)}), bf16[32,64,128]{2,1,0:T(8,128)(2,1)S(1)}, u32[]{:S(2)}, u32[]{:S(2)}) %all-to-all-start.2) | async-done | bytes 524320 | tf_op jit(solution)/shard_map/all_to_all | solution.py:396
  71.4 5.5 %shard_map.128 = (f32[8,8,512]{2,1,0:T(8,128)}, f32[512,128]{1,0:T(8,128)}) custom-call(s32[8]{0:T(128)S(1)} %multiply_add_fusion.slot_ref, bf16[32,64,128]{2,1,0:T(8,128)(2,1)S(1)} %all-to-all-done.2.got_ref, bf16[8,192,512]{2,1,0:T(8,128)(2,1)S(1)} %get-tuple-element.10.row_wave_in, f32[8,64,512]{2,1,0:T(8,128)S(1)} %get-tuple-element.11.column_wave_in, ...), custom_call_target="tpu_custom_call" | custom-call | tf_op jit(solution)/shard_map/pallas_call | solution.py:401
  77.0 4.8 %all-to-all-start.3 = ((f32[32,16,128]{2,1,0:T(8,128)}), f32[32,16,128]{2,1,0:T(8,128)S(1)}, u32[]{:S(2)}, u32[]{:S(2)}) async-start(f32[32,16,128]{2,1,0:T(8,128)} %bitcast.8), calls=%async_computation.3 | async-start | bytes 524288 | tf_op jit(solution)/shard_map/all_to_all | solution.py:396
  81.8 0.1 broadcast_in_dim_reshape.8.row_ref
  81.9 12.0 %all-to-all-done.3 = f32[32,16,128]{2,1,0:T(8,128)S(1)} async-done(((f32[32,16,128]{2,1,0:T(8,128)}), f32[32,16,128]{2,1,0:T(8,128)S(1)}, u32[]{:S(2)}, u32[]{:S(2)}) %all-to-all-start.3) | async-done | bytes 262176 | tf_op jit(solution)/shard_map/all_to_all | solution.py:396
  93.9 0.3 shard_map.130
  94.2 1.9 %collective-permute-start.1 = (f32[512,128]{1,0:T(8,128)S(1)}, f32[512,128]{1,0:T(8,128)S(1)}, u32[]{:S(2)}, u32[]{:S(2)}) collective-permute-start(f32[512,128]{1,0:T(8,128)S(1)} %shard_map.130), channel_id=1, source_target_pairs={{0,8},{8,0},{1,9},{9,1},{2,10},{10,2},{3,11},{11,3},{4,12},{12,4},... | collective-permute-start | bytes 786440 | tf_op jit(solution)/shard_map/ppermute | solution.py:472
  96.1 0.3 shard_map.129.keep_ref
  96.5 1.2 collective-permute-done.1.other_ref
  97.7 14.9 %all_to_all.30.parts_ref = f32[8,64,128]{2,1,0:T(8,128)S(1)} all-to-all(f32[8,64,128]{2,1,0:T(8,128)S(1)} %bitcast.19), channel_id=1, replica_groups=mesh['z'=8,'x'=4,'core'=2,'tile'=8] {'z'}, dimensions={0} | all-to-all | bytes 524288 | tf_op jit(solution)/shard_map/all_to_all | solution.py:396
  112.6 16.9 %all_to_all.31.parts_ref = f32[32,16,128]{2,1,0:T(8,128)S(1)} all-to-all(f32[32,16,128]{2,1,0:T(8,128)S(1)} %shard_map.132), channel_id=1, replica_groups=mesh['z'=8,'x'=4,'core'=2,'tile'=8] {'x','tile'}, dimensions={0} | all-to-all | bytes 524288 | tf_op jit(solution)/shard_map/all_to_all | solution.py:396
  129.4 1.1 shard_map.133
  (21 shorter events, 0.1 us)
Async XLA Ops:
  0.6 32.3 %copy-start = (bf16[8,256,128]{2,1,0:T(8,128)(2,1)S(1)}, bf16[8,256,128]{2,1,0:T(8,128)(2,1)}, u32[]{:S(2)}) copy-start(bf16[8,256,128]{2,1,0:T(8,128)(2,1)} %strip_ref.1) | copy-start | bytes 1572868
  2.5 19.3 %all-to-all-start = ((f32[32,4,128]{2,1,0:T(4,128)}), f32[32,4,128]{2,1,0:T(4,128)S(1)}, u32[]{:S(2)}, u32[]{:S(2)}) async-start(f32[32,4,128]{2,1,0:T(4,128)} %shard_map.122), calls=%async_computation | async-start | bytes 131072 | tf_op jit(solution)/shard_map/all_to_all | solution.py:396
  22.5 21.0 %all-to-all-start.1 = ((f32[8,64,128]{2,1,0:T(8,128)}), f32[8,64,128]{2,1,0:T(8,128)S(1)}, u32[]{:S(2)}, u32[]{:S(2)}) async-start(f32[8,64,128]{2,1,0:T(8,128)} %shard_map.123), calls=%async_computation.1 | async-start | bytes 524288 | tf_op jit(solution)/shard_map/all_to_all | solution.py:396
  33.0 15.6 %copy-start.7 = (s32[32,16]{1,0:T(8,128)}, s32[32,16]{1,0:T(8,128)S(1)}, u32[]{:S(2)}) copy-start(s32[32,16]{1,0:T(8,128)S(1)} %get-tuple-element.14) | copy-start | bytes 6148
  43.5 3.4 %collective-permute-start = (f32[512,128]{1,0:T(8,128)S(1)}, f32[512,128]{1,0:T(8,128)S(1)}, u32[]{:S(2)}, u32[]{:S(2)}) collective-permute-start(f32[512,128]{1,0:T(8,128)S(1)} %bitcast.20), channel_id=1, source_target_pairs={{0,8},{8,0},{1,9},{9,1},{2,10},{10,2},{3,11},{11,3},{4,12},{12,4},... | collective-permute-start | bytes 786440 | tf_op jit(solution)/shard_map/ppermute | solution.py:448
  45.6 7.5 %copy-start.3 = (f32[8,2,512]{2,1,0:T(2,128)S(1)}, f32[8,2,512]{2,1,0:T(2,128)}, u32[]{:S(2)}) copy-start(f32[8,2,512]{2,1,0:T(2,128)} %uv_ref.1) | copy-start | bytes 98308
  45.6 25.8 %copy-start.1 = (bf16[384,256]{1,0:T(8,128)(2,1)S(1)}, bf16[384,256]{1,0:T(8,128)(2,1)}, u32[]{:S(2)}) copy-start(bf16[384,256]{1,0:T(8,128)(2,1)} %constant.29.clone.cols_ref) | copy-start | bytes 589828
  45.6 25.8 %copy-start.2 = (f32[8,8,512]{2,1,0:T(8,128)S(1)}, f32[8,8,512]{2,1,0:T(8,128)}, u32[]{:S(2)}) copy-start(f32[8,8,512]{2,1,0:T(8,128)} %seen_in.1) | copy-start | bytes 393220
  45.6 25.8 %copy-start.4 = (s32[8,512]{1,0:T(8,128)S(1)}, s32[8,512]{1,0:T(8,128)}, u32[]{:S(2)}) copy-start(s32[8,512]{1,0:T(8,128)} %flag_in.1) | copy-start | bytes 49156
  45.6 25.8 %copy-start.5 = (f32[32,128]{1,0:T(8,128)S(1)}, f32[32,128]{1,0:T(8,128)}, u32[]{:S(2)}) copy-start(f32[32,128]{1,0:T(8,128)} %constant.30.clone.taper_ref) | copy-start | bytes 49156
  45.6 25.8 %copy-start.6 = (bf16[64,96]{1,0:T(8,128)(2,1)S(1)}, bf16[64,96]{1,0:T(8,128)(2,1)}, u32[]{:S(2)}) copy-start(bf16[64,96]{1,0:T(8,128)(2,1)} %constant.28.clone.rows_ref) | copy-start | bytes 36868
  48.6 22.8 %all-to-all-start.2 = ((bf16[32,64,128]{2,1,0:T(8,128)(2,1)}), bf16[32,64,128]{2,1,0:T(8,128)(2,1)S(1)}, u32[]{:S(2)}, u32[]{:S(2)}) async-start(bf16[32,64,128]{2,1,0:T(8,128)(2,1)} %shard_map.126), calls=%async_computation.2 | async-start | bytes 1048576 | tf_op jit(solution)/shard_map/all_to_all | solution.py:396
  71.4 10.4 %copy-start.8 = (s32[32,16]{1,0:T(8,128)S(1)}, s32[32,16]{1,0:T(8,128)}, u32[]{:S(2)}) copy-start(s32[32,16]{1,0:T(8,128)} %copy-done.7) | copy-start | bytes 6148
  77.0 17.0 %all-to-all-start.3 = ((f32[32,16,128]{2,1,0:T(8,128)}), f32[32,16,128]{2,1,0:T(8,128)S(1)}, u32[]{:S(2)}, u32[]{:S(2)}) async-start(f32[32,16,128]{2,1,0:T(8,128)} %bitcast.8), calls=%async_computation.3 | async-start | bytes 524288 | tf_op jit(solution)/shard_map/all_to_all | solution.py:396
  94.2 3.4 %collective-permute-start.1 = (f32[512,128]{1,0:T(8,128)S(1)}, f32[512,128]{1,0:T(8,128)S(1)}, u32[]{:S(2)}, u32[]{:S(2)}) collective-permute-start(f32[512,128]{1,0:T(8,128)S(1)} %shard_map.130), channel_id=1, source_target_pairs={{0,8},{8,0},{1,9},{9,1},{2,10},{10,2},{3,11},{11,3},{4,12},{12,4},... | collective-permute-start | bytes 786440 | tf_op jit(solution)/shard_map/ppermute | solution.py:472

commit v3 on v2

v3 whole, which is shorter than its diff:
```python
import jax
import jax.numpy as jnp
import numpy as np
from jax import lax
from jax.experimental import pallas as pl
from jax.experimental.pallas import tpu as pltpu
from jax.sharding import Mesh
from jax.sharding import PartitionSpec as P

SIDE = 32
SUBS = 8
ENDS = 2 * SUBS
VIS = 512
PEERS = 64
GROUPS = 8
ROWS = 64
TABLE = GROUPS * ROWS
LANES = 128
SLOTS = 16

F32 = jnp.float32
BF16 = jnp.bfloat16
S32 = jnp.int32


def bf16_parts(array, count):
    rest = np.asarray(array, np.float64)
    parts = []
    for _ in range(count):
        part = rest.astype(np.float32).astype(jnp.bfloat16)
        parts.append(part)
        rest = rest - part.astype(np.float64)
    return parts


def dft_tables():
    index = np.arange(SIDE)
    angle = 2.0 * np.pi * (index[:, None] * index[None, :] % SIDE) / SIDE
    f_real = np.cos(angle) / SIDE
    f_imag = np.sin(angle) / SIDE
    rows = np.concatenate([f_real, f_imag], axis=0)
    rows_parts = np.concatenate(bf16_parts(rows, 3), axis=1)
    eye = np.eye(4)
    cols = np.concatenate([np.kron(eye, f_real.T), np.kron(eye, f_imag.T)], axis=1)
    hi, lo = bf16_parts(cols, 2)
    cols_parts = np.concatenate([hi, hi, lo], axis=0)
    edge = np.cos(np.pi * (index - (SIDE - 1) / 2.0) / SIDE)
    taper = np.tile(edge[:, None] * edge[None, :], (1, 4)).astype(np.float32)
    return rows_parts, cols_parts, taper


def turn_polynomials():
    nodes = 0.25 * np.cos(np.pi * (np.arange(400) + 0.5) / 400) ** 2
    r = np.sqrt(nodes)
    scaled = nodes * 4.0
    sine = np.polynomial.polynomial.polyfit(scaled, np.sin(2 * np.pi * r) / r, 7)
    cosine = np.polynomial.polynomial.polyfit(scaled, np.cos(2 * np.pi * r), 8)
    power = 4.0 ** np.arange(9)
    return [float(a) for a in sine * power[:8]], [float(a) for a in cosine * power]


SINE, COSINE = turn_polynomials()


def unit_circle(turns):
    r = turns - jnp.floor(turns + 0.5)
    r2 = r * r
    s = jnp.full_like(r, SINE[-1])
    for a in SINE[-2::-1]:
        s = s * r2 + a
    c = jnp.full_like(r, COSINE[-1])
    for a in COSINE[-2::-1]:
        c = c * r2 + a
    return c, s * r


def split(x):
    hi = x.astype(BF16)
    return hi, (x - hi.astype(F32)).astype(BF16)


def dot(a, b, contract):
    return lax.dot_general(a, b, ((contract[:1], contract[1:]), ((), ())), preferred_element_type=F32)


def slots(offsets_ref):
    tiles = [offsets_ref[0, k] >> 8 for k in range(SUBS)]
    seconds = []
    for k in range(SUBS):
        second = jnp.zeros((), S32)
        for j in range(k):
            second = jnp.where(tiles[j] == tiles[k], 1, second)
        seconds.append(second)
    return tiles, seconds


def prep_kernel(
    stations_in, intervals_in, offsets_in, terms_in, out_ref, stations_ref, intervals_ref, offsets_ref, terms_ref, sems
):
    own = lax.axis_index("tile")
    copies = [
        pltpu.make_async_copy(stations_in, stations_ref, sems.at[0]),
        pltpu.make_async_copy(intervals_in, intervals_ref, sems.at[1]),
        pltpu.make_async_copy(offsets_in, offsets_ref, sems.at[2]),
        pltpu.make_async_copy(terms_in.at[own], terms_ref, sems.at[3]),
    ]
    for copy in copies:
        copy.start()
    for copy in copies[:3]:
        copy.wait()
    spot = lax.broadcasted_iota(S32, (1, LANES), 1)
    asked = jnp.zeros((1, LANES), S32)
    tiles, seconds = slots(offsets_ref)
    for k in range(SUBS):
        for end in range(2):
            station = stations_ref[end, k]
            row = ((station >> 3) & 7) * ROWS + (station >> 6) * 8 + (station & 7)
            asked = jnp.where(spot == end * SUBS + k, row + TABLE * intervals_ref[k], asked)
        code = (offsets_ref[0, k] & 255) * LANES + offsets_ref[1, k]
        asked = jnp.where(spot == ENDS + 2 * tiles[k] + seconds[k], code, asked)
    out_ref[:, 1:2, :] = jnp.broadcast_to(asked.astype(F32).reshape(1, 1, LANES), (PEERS, 1, LANES))
    copies[3].wait()
    lane = spot // SIDE
    for block in range(8):
        turned = []
        for interval in range(2):
            comps = terms_ref[interval, :, block * LANES : (block + 1) * LANES]
            turned.append([comps if d == 0 else pltpu.roll(comps, d * SIDE, 1) for d in range(4)])
        for i in range(4):
            for half in range(2):
                total = jnp.zeros((1, LANES), F32)
                for place in range(4):
                    comp = 2 * half + (place & 1)
                    piece = turned[place >> 1][(place - i) % 4][comp : comp + 1, :]
                    total = piece if place == 0 else jnp.where(lane == place, piece, total)
                out_ref[(4 * block + i) * 2 + half, 0:1, :] = total


def wave_kernel(uv_ref, row_wave_ref, column_wave_ref):
    centre = (lax.broadcasted_iota(S32, (SIDE, VIS), 0).astype(F32) - SIDE / 2.0) * (1.0 / SIDE)

    def one(k, carry):
        real, imag = unit_circle(uv_ref[k, 0:1, :] * centre)
        hi, lo = split(jnp.concatenate([real, imag], axis=0))
        row_wave_ref[k] = jnp.concatenate([hi, lo], axis=0)
        real, imag = unit_circle(uv_ref[k, 1:2, :] * centre)
        column_wave_ref[k] = jnp.concatenate([real, imag], axis=0)
        return carry

    lax.fori_loop(0, SUBS, one, 0)


def cut_kernel(place_ref, wanted_ref, strip_ref, out_ref, wide_ref):
    wide_ref[...] = strip_ref[0].astype(F32)
    tile = place_ref[0]
    part_of = place_ref[1]
    half = SIDE // 2
    lane = lax.broadcasted_iota(S32, (half, LANES), 1) // SIDE

    def one(i, carry):
        total = jnp.zeros((half, LANES), F32)
        for slot in range(2):
            code = wanted_ref[i, 2 * tile + slot]
            row = code >> 7
            column = code & (LANES - 1)
            for part in range(2):
                spot = (part_of + 2 * slot + part) & 3
                piece = wide_ref[pl.ds(row + half * part, half), :]
                piece = pltpu.roll(piece, (spot * SIDE + LANES - column) & (LANES - 1), 1)
                total = jnp.where(lane == spot, piece, total)
        out_ref[i] = total.astype(BF16)
        return carry

    lax.fori_loop(0, PEERS, one, 0, unroll=8)


def spread_kernel(got_ref, out_ref):
    part = got_ref[:, 0:1, :].reshape(ROWS, LANES)
    for i in range(GROUPS):
        out_ref[i] = part


def gather_kernel(table_ref, first_ref, second_ref, patch_ref, out_ref):
    hi, lo = split(table_ref[...])
    table = jnp.concatenate([hi, lo], axis=1)
    ids = lax.broadcasted_iota(S32, (TABLE, TABLE), 1)
    left = lax.broadcasted_iota(S32, (TABLE, LANES), 1) < LANES // 2
    sides = []
    for code_ref in (first_ref, second_ref):
        code = code_ref[...]
        chosen = jnp.where(ids == (code & (TABLE - 1)), 1.0, 0.0).astype(BF16)
        found = dot(chosen, table, (1, 0))
        found = found[:, :LANES] + found[:, LANES:]
        sides.append((found, pltpu.roll(found, LANES // 2, 1), code >= TABLE))
    first = jnp.where(sides[0][2], sides[0][1], sides[0][0])
    second = jnp.where(sides[1][2], sides[1][0], sides[1][1])
    beams = jnp.where(left, first, second)
    hi = beams.astype(BF16).astype(F32)
    both = jnp.concatenate([hi.reshape(PEERS, SUBS, LANES), (beams - hi).reshape(PEERS, SUBS, LANES)], axis=1)
    out_ref[:, 0:ENDS, :] = both.astype(BF16)
    out_ref[:, ENDS : 2 * ENDS, :] = patch_ref[...]


def scatter_kernel(got_ref, first_ref, second_ref, first_row_ref, second_row_ref, out_ref):
    got = got_ref[...]
    turned = pltpu.roll(got, LANES // 2, 1)
    left = lax.broadcasted_iota(S32, (TABLE, LANES), 1) < LANES // 2
    ids = lax.broadcasted_iota(S32, (TABLE, TABLE), 0)
    values, chosen = [], []
    for spread, code_ref, row_ref in (
        (jnp.where(left, got, turned), first_ref, first_row_ref),
        (jnp.where(left, turned, got), second_ref, second_row_ref),
    ):
        late = code_ref[...] >= TABLE
        values.append(jnp.where(late != left, spread, 0.0))
        chosen.append(jnp.where(ids == (row_ref[...] & (TABLE - 1)), 1.0, 0.0).astype(BF16))
    hi, lo = split(jnp.concatenate(values, axis=0))
    total = dot(jnp.concatenate(chosen, axis=1), jnp.concatenate([hi, lo], axis=1), (1, 0))
    out_ref[...] = total[:, :LANES] + total[:, LANES:]


def add_kernel(parts_ref, out_ref):
    total = parts_ref[0]
    for i in range(1, GROUPS):
        total = total + parts_ref[i]
    for i in range(PEERS):
        part = i // 8
        out_ref[i] = total[part * SUBS : (part + 1) * SUBS, :]


def place_kernel(parts_ref, out_ref):
    lane = lax.broadcasted_iota(S32, (SUBS, LANES), 1) // SIDE
    for block in range(8):
        for half in range(2):
            rows = [parts_ref[2 * (4 * block + i) + half] for i in range(4)]
            turned = [[rows[i] if d == 0 else pltpu.roll(rows[i], d * SIDE, 1) for d in range(4)] for i in range(4)]
            for interval in range(2):
                for part in range(2):
                    at = 2 * interval + part
                    total = turned[0][(0 - at) % 4]
                    for i in range(1, 4):
                        total = jnp.where(lane == i, turned[i][(i - at) % 4], total)
                    out_ref[:, interval, 2 * half + part, block * LANES : (block + 1) * LANES] = total


def main_kernel(
    slot_ref, got_ref, row_wave_in, column_wave_in, seen_in, flag_in, rows_ref, cols_ref, taper_ref,
    res_ref, grad_ref, beam_ref, row_wave_ref, column_wave_ref, seen_ref, flag_ref, side_ref, z_ref, dz_ref, held_ref, sems,
):
    copies = [
        pltpu.make_async_copy(a, b, sems.at[i])
        for i, (a, b) in enumerate(
            ((row_wave_in, row_wave_ref), (column_wave_in, column_wave_ref), (seen_in, seen_ref), (flag_in, flag_ref))
        )
    ]
    for copy in copies:
        copy.start()
    got = got_ref[:, 0:ENDS, :].astype(F32)
    beam_ref[...] = (got[:, :SUBS] + got[:, SUBS:]).reshape(TABLE, LANES)
    narrow = lax.broadcasted_iota(S32, (SIDE // 2, LANES), 1) // SIDE
    lane = lax.broadcasted_iota(S32, (SIDE, LANES), 1) // SIDE
    taper = taper_ref[...]

    def turn(x, blocks):
        return pltpu.roll(x, blocks * SIDE, 1)

    patches = []
    for k in range(SUBS):
        slot = slot_ref[k]
        tile = slot >> 1
        second = (slot & 1) > 0
        shift = 2 * (slot & 1)
        upper = (narrow - shift) & 3
        lower = (narrow - shift - 1) & 3
        for part in range(2):
            top = jnp.zeros((SIDE // 2, LANES), F32)
            low = top
            for i in range(4):
                piece = got_ref[8 * (4 * part + i) + tile, ENDS : 2 * ENDS, :].astype(F32)
                top = jnp.where(upper == i, piece, top)
                low = jnp.where(lower == i, piece, low)
            top = jnp.where(second, turn(top, 2), top)
            low = jnp.where(second, turn(low, 1), turn(low, 3))
            patches.append(jnp.concatenate([top, low], axis=0).astype(BF16))
    patch = jnp.concatenate(patches, axis=1)
    a = dot(rows_ref[...], jnp.concatenate([patch, patch, patch], axis=0), (1, 0))
    mixed = []
    for k in range(SUBS):
        re = a[:, 2 * k * LANES : (2 * k + 1) * LANES]
        im = a[:, (2 * k + 1) * LANES : (2 * k + 2) * LANES]
        mixed += [re[:SIDE] - im[SIDE:], im[:SIDE] + re[SIDE:]]
    hi, lo = split(jnp.concatenate(mixed, axis=0))
    images = dot(jnp.concatenate([hi, lo, hi], axis=1), cols_ref[...], (1, 0))

    for k in range(SUBS):
        b = images[2 * k * SIDE : 2 * (k + 1) * SIDE]
        i_re = b[:SIDE, :LANES] - b[SIDE:, LANES:]
        i_im = b[:SIDE, LANES:] + b[SIDE:, :LANES]

        sides = []
        for half in range(2):
            g = beam_ref[pl.ds(k + SUBS * half, SIDE, stride=2 * SUBS), :]
            g1, g2 = turn(g, 1), turn(g, 2)
            sides.append((jnp.where(lane == 0, g, jnp.where(lane == 3, g2, g1)), jnp.where(lane < 2, g2, g)))
        (p_re, q_re), (p_im, q_im) = sides

        y_re = i_re * q_re + i_im * q_im
        y_im = i_im * q_re - i_re * q_im
        z_re = (p_re * y_re - p_im * y_im) * taper
        z_im = (p_re * y_im + p_im * y_re) * taper
        for i, part in enumerate((i_re, i_im, p_re, p_im, y_re, y_im)):
            side_ref[k, i] = part * taper if i > 3 else part
        z = jnp.concatenate(
            [jnp.concatenate([z_re, z_im], axis=1), jnp.concatenate([-z_im, z_re], axis=1)], axis=0
        )
        z_hi, z_lo = split(z)
        z_ref[k] = jnp.concatenate([z_hi, z_lo, z_hi], axis=0)

    for copy in copies:
        copy.wait()

    def one(k, carry):
        row_wave = row_wave_ref[k]
        ev_re = column_wave_ref[k, :SIDE, :]
        ev_im = column_wave_ref[k, SIDE:, :]
        w = dot(z_ref[k], jnp.concatenate([row_wave[: 2 * SIDE], row_wave], axis=0), (0, 0))
        reals, imags = [], []
        for pol in range(4):
            w_re = w[pol * SIDE : (pol + 1) * SIDE]
            w_im = w[LANES + pol * SIDE : LANES + (pol + 1) * SIDE]
            reals.append(jnp.sum(w_re * ev_re - w_im * ev_im, axis=0, keepdims=True))
            imags.append(jnp.sum(w_re * ev_im + w_im * ev_re, axis=0, keepdims=True))
        model = jnp.concatenate(reals + imags, axis=0)
        used = flag_ref[pl.ds(k, 1), :].astype(F32)
        res = used * (seen_ref[k] - model)
        res_ref[k] = res
        back = -used * res

        t_re, t_im = [], []
        for pol in range(4):
            d_re = back[pol : pol + 1]
            d_im = back[4 + pol : 5 + pol]
            t_re.append(ev_re * d_re + ev_im * d_im)
            t_im.append(ev_re * d_im - ev_im * d_re)
        t_hi, t_lo = split(jnp.concatenate(t_re + t_im, axis=0))
        held_ref[k, 0] = t_hi
        held_ref[k, 1] = t_lo
        return carry

    def two(k, carry):
        row_wave = row_wave_ref[k]
        t_hi = held_ref[k, 0]
        t_lo = held_ref[k, 1]
        both = dot(row_wave, t_hi, (1, 1))
        dz_ref[k] = both[: 2 * SIDE] + both[2 * SIDE :] + dot(row_wave[: 2 * SIDE], t_lo, (1, 1))
        return carry

    for k in range(SUBS):
        one(k, 0)
    for k in range(SUBS):
        two(k, 0)

    for k in range(SUBS):
        d = dz_ref[k]
        i_re, i_im, p_re, p_im, y_re, y_im = (side_ref[k, i] for i in range(6))
        dz_re = d[:SIDE, :LANES] + d[SIDE:, LANES:]
        dz_im = d[:SIDE, LANES:] - d[SIDE:, :LANES]

        dp_re = dz_re * y_re + dz_im * y_im
        dp_im = dz_im * y_re - dz_re * y_im
        dp_re = dp_re + turn(dp_re, 3)
        dp_im = dp_im + turn(dp_im, 3)
        i_re = i_re * taper
        i_im = i_im * taper
        dy_re = dz_re * p_re + dz_im * p_im
        dy_im = dz_im * p_re - dz_re * p_im
        dq_re = dy_re * i_re + dy_im * i_im
        dq_im = dy_re * i_im - dy_im * i_re
        dq_re = dq_re + turn(dq_re, 2)
        dq_im = dq_im + turn(dq_im, 2)
        for half, (dp, dq) in enumerate(((dp_re, dq_re), (dp_im, dq_im))):
            grad = jnp.where(lane == 0, dp, jnp.where(lane == 1, turn(dp, 3), dq))
            grad_ref[pl.ds(k + SUBS * half, SIDE, stride=2 * SUBS), :] = grad


SMEM = pl.BlockSpec(memory_space=pltpu.SMEM)
VMEM = pl.BlockSpec(memory_space=pltpu.VMEM)
HBM = pl.BlockSpec(memory_space=pltpu.HBM)
PARAMS = pltpu.CompilerParams(vmem_limit_bytes=40 * 1024 * 1024)


def call(kernel, shapes, specs, out_specs, scratch=()):
    return pl.pallas_call(
        kernel,
        out_shape=shapes,
        in_specs=specs,
        out_specs=out_specs,
        scratch_shapes=list(scratch),
        compiler_params=PARAMS,
    )


def shape(dims, dtype=F32):
    return jax.ShapeDtypeStruct(dims, dtype)


def cut(place, wanted, grid):
    return pl.pallas_call(
        cut_kernel,
        out_shape=shape((PEERS, ENDS, LANES), BF16),
        grid_spec=pltpu.PrefetchScalarGridSpec(
            num_scalar_prefetch=2,
            grid=(1,),
            in_specs=[pl.BlockSpec((1, grid.shape[1], LANES), lambda i, place, wanted: (place[1], 0, 0))],
            out_specs=pl.BlockSpec((PEERS, ENDS, LANES), lambda i, place, wanted: (0, 0, 0)),
            scratch_shapes=[pltpu.VMEM((grid.shape[1], LANES), F32)],
        ),
        compiler_params=PARAMS,
    )(place, wanted, grid)


def in_hbm(x):
    return pltpu.with_memory_space_constraint(x, pltpu.HBM)


def exchange(x, axes):
    return lax.all_to_all(x, axes, split_axis=0, concat_axis=0, tiled=True)


def main(slot, got, *rest):
    tables = [jnp.asarray(t) for t in dft_tables()]
    return call(
        main_kernel,
        (shape((SUBS, 8, VIS)), shape((TABLE, LANES))),
        [SMEM, VMEM] + [HBM] * 4 + [VMEM] * 3,
        (VMEM, VMEM),
        [
            pltpu.VMEM((TABLE, LANES), F32),
            pltpu.VMEM((SUBS, 4 * SIDE, VIS), BF16),
            pltpu.VMEM((SUBS, 2 * SIDE, VIS), F32),
            pltpu.VMEM((SUBS, 8, VIS), F32),
            pltpu.VMEM((SUBS, VIS), S32),
            pltpu.VMEM((SUBS, 6, SIDE, LANES), F32),
            pltpu.VMEM((SUBS, 6 * SIDE, 2 * LANES), BF16),
            pltpu.VMEM((SUBS, 2 * SIDE, 2 * LANES), F32),
            pltpu.VMEM((SUBS, 2, 2 * LANES, VIS), BF16),
            pltpu.SemaphoreType.DMA((4,)),
        ],
    )(slot, got, *(in_hbm(x) for x in rest), *tables)


ACROSS = ("z", "tile")
NEAR = ("x", "core")


def body(grid, a_terms, stations, intervals, offsets, uv, observed, flags):
    place = jnp.stack([lax.axis_index(name).astype(S32) for name in ("tile", "z")])
    offsets = offsets.T
    sent = call(
        prep_kernel,
        shape((PEERS, 2, LANES)),
        [HBM] * 4,
        VMEM,
        [
            pltpu.SMEM((2, SUBS), S32),
            pltpu.SMEM((SUBS,), S32),
            pltpu.SMEM((2, SUBS), S32),
            pltpu.VMEM((2, 4, SIDE * SIDE), F32),
            pltpu.SemaphoreType.DMA((4,)),
        ],
    )(*(in_hbm(x) for x in (stations.T, intervals, offsets, a_terms)))
    got_a = exchange(sent, ACROSS)
    spread = call(spread_kernel, shape((GROUPS, ROWS, LANES)), [VMEM], VMEM)(got_a)
    table = exchange(spread, NEAR).reshape(TABLE, LANES)

    wanted = got_a[:, 1, :].astype(S32)
    first = wanted[:, :SUBS].reshape(TABLE)
    second = wanted[:, SUBS:ENDS].reshape(TABLE)
    columns = (first[:, None], second[:, None])
    patches = cut(place, wanted[:, ENDS : ENDS + SLOTS], grid)
    waves = call(
        wave_kernel, (shape((SUBS, 4 * SIDE, VIS), BF16), shape((SUBS, 2 * SIDE, VIS))), [VMEM], (VMEM, VMEM)
    )(uv)

    found = call(gather_kernel, shape((PEERS, 2 * ENDS, LANES), BF16), [VMEM] * 4, VMEM)(table, *columns, patches)
    got_c = exchange(found, ACROSS)

    owner = offsets[0] >> 8
    same = owner[:, None] == owner[None, :]
    earlier = jnp.arange(SUBS)[:, None] > jnp.arange(SUBS)[None, :]
    slot = owner * 2 + jnp.sum((same & earlier).astype(S32), axis=1)
    result, grads = main(slot, got_c, *waves, observed, flags)

    back_c = exchange(grads.reshape(PEERS, SUBS, LANES), ACROSS).reshape(TABLE, LANES)
    dense = call(scatter_kernel, shape((TABLE, LANES)), [VMEM] * 5, VMEM)(
        back_c, *columns, first[None, :], second[None, :]
    )
    back_b = exchange(dense.reshape(GROUPS, ROWS, LANES), NEAR)
    summed = call(add_kernel, shape((PEERS, SUBS, LANES)), [VMEM], VMEM)(back_b)
    back_a = exchange(summed, ACROSS)
    total = call(place_kernel, shape((SUBS, 2, 4, SIDE * SIDE)), [VMEM], VMEM)(back_a)
    return (result, total)


def solution(mesh):
    fine = Mesh(mesh.devices.reshape(8, 4, 2, 8), ("z", "x", "core", "tile"))
    st = ("z", "x", "core")
    every = ("z", "x", "core", "tile")
    placed = (
        P(None, "tile", None),
        P(st, None, None, None),
        P(every, None),
        P(every),
        P(every, None),
        P(every, None, None),
        P(every, None, None),
        P(every, None),
    )
    return jax.shard_map(
        body,
        mesh=fine,
        in_specs=placed,
        out_specs=(P(every, None, None), P(st, None, None, None)),
        check_vma=False,
    )
```

time: 131 us -> 125 us (0.954)
  blocking collectives: 31.7 us -> 28.6 us
  local copies, waits for them, and re-layouts: 0.38 us -> 3.16 us
  waiting for transfers between devices: 46.8 us -> 44.7 us
  starting transfers between devices: 33.6 us -> 31.8 us
  other arithmetic: 1.63 us -> 0.28 us
    ppermute x2 -> x0, starting transfers between devices: 3.83 us -> none  [the longest x1 1.92 us: body(): other = lax.ppermute(lend, 'core', SWAP)]
    all_to_all x2, blocking collectives: 31.7 us -> 28.6 us  [exchange(): return lax.all_to_all(x, axes, split_axis=0, concat_axis=0, tiled=True)]
    unnamed x18 -> x16, local copies, waits for them, and re-layouts: 0.05 us -> 2.54 us
    all_to_all x4, starting transfers between devices: 29.8 us -> 31.8 us  [exchange(): return lax.all_to_all(x, axes, split_axis=0, concat_axis=0, tiled=True)]
    ppermute x2 -> x0, waiting for transfers between devices: 1.57 us -> none  [the longest x1 1.19 us: body(): other = lax.ppermute(lend, 'core', SWAP)]
    pallas_call x12 -> x9, Pallas kernels: 15.5 us -> 14.9 us  [the longest x1 5.91 us: main(): call(main_kernel, (shape((SUBS, 8, VIS)), shape((TABLE, LANES))), [SMEM,...]
  transfers between devices with their start and end apart: 6 -> 4, of which waited for: 6 -> 4; matrix products, arithmetic and copies ran while one was open for 2% -> 1% of each run, Pallas kernels for 3% -> 3%
where the time goes in v3:
time: 125 us; the launch traced here: 124 us
  waiting for transfers between devices  44.7 us (36%)
  starting transfers between devices  31.8 us (25%)
  blocking collectives  28.6 us (23%)
  Pallas kernels  14.9 us (12%)
  local copies, waits for them, and re-layouts  3.16 us (3%)
    all_to_all x4, waiting for transfers between devices, exchange(): return lax.all_to_all(x, axes, split_axis=0, concat_axis=0, tiled=True)  44.7 us
    all_to_all x4, starting transfers between devices, exchange(): return lax.all_to_all(x, axes, split_axis=0, concat_axis=0, tiled=True)  31.8 us
    all_to_all x2, blocking collectives, exchange(): return lax.all_to_all(x, axes, split_axis=0, concat_axis=0, tiled=True)  28.6 us
    pallas_call x1, Pallas kernels, main(): call(main_kernel, (shape((SUBS, 8, VIS)), shape((TABLE, LANES))), [SMEM,...  5.91 us
    unnamed x16, local copies, waits for them, and re-layouts  2.54 us
  transfers between devices with their start and end apart: 4, of which 4 were waited for; matrix products, arithmetic and copies ran while one was open for 1% of the time, Pallas kernels for 3%

profile of v3, /device:TPU:8, one launch (start us, length us, event | category | flops | bytes accessed | tf_op | source)
XLA Modules:
  0.0 124.2 jit_solution(3811549467775147077)
XLA Ops:
  0.6 1.6 %shard_map.122 = f32[64,2,128]{2,1,0:T(2,128)} custom-call(s32[2,8]{1,0:T(2,128)} %bitcast.19, s32[8]{0:T(128)} %intervals_in.1, s32[2,8]{1,0:T(2,128)} %bitcast.20, f32[8,2,4,1024]{3,2,1,0:T(4,128)} %terms_in.1), custom_call_target="tpu_custom_call" | custom-call | tf_op jit(solution)/shard_map/pallas_call | solution.py:459
  2.2 16.6 %all-to-all-start = ((f32[64,2,128]{2,1,0:T(2,128)}), f32[64,2,128]{2,1,0:T(2,128)S(1)}, u32[]{:S(2)}, u32[]{:S(2)}) async-start(f32[64,2,128]{2,1,0:T(2,128)} %shard_map.122), calls=%async_computation | async-start | bytes 131072 | tf_op jit(solution)/shard_map/all_to_all | solution.py:427
  18.9 0.1 pad_add_fusion.place_ref
  18.9 11.3 %all-to-all-done.got_ref = f32[64,2,128]{2,1,0:T(2,128)S(1)} async-done(((f32[64,2,128]{2,1,0:T(2,128)}), f32[64,2,128]{2,1,0:T(2,128)S(1)}, u32[]{:S(2)}, u32[]{:S(2)}) %all-to-all-start) | async-done | bytes 65568 | tf_op jit(solution)/shard_map/all_to_all | solution.py:427
  30.2 0.7 shard_map.123
  31.0 4.3 %all-to-all-start.1 = ((f32[8,64,128]{2,1,0:T(8,128)}), f32[8,64,128]{2,1,0:T(8,128)S(1)}, u32[]{:S(2)}, u32[]{:S(2)}) async-start(f32[8,64,128]{2,1,0:T(8,128)} %shard_map.123), calls=%async_computation.1 | async-start | bytes 524288 | tf_op jit(solution)/shard_map/all_to_all | solution.py:427
  35.3 0.1 slice.23.wanted_ref
  35.4 0.1 fusion.1
  35.5 0.1 broadcast_in_dim_reshape.16.first_ref
  35.6 0.1 broadcast_in_dim_reshape.17.second_ref
  35.7 0.6 copy-done.2
  36.3 2.1 %shard_map.124.patch_ref = bf16[64,16,128]{2,1,0:T(8,128)(2,1)S(1)} custom-call(s32[2]{0:T(128)S(1)} %pad_add_fusion.place_ref, s32[64,16]{1,0:T(8,128)S(1)} %slice.23.wanted_ref, bf16[8,256,128]{2,1,0:T(8,128)(2,1)S(1)} %copy-done.2), custom_call_target="tpu_custom_call" | custom-call | tf_op jit(solution)/shard_map/pallas_call | solution.py:408
  38.4 4.4 %all-to-all-done.1 = f32[8,64,128]{2,1,0:T(8,128)S(1)} async-done(((f32[8,64,128]{2,1,0:T(8,128)}), f32[8,64,128]{2,1,0:T(8,128)S(1)}, u32[]{:S(2)}, u32[]{:S(2)}) %all-to-all-start.1) | async-done | bytes 262176 | tf_op jit(solution)/shard_map/all_to_all | solution.py:427
  42.8 1.4 %shard_map.125 = bf16[64,32,128]{2,1,0:T(8,128)(2,1)} custom-call(f32[512,128]{1,0:T(8,128)S(1)} %bitcast.15, s32[512,1]{1,0:T(8,128)S(1)} %broadcast_in_dim_reshape.16.first_ref, s32[512,1]{1,0:T(8,128)S(1)} %broadcast_in_dim_reshape.17.second_ref, bf16[64,16,128]{2,1,0:T(8,128)(2,1)S(1)} %shard_map.124.patch_ref), custom_call_target="tpu_custom_call" | custom-call | tf_op jit(solution)/shard_map/pallas_call | solution.py:485
  44.2 5.5 %all-to-all-start.2 = ((bf16[64,32,128]{2,1,0:T(8,128)(2,1)}), bf16[64,32,128]{2,1,0:T(8,128)(2,1)S(1)}, u32[]{:S(2)}, u32[]{:S(2)}) async-start(bf16[64,32,128]{2,1,0:T(8,128)(2,1)} %shard_map.125), calls=%async_computation.2 | async-start | bytes 1048576 | tf_op jit(solution)/shard_map/all_to_all | solution.py:427
  49.7 0.0 copy-start.5
  49.8 0.0 copy-start.6
  49.8 1.5 %shard_map.126 = (bf16[8,128,512]{2,1,0:T(8,128)(2,1)S(1)}, f32[8,64,512]{2,1,0:T(8,128)S(1)}) custom-call(f32[8,2,512]{2,1,0:T(2,128)S(1)} %copy-done.4), custom_call_target="tpu_custom_call" | custom-call | tf_op jit(solution)/shard_map/pallas_call | solution.py:481
  51.2 1.0 copy-done
  52.2 1.0 copy-done.1
  53.2 0.2 convert_reduce_fusion
  53.4 15.7 %all-to-all-done.2.got_ref = bf16[64,32,128]{2,1,0:T(8,128)(2,1)S(1)} async-done(((bf16[64,32,128]{2,1,0:T(8,128)(2,1)}), bf16[64,32,128]{2,1,0:T(8,128)(2,1)S(1)}, u32[]{:S(2)}, u32[]{:S(2)}) %all-to-all-start.2) | async-done | bytes 524320 | tf_op jit(solution)/shard_map/all_to_all | solution.py:427
  69.1 0.0 copy-done.3
  69.1 5.9 %shard_map.127 = (f32[8,8,512]{2,1,0:T(8,128)}, f32[512,128]{1,0:T(8,128)}) custom-call(s32[8]{0:T(128)S(1)} %multiply_add_fusion.slot_ref, bf16[64,32,128]{2,1,0:T(8,128)(2,1)S(1)} %all-to-all-done.2.got_ref, bf16[8,128,512]{2,1,0:T(8,128)(2,1)} %copy-done, f32[8,64,512]{2,1,0:T(8,128)} %copy-done.1, f32[8,8,512]{2,1,0:T(8,128)} %seen_in.1, ...), custom_call_target="tpu_custom_call" | custom-call | tf_op jit(solution)/shard_map/pallas_call | solution.py:432
  75.0 5.4 %all-to-all-start.3 = ((f32[64,8,128]{2,1,0:T(8,128)}), f32[64,8,128]{2,1,0:T(8,128)S(1)}, u32[]{:S(2)}, u32[]{:S(2)}) async-start(f32[64,8,128]{2,1,0:T(8,128)} %bitcast.7), calls=%async_computation.3 | async-start | bytes 524288 | tf_op jit(solution)/shard_map/all_to_all | solution.py:427
  80.4 0.1 broadcast_in_dim_reshape.15.second_row_ref
  80.5 0.1 broadcast_in_dim_reshape.14.first_row_ref
  80.6 13.3 %all-to-all-done.3 = f32[64,8,128]{2,1,0:T(8,128)S(1)} async-done(((f32[64,8,128]{2,1,0:T(8,128)}), f32[64,8,128]{2,1,0:T(8,128)S(1)}, u32[]{:S(2)}, u32[]{:S(2)}) %all-to-all-start.3) | async-done | bytes 262176 | tf_op jit(solution)/shard_map/all_to_all | solution.py:427
  93.9 0.6 shard_map.128
  94.5 9.9 %all_to_all.30.parts_ref = f32[8,64,128]{2,1,0:T(8,128)S(1)} all-to-all(f32[8,64,128]{2,1,0:T(8,128)S(1)} %bitcast.17), channel_id=1, replica_groups=mesh['z'=8,'x'=4,'core'=2,'tile'=8] {'x','core'}, dimensions={0} | all-to-all | bytes 524288 | tf_op jit(solution)/shard_map/all_to_all | solution.py:427
  104.5 18.7 %all_to_all.31.parts_ref = f32[64,8,128]{2,1,0:T(8,128)S(1)} all-to-all(f32[64,8,128]{2,1,0:T(8,128)S(1)} %shard_map.129), channel_id=1, replica_groups=mesh['z'=8,'x'=4,'core'=2,'tile'=8] {'z','tile'}, dimensions={0} | all-to-all | bytes 524288 | tf_op jit(solution)/shard_map/all_to_all | solution.py:427
  123.2 1.0 shard_map.130
  (15 shorter events, 0.1 us)
Async XLA Ops:
  2.2 28.0 %all-to-all-start = ((f32[64,2,128]{2,1,0:T(2,128)}), f32[64,2,128]{2,1,0:T(2,128)S(1)}, u32[]{:S(2)}, u32[]{:S(2)}) async-start(f32[64,2,128]{2,1,0:T(2,128)} %shard_map.122), calls=%async_computation | async-start | bytes 131072 | tf_op jit(solution)/shard_map/all_to_all | solution.py:427
  31.0 11.8 %all-to-all-start.1 = ((f32[8,64,128]{2,1,0:T(8,128)}), f32[8,64,128]{2,1,0:T(8,128)S(1)}, u32[]{:S(2)}, u32[]{:S(2)}) async-start(f32[8,64,128]{2,1,0:T(8,128)} %shard_map.123), calls=%async_computation.1 | async-start | bytes 524288 | tf_op jit(solution)/shard_map/all_to_all | solution.py:427
  35.3 1.0 copy-start.2
  44.2 5.5 %copy-start.4 = (f32[8,2,512]{2,1,0:T(2,128)S(1)}, f32[8,2,512]{2,1,0:T(2,128)}, u32[]{:S(2)}) copy-start(f32[8,2,512]{2,1,0:T(2,128)} %uv_ref.1) | copy-start | bytes 98308
  44.2 9.0 %copy-start.7 = (s32[8,2]{0,1:T(2,128)S(1)}, s32[8,2]{0,1:T(2,128)}, u32[]{:S(2)}) copy-start(s32[8,2]{0,1:T(2,128)} %param.15) | copy-start | bytes 196
  44.2 24.9 %copy-start.3 = (bf16[384,256]{1,0:T(8,128)(2,1)S(1)}, bf16[384,256]{1,0:T(8,128)(2,1)}, u32[]{:S(2)}) copy-start(bf16[384,256]{1,0:T(8,128)(2,1)} %constant.21.clone.cols_ref) | copy-start | bytes 589828
  44.2 24.9 %all-to-all-start.2 = ((bf16[64,32,128]{2,1,0:T(8,128)(2,1)}), bf16[64,32,128]{2,1,0:T(8,128)(2,1)S(1)}, u32[]{:S(2)}, u32[]{:S(2)}) async-start(bf16[64,32,128]{2,1,0:T(8,128)(2,1)} %shard_map.125), calls=%async_computation.2 | async-start | bytes 1048576 | tf_op jit(solution)/shard_map/all_to_all | solution.py:427
  49.7 19.4 %copy-start.5 = (f32[32,128]{1,0:T(8,128)S(1)}, f32[32,128]{1,0:T(8,128)}, u32[]{:S(2)}) copy-start(f32[32,128]{1,0:T(8,128)} %constant.22.clone.taper_ref) | copy-start | bytes 49156
  49.8 19.4 %copy-start.6 = (bf16[64,96]{1,0:T(8,128)(2,1)S(1)}, bf16[64,96]{1,0:T(8,128)(2,1)}, u32[]{:S(2)}) copy-start(bf16[64,96]{1,0:T(8,128)(2,1)} %constant.20.clone.rows_ref) | copy-start | bytes 36868
  51.2 1.0 copy-start
  52.2 1.0 copy-start.1
  75.0 18.8 %all-to-all-start.3 = ((f32[64,8,128]{2,1,0:T(8,128)}), f32[64,8,128]{2,1,0:T(8,128)S(1)}, u32[]{:S(2)}, u32[]{:S(2)}) async-start(f32[64,8,128]{2,1,0:T(8,128)} %bitcast.7), calls=%async_computation.3 | async-start | bytes 524288 | tf_op jit(solution)/shard_map/all_to_all | solution.py:427

commit v4 on v3

--- a/solution.py
+++ b/solution.py
@@ -228,7 +228,8 @@
         out_ref[i] = total[part * SUBS : (part + 1) * SUBS, :]
 
 
-def place_kernel(parts_ref, out_ref):
+def place_kernel(parts_ref, out_hbm, out_ref, sems):
+    copies = []
     lane = lax.broadcasted_iota(S32, (SUBS, LANES), 1) // SIDE
     for block in range(8):
         for half in range(2):
@@ -241,16 +242,23 @@
                     for i in range(1, 4):
                         total = jnp.where(lane == i, turned[i][(i - at) % 4], total)
                     out_ref[:, interval, 2 * half + part, block * LANES : (block + 1) * LANES] = total
+        lanes = pl.ds(block * LANES, LANES)
+        copies.append(
+            pltpu.make_async_copy(out_ref.at[:, :, :, lanes], out_hbm.at[:, :, :, lanes], sems.at[block])
+        )
+        copies[-1].start()
+    for copy in copies:
+        copy.wait()
 
 
 def main_kernel(
-    slot_ref, got_ref, row_wave_in, column_wave_in, seen_in, flag_in, rows_ref, cols_ref, taper_ref,
-    res_ref, grad_ref, beam_ref, row_wave_ref, column_wave_ref, seen_ref, flag_ref, side_ref, z_ref, dz_ref, held_ref, sems,
+    slot_ref, got_ref, row_wave_ref, column_wave_ref, seen_in, flag_in, rows_ref, cols_ref, taper_ref,
+    res_ref, grad_ref, beam_ref, seen_ref, flag_ref, side_ref, z_ref, dz_ref, held_ref, sems,
 ):
     copies = [
         pltpu.make_async_copy(a, b, sems.at[i])
         for i, (a, b) in enumerate(
-            ((row_wave_in, row_wave_ref), (column_wave_in, column_wave_ref), (seen_in, seen_ref), (flag_in, flag_ref))
+            ((seen_in, seen_ref), (flag_in, flag_ref))
         )
     ]
     for copy in copies:
@@ -427,17 +435,16 @@
     return lax.all_to_all(x, axes, split_axis=0, concat_axis=0, tiled=True)
 
 
-def main(slot, got, *rest):
+def main(slot, got, row_waves, column_waves, *rest):
+    waves = [pltpu.with_memory_space_constraint(x, pltpu.VMEM) for x in (row_waves, column_waves)]
     tables = [jnp.asarray(t) for t in dft_tables()]
     return call(
         main_kernel,
         (shape((SUBS, 8, VIS)), shape((TABLE, LANES))),
-        [SMEM, VMEM] + [HBM] * 4 + [VMEM] * 3,
+        [SMEM] + [VMEM] * 3 + [HBM] * 2 + [VMEM] * 3,
         (VMEM, VMEM),
         [
             pltpu.VMEM((TABLE, LANES), F32),
-            pltpu.VMEM((SUBS, 4 * SIDE, VIS), BF16),
-            pltpu.VMEM((SUBS, 2 * SIDE, VIS), F32),
             pltpu.VMEM((SUBS, 8, VIS), F32),
             pltpu.VMEM((SUBS, VIS), S32),
             pltpu.VMEM((SUBS, 6, SIDE, LANES), F32),
@@ -446,7 +453,7 @@
             pltpu.VMEM((SUBS, 2, 2 * LANES, VIS), BF16),
             pltpu.SemaphoreType.DMA((4,)),
         ],
-    )(slot, got, *(in_hbm(x) for x in rest), *tables)
+    )(slot, got, *waves, *(in_hbm(x) for x in rest), *tables)
 
 
 ACROSS = ("z", "tile")
@@ -498,7 +505,13 @@
     back_b = exchange(dense.reshape(GROUPS, ROWS, LANES), NEAR)
     summed = call(add_kernel, shape((PEERS, SUBS, LANES)), [VMEM], VMEM)(back_b)
     back_a = exchange(summed, ACROSS)
-    total = call(place_kernel, shape((SUBS, 2, 4, SIDE * SIDE)), [VMEM], VMEM)(back_a)
+    total = call(
+        place_kernel,
+        shape((SUBS, 2, 4, SIDE * SIDE)),
+        [VMEM],
+        HBM,
+        [pltpu.VMEM((SUBS, 2, 4, SIDE * SIDE), F32), pltpu.SemaphoreType.DMA((8,))],
+    )(back_a)
     return (result, total)
 
 

time: 125 us -> 124 us (level)
  local copies, waits for them, and re-layouts: 3.16 us -> 1.2 us
  waiting for transfers between devices: 44.7 us -> 46.6 us
    all_to_all x4, waiting for transfers between devices: 44.7 us -> 46.6 us  [exchange(): return lax.all_to_all(x, axes, split_axis=0, concat_axis=0, tiled=True)]
    unnamed x16 -> x12, local copies, waits for them, and re-layouts: 2.54 us -> 0.59 us
where the time goes in v4:
time: 124 us; the launch traced here: 123 us
  waiting for transfers between devices  46.6 us (38%)
  starting transfers between devices  31.8 us (26%)
  blocking collectives  28.6 us (23%)
  Pallas kernels  14.2 us (11%)
    all_to_all x4, waiting for transfers between devices, exchange(): return lax.all_to_all(x, axes, split_axis=0, concat_axis=0, tiled=True)  46.6 us
    all_to_all x4, starting transfers between devices, exchange(): return lax.all_to_all(x, axes, split_axis=0, concat_axis=0, tiled=True)  31.8 us
    all_to_all x2, blocking collectives, exchange(): return lax.all_to_all(x, axes, split_axis=0, concat_axis=0, tiled=True)  28.6 us
    pallas_call x1, Pallas kernels, main(): call(main_kernel, (shape((SUBS, 8, VIS)), shape((TABLE, LANES))), [SMEM]...  5.21 us
  transfers between devices with their start and end apart: 4, of which 4 were waited for; matrix products, arithmetic and copies ran while one was open for 1% of the time, Pallas kernels for 3%

profile of v4, /device:TPU:8, one launch (start us, length us, event | category | flops | bytes accessed | tf_op | source)
XLA Modules:
  0.0 123.4 jit_solution(8734102906943904864)
XLA Ops:
  0.6 1.6 %shard_map.122 = f32[64,2,128]{2,1,0:T(2,128)} custom-call(s32[2,8]{1,0:T(2,128)} %bitcast.19, s32[8]{0:T(128)} %intervals_in.1, s32[2,8]{1,0:T(2,128)} %bitcast.20, f32[8,2,4,1024]{3,2,1,0:T(4,128)} %terms_in.1), custom_call_target="tpu_custom_call" | custom-call | tf_op jit(solution)/shard_map/pallas_call | solution.py:466
  2.2 16.6 %all-to-all-start = ((f32[64,2,128]{2,1,0:T(2,128)}), f32[64,2,128]{2,1,0:T(2,128)S(1)}, u32[]{:S(2)}, u32[]{:S(2)}) async-start(f32[64,2,128]{2,1,0:T(2,128)} %shard_map.122), calls=%async_computation | async-start | bytes 131072 | tf_op jit(solution)/shard_map/all_to_all | solution.py:435
  18.9 0.1 pad_add_fusion.place_ref
  18.9 11.3 %all-to-all-done.got_ref = f32[64,2,128]{2,1,0:T(2,128)S(1)} async-done(((f32[64,2,128]{2,1,0:T(2,128)}), f32[64,2,128]{2,1,0:T(2,128)S(1)}, u32[]{:S(2)}, u32[]{:S(2)}) %all-to-all-start) | async-done | bytes 65568 | tf_op jit(solution)/shard_map/all_to_all | solution.py:435
  30.2 0.7 shard_map.123
  31.0 4.3 %all-to-all-start.1 = ((f32[8,64,128]{2,1,0:T(8,128)}), f32[8,64,128]{2,1,0:T(8,128)S(1)}, u32[]{:S(2)}, u32[]{:S(2)}) async-start(f32[8,64,128]{2,1,0:T(8,128)} %shard_map.123), calls=%async_computation.1 | async-start | bytes 524288 | tf_op jit(solution)/shard_map/all_to_all | solution.py:435
  35.3 0.1 slice.23.wanted_ref
  35.4 0.1 fusion.1
  35.5 0.1 broadcast_in_dim_reshape.16.first_ref
  35.6 0.1 broadcast_in_dim_reshape.17.second_ref
  35.7 0.6 copy-done
  36.3 2.1 %shard_map.124.patch_ref = bf16[64,16,128]{2,1,0:T(8,128)(2,1)S(1)} custom-call(s32[2]{0:T(128)S(1)} %pad_add_fusion.place_ref, s32[64,16]{1,0:T(8,128)S(1)} %slice.23.wanted_ref, bf16[8,256,128]{2,1,0:T(8,128)(2,1)S(1)} %copy-done), custom_call_target="tpu_custom_call" | custom-call | tf_op jit(solution)/shard_map/pallas_call | solution.py:416
  38.4 4.4 %all-to-all-done.1 = f32[8,64,128]{2,1,0:T(8,128)S(1)} async-done(((f32[8,64,128]{2,1,0:T(8,128)}), f32[8,64,128]{2,1,0:T(8,128)S(1)}, u32[]{:S(2)}, u32[]{:S(2)}) %all-to-all-start.1) | async-done | bytes 262176 | tf_op jit(solution)/shard_map/all_to_all | solution.py:435
  42.8 1.4 %shard_map.125 = bf16[64,32,128]{2,1,0:T(8,128)(2,1)} custom-call(f32[512,128]{1,0:T(8,128)S(1)} %bitcast.15, s32[512,1]{1,0:T(8,128)S(1)} %broadcast_in_dim_reshape.16.first_ref, s32[512,1]{1,0:T(8,128)S(1)} %broadcast_in_dim_reshape.17.second_ref, bf16[64,16,128]{2,1,0:T(8,128)(2,1)S(1)} %shard_map.124.patch_ref), custom_call_target="tpu_custom_call" | custom-call | tf_op jit(solution)/shard_map/pallas_call | solution.py:492
  44.2 5.5 %all-to-all-start.2 = ((bf16[64,32,128]{2,1,0:T(8,128)(2,1)}), bf16[64,32,128]{2,1,0:T(8,128)(2,1)S(1)}, u32[]{:S(2)}, u32[]{:S(2)}) async-start(bf16[64,32,128]{2,1,0:T(8,128)(2,1)} %shard_map.125), calls=%async_computation.2 | async-start | bytes 1048576 | tf_op jit(solution)/shard_map/all_to_all | solution.py:435
  49.7 0.0 copy-done.2
  49.7 0.0 copy-start.3
  49.7 0.0 copy-start.4
  49.7 1.5 %shard_map.126 = (bf16[8,128,512]{2,1,0:T(8,128)(2,1)S(1)}, f32[8,64,512]{2,1,0:T(8,128)S(1)}) custom-call(f32[8,2,512]{2,1,0:T(2,128)S(1)} %copy-done.2), custom_call_target="tpu_custom_call" | custom-call | tf_op jit(solution)/shard_map/pallas_call | solution.py:488
  51.2 0.0 copy-done.5
  51.2 0.2 convert_reduce_fusion
  51.4 17.7 %all-to-all-done.2.got_ref = bf16[64,32,128]{2,1,0:T(8,128)(2,1)S(1)} async-done(((bf16[64,32,128]{2,1,0:T(8,128)(2,1)}), bf16[64,32,128]{2,1,0:T(8,128)(2,1)S(1)}, u32[]{:S(2)}, u32[]{:S(2)}) %all-to-all-start.2) | async-done | bytes 524320 | tf_op jit(solution)/shard_map/all_to_all | solution.py:435
  69.1 0.0 copy-done.1
  69.1 5.2 %shard_map.127 = (f32[8,8,512]{2,1,0:T(8,128)}, f32[512,128]{1,0:T(8,128)}) custom-call(s32[8]{0:T(128)S(1)} %multiply_add_fusion.slot_ref, bf16[64,32,128]{2,1,0:T(8,128)(2,1)S(1)} %all-to-all-done.2.got_ref, bf16[8,128,512]{2,1,0:T(8,128)(2,1)S(1)} %get-tuple-element.6.row_wave_ref, f32[8,64,512]{2,1,0:T(8,128)S(1)} %get-tuple-element.7.column_wave_ref, ...), custom_call_target="tpu_custom_call" | custom-call | tf_op jit(solution)/shard_map/pallas_call | solution.py:441
  74.3 5.4 %all-to-all-start.3 = ((f32[64,8,128]{2,1,0:T(8,128)}), f32[64,8,128]{2,1,0:T(8,128)S(1)}, u32[]{:S(2)}, u32[]{:S(2)}) async-start(f32[64,8,128]{2,1,0:T(8,128)} %bitcast.7), calls=%async_computation.3 | async-start | bytes 524288 | tf_op jit(solution)/shard_map/all_to_all | solution.py:435
  79.7 0.1 broadcast_in_dim_reshape.15.second_row_ref
  79.8 0.1 broadcast_in_dim_reshape.14.first_row_ref
  79.9 13.3 %all-to-all-done.3 = f32[64,8,128]{2,1,0:T(8,128)S(1)} async-done(((f32[64,8,128]{2,1,0:T(8,128)}), f32[64,8,128]{2,1,0:T(8,128)S(1)}, u32[]{:S(2)}, u32[]{:S(2)}) %all-to-all-start.3) | async-done | bytes 262176 | tf_op jit(solution)/shard_map/all_to_all | solution.py:435
  93.2 0.6 shard_map.128
  93.8 9.9 %all_to_all.30.parts_ref = f32[8,64,128]{2,1,0:T(8,128)S(1)} all-to-all(f32[8,64,128]{2,1,0:T(8,128)S(1)} %bitcast.17), channel_id=1, replica_groups=mesh['z'=8,'x'=4,'core'=2,'tile'=8] {'x','core'}, dimensions={0} | all-to-all | bytes 524288 | tf_op jit(solution)/shard_map/all_to_all | solution.py:435
  103.8 18.7 %all_to_all.31.parts_ref = f32[64,8,128]{2,1,0:T(8,128)S(1)} all-to-all(f32[64,8,128]{2,1,0:T(8,128)S(1)} %shard_map.129), channel_id=1, replica_groups=mesh['z'=8,'x'=4,'core'=2,'tile'=8] {'z','tile'}, dimensions={0} | all-to-all | bytes 524288 | tf_op jit(solution)/shard_map/all_to_all | solution.py:435
  122.5 1.0 shard_map.130
  (11 shorter events, 0.1 us)
Async XLA Ops:
  2.2 28.0 %all-to-all-start = ((f32[64,2,128]{2,1,0:T(2,128)}), f32[64,2,128]{2,1,0:T(2,128)S(1)}, u32[]{:S(2)}, u32[]{:S(2)}) async-start(f32[64,2,128]{2,1,0:T(2,128)} %shard_map.122), calls=%async_computation | async-start | bytes 131072 | tf_op jit(solution)/shard_map/all_to_all | solution.py:435
  31.0 11.8 %all-to-all-start.1 = ((f32[8,64,128]{2,1,0:T(8,128)}), f32[8,64,128]{2,1,0:T(8,128)S(1)}, u32[]{:S(2)}, u32[]{:S(2)}) async-start(f32[8,64,128]{2,1,0:T(8,128)} %shard_map.123), calls=%async_computation.1 | async-start | bytes 524288 | tf_op jit(solution)/shard_map/all_to_all | solution.py:435
  35.3 1.0 copy-start
  44.2 5.5 %copy-start.2 = (f32[8,2,512]{2,1,0:T(2,128)S(1)}, f32[8,2,512]{2,1,0:T(2,128)}, u32[]{:S(2)}) copy-start(f32[8,2,512]{2,1,0:T(2,128)} %uv_ref.1) | copy-start | bytes 98308
  44.2 7.0 %copy-start.5 = (s32[8,2]{0,1:T(2,128)S(1)}, s32[8,2]{0,1:T(2,128)}, u32[]{:S(2)}) copy-start(s32[8,2]{0,1:T(2,128)} %param.15) | copy-start | bytes 196
  44.2 24.9 %copy-start.1 = (bf16[384,256]{1,0:T(8,128)(2,1)S(1)}, bf16[384,256]{1,0:T(8,128)(2,1)}, u32[]{:S(2)}) copy-start(bf16[384,256]{1,0:T(8,128)(2,1)} %constant.21.clone.cols_ref) | copy-start | bytes 589828
  44.2 24.9 %all-to-all-start.2 = ((bf16[64,32,128]{2,1,0:T(8,128)(2,1)}), bf16[64,32,128]{2,1,0:T(8,128)(2,1)S(1)}, u32[]{:S(2)}, u32[]{:S(2)}) async-start(bf16[64,32,128]{2,1,0:T(8,128)(2,1)} %shard_map.125), calls=%async_computation.2 | async-start | bytes 1048576 | tf_op jit(solution)/shard_map/all_to_all | solution.py:435
  49.7 19.4 %copy-start.3 = (f32[32,128]{1,0:T(8,128)S(1)}, f32[32,128]{1,0:T(8,128)}, u32[]{:S(2)}) copy-start(f32[32,128]{1,0:T(8,128)} %constant.22.clone.taper_ref) | copy-start | bytes 49156
  49.7 19.4 %copy-start.4 = (bf16[64,96]{1,0:T(8,128)(2,1)S(1)}, bf16[64,96]{1,0:T(8,128)(2,1)}, u32[]{:S(2)}) copy-start(bf16[64,96]{1,0:T(8,128)(2,1)} %constant.20.clone.rows_ref) | copy-start | bytes 36868
  74.3 18.8 %all-to-all-start.3 = ((f32[64,8,128]{2,1,0:T(8,128)}), f32[64,8,128]{2,1,0:T(8,128)S(1)}, u32[]{:S(2)}, u32[]{:S(2)}) async-start(f32[64,8,128]{2,1,0:T(8,128)} %bitcast.7), calls=%async_computation.3 | async-start | bytes 524288 | tf_op jit(solution)/shard_map/all_to_all | solution.py:435

commit v5 on v4

--- a/solution.py
+++ b/solution.py
@@ -106,7 +106,7 @@
     ]
     for copy in copies:
         copy.start()
-    for copy in copies[:3]:
+    for copy in copies:
         copy.wait()
     spot = lax.broadcasted_iota(S32, (1, LANES), 1)
     asked = jnp.zeros((1, LANES), S32)
@@ -119,7 +119,6 @@
         code = (offsets_ref[0, k] & 255) * LANES + offsets_ref[1, k]
         asked = jnp.where(spot == ENDS + 2 * tiles[k] + seconds[k], code, asked)
     out_ref[:, 1:2, :] = jnp.broadcast_to(asked.astype(F32).reshape(1, 1, LANES), (PEERS, 1, LANES))
-    copies[3].wait()
     lane = spot // SIDE
     for block in range(8):
         turned = []
@@ -150,7 +149,7 @@
     lax.fori_loop(0, SUBS, one, 0)
 
 
-def cut_kernel(place_ref, wanted_ref, strip_ref, out_ref, wide_ref):
+def cut_kernel(place_ref, wanted_ref, strip_ref, out_hbm, wide_ref, out_ref, sem):
     wide_ref[...] = strip_ref[0].astype(F32)
     tile = place_ref[0]
     part_of = place_ref[1]
@@ -172,15 +171,21 @@
         return carry
 
     lax.fori_loop(0, PEERS, one, 0, unroll=8)
-
-
-def spread_kernel(got_ref, out_ref):
-    part = got_ref[:, 0:1, :].reshape(ROWS, LANES)
-    for i in range(GROUPS):
-        out_ref[i] = part
-
-
-def gather_kernel(table_ref, first_ref, second_ref, patch_ref, out_ref):
+    copy = pltpu.make_async_copy(out_ref, out_hbm.at[:, pl.ds(ENDS, ENDS), :], sem)
+    copy.start()
+    copy.wait()
+
+
+def spread_kernel(got_ref, out_hbm, part_ref, sems):
+    part_ref[...] = got_ref[:, 0:1, :].reshape(ROWS, LANES)
+    copies = [pltpu.make_async_copy(part_ref, out_hbm.at[i], sems.at[i]) for i in range(GROUPS)]
+    for copy in copies:
+        copy.start()
+    for copy in copies:
+        copy.wait()
+
+
+def gather_kernel(table_ref, first_ref, second_ref, patched_hbm, out_hbm, out_ref, sem):
     hi, lo = split(table_ref[...])
     table = jnp.concatenate([hi, lo], axis=1)
     ids = lax.broadcasted_iota(S32, (TABLE, TABLE), 1)
@@ -197,8 +202,10 @@
     beams = jnp.where(left, first, second)
     hi = beams.astype(BF16).astype(F32)
     both = jnp.concatenate([hi.reshape(PEERS, SUBS, LANES), (beams - hi).reshape(PEERS, SUBS, LANES)], axis=1)
-    out_ref[:, 0:ENDS, :] = both.astype(BF16)
-    out_ref[:, ENDS : 2 * ENDS, :] = patch_ref[...]
+    out_ref[...] = both.astype(BF16)
+    copy = pltpu.make_async_copy(out_ref, out_hbm.at[:, pl.ds(0, ENDS), :], sem)
+    copy.start()
+    copy.wait()
 
 
 def scatter_kernel(got_ref, first_ref, second_ref, first_row_ref, second_row_ref, out_ref):
@@ -363,10 +370,11 @@
         dz_ref[k] = both[: 2 * SIDE] + both[2 * SIDE :] + dot(row_wave[: 2 * SIDE], t_lo, (1, 1))
         return carry
 
-    for k in range(SUBS):
-        one(k, 0)
-    for k in range(SUBS):
-        two(k, 0)
+    for k in range(SUBS + 1):
+        if k < SUBS:
+            one(k, 0)
+        if k > 0:
+            two(k - 1, 0)
 
     for k in range(SUBS):
         d = dz_ref[k]
@@ -397,13 +405,14 @@
 PARAMS = pltpu.CompilerParams(vmem_limit_bytes=40 * 1024 * 1024)
 
 
-def call(kernel, shapes, specs, out_specs, scratch=()):
+def call(kernel, shapes, specs, out_specs, scratch=(), aliases=None):
     return pl.pallas_call(
         kernel,
         out_shape=shapes,
         in_specs=specs,
         out_specs=out_specs,
         scratch_shapes=list(scratch),
+        input_output_aliases=aliases or {},
         compiler_params=PARAMS,
     )
 
@@ -415,13 +424,17 @@
 def cut(place, wanted, grid):
     return pl.pallas_call(
         cut_kernel,
-        out_shape=shape((PEERS, ENDS, LANES), BF16),
+        out_shape=shape((PEERS, 2 * ENDS, LANES), BF16),
         grid_spec=pltpu.PrefetchScalarGridSpec(
             num_scalar_prefetch=2,
             grid=(1,),
             in_specs=[pl.BlockSpec((1, grid.shape[1], LANES), lambda i, place, wanted: (place[1], 0, 0))],
-            out_specs=pl.BlockSpec((PEERS, ENDS, LANES), lambda i, place, wanted: (0, 0, 0)),
-            scratch_shapes=[pltpu.VMEM((grid.shape[1], LANES), F32)],
+            out_specs=HBM,
+            scratch_shapes=[
+                pltpu.VMEM((grid.shape[1], LANES), F32),
+                pltpu.VMEM((PEERS, ENDS, LANES), BF16),
+                pltpu.SemaphoreType.DMA,
+            ],
         ),
         compiler_params=PARAMS,
     )(place, wanted, grid)
@@ -477,7 +490,13 @@
         ],
     )(*(in_hbm(x) for x in (stations.T, intervals, offsets, a_terms)))
     got_a = exchange(sent, ACROSS)
-    spread = call(spread_kernel, shape((GROUPS, ROWS, LANES)), [VMEM], VMEM)(got_a)
+    spread = call(
+        spread_kernel,
+        shape((GROUPS, ROWS, LANES)),
+        [VMEM],
+        HBM,
+        [pltpu.VMEM((ROWS, LANES), F32), pltpu.SemaphoreType.DMA((GROUPS,))],
+    )(got_a)
     table = exchange(spread, NEAR).reshape(TABLE, LANES)
 
     wanted = got_a[:, 1, :].astype(S32)
@@ -489,7 +508,14 @@
         wave_kernel, (shape((SUBS, 4 * SIDE, VIS), BF16), shape((SUBS, 2 * SIDE, VIS))), [VMEM], (VMEM, VMEM)
     )(uv)
 
-    found = call(gather_kernel, shape((PEERS, 2 * ENDS, LANES), BF16), [VMEM] * 4, VMEM)(table, *columns, patches)
+    found = call(
+        gather_kernel,
+        shape((PEERS, 2 * ENDS, LANES), BF16),
+        [VMEM] * 3 + [HBM],
+        HBM,
+        [pltpu.VMEM((PEERS, ENDS, LANES), BF16), pltpu.SemaphoreType.DMA],
+        {3: 0},
+    )(table, *columns, patches)
     got_c = exchange(found, ACROSS)
 
     owner = offsets[0] >> 8

time: 124 us -> 124 us (level)
  no operation moved by 1% of the time
where the time goes in v5:
time: 124 us; the launch traced here: 123 us
  waiting for transfers between devices  45.9 us (37%)
  starting transfers between devices  31.8 us (26%)
  blocking collectives  28.6 us (23%)
  Pallas kernels  14.5 us (12%)
    all_to_all x4, waiting for transfers between devices, exchange(): return lax.all_to_all(x, axes, split_axis=0, concat_axis=0, tiled=True)  45.9 us
    all_to_all x4, starting transfers between devices, exchange(): return lax.all_to_all(x, axes, split_axis=0, concat_axis=0, tiled=True)  31.8 us
    all_to_all x2, blocking collectives, exchange(): return lax.all_to_all(x, axes, split_axis=0, concat_axis=0, tiled=True)  28.6 us
    pallas_call x1, Pallas kernels, main(): call(main_kernel, (shape((SUBS, 8, VIS)), shape((TABLE, LANES))), [SMEM]...  4.91 us
    pallas_call x1, Pallas kernels, cut(): pl.pallas_call(cut_kernel, out_shape=shape((PEERS, 2 * ENDS, LANES), BF16...  2.82 us
  transfers between devices with their start and end apart: 4, of which 4 were waited for; matrix products, arithmetic and copies ran while one was open for 1% of the time, Pallas kernels for 3%

profile of v5, /device:TPU:8, one launch (start us, length us, event | category | flops | bytes accessed | tf_op | source)
XLA Modules:
  0.0 123.1 jit_solution(12538768128656005483)
XLA Ops:
  0.6 1.6 %shard_map.122 = f32[64,2,128]{2,1,0:T(2,128)} custom-call(s32[2,8]{1,0:T(2,128)} %bitcast.19, s32[8]{0:T(128)} %intervals_in.1, s32[2,8]{1,0:T(2,128)} %bitcast.20, f32[8,2,4,1024]{3,2,1,0:T(4,128)} %terms_in.1), custom_call_target="tpu_custom_call" | custom-call | tf_op jit(solution)/shard_map/pallas_call | solution.py:479
  2.2 16.6 %all-to-all-start = ((f32[64,2,128]{2,1,0:T(2,128)}), f32[64,2,128]{2,1,0:T(2,128)S(1)}, u32[]{:S(2)}, u32[]{:S(2)}) async-start(f32[64,2,128]{2,1,0:T(2,128)} %shard_map.122), calls=%async_computation | async-start | bytes 131072 | tf_op jit(solution)/shard_map/all_to_all | solution.py:448
  18.8 0.1 pad_add_fusion.place_ref
  18.9 11.3 %all-to-all-done.got_ref = f32[64,2,128]{2,1,0:T(2,128)S(1)} async-done(((f32[64,2,128]{2,1,0:T(2,128)}), f32[64,2,128]{2,1,0:T(2,128)S(1)}, u32[]{:S(2)}, u32[]{:S(2)}) %all-to-all-start) | async-done | bytes 65568 | tf_op jit(solution)/shard_map/all_to_all | solution.py:448
  30.2 0.8 shard_map.123
  31.0 4.3 %all-to-all-start.1 = ((f32[8,64,128]{2,1,0:T(8,128)}), f32[8,64,128]{2,1,0:T(8,128)S(1)}, u32[]{:S(2)}, u32[]{:S(2)}) async-start(f32[8,64,128]{2,1,0:T(8,128)} %shard_map.123), calls=%async_computation.1 | async-start | bytes 524288 | tf_op jit(solution)/shard_map/all_to_all | solution.py:448
  35.4 0.1 slice.23.wanted_ref
  35.4 0.1 fusion.1
  35.5 0.1 broadcast_in_dim_reshape.16.first_ref
  35.6 0.1 broadcast_in_dim_reshape.17.second_ref
  35.8 0.6 copy-done
  36.3 2.8 %shard_map.124.patched_hbm = bf16[64,32,128]{2,1,0:T(8,128)(2,1)} custom-call(s32[2]{0:T(128)S(1)} %pad_add_fusion.place_ref, s32[64,16]{1,0:T(8,128)S(1)} %slice.23.wanted_ref, bf16[8,256,128]{2,1,0:T(8,128)(2,1)S(1)} %copy-done), custom_call_target="tpu_custom_call" | custom-call | tf_op jit(solution)/shard_map/pallas_call | solution.py:425
  39.2 3.7 %all-to-all-done.1 = f32[8,64,128]{2,1,0:T(8,128)S(1)} async-done(((f32[8,64,128]{2,1,0:T(8,128)}), f32[8,64,128]{2,1,0:T(8,128)S(1)}, u32[]{:S(2)}, u32[]{:S(2)}) %all-to-all-start.1) | async-done | bytes 262176 | tf_op jit(solution)/shard_map/all_to_all | solution.py:448
  42.8 1.3 %shard_map.125 = bf16[64,32,128]{2,1,0:T(8,128)(2,1)} custom-call(f32[512,128]{1,0:T(8,128)S(1)} %bitcast.15, s32[512,1]{1,0:T(8,128)S(1)} %broadcast_in_dim_reshape.16.first_ref, s32[512,1]{1,0:T(8,128)S(1)} %broadcast_in_dim_reshape.17.second_ref, bf16[64,32,128]{2,1,0:T(8,128)(2,1)} %shard_map.124.patched_hbm), custom_call_target="tpu_custom_call", output_to_operand_aliasing={{}: (3, {})} | custom-call | tf_op jit(solution)/shard_map/pallas_call | solution.py:511
  44.2 0.0 copy-start.2
  44.2 0.0 copy-start.5
  44.2 0.0 copy-start.1
  44.2 5.5 %all-to-all-start.2 = ((bf16[64,32,128]{2,1,0:T(8,128)(2,1)}), bf16[64,32,128]{2,1,0:T(8,128)(2,1)S(1)}, u32[]{:S(2)}, u32[]{:S(2)}) async-start(bf16[64,32,128]{2,1,0:T(8,128)(2,1)} %shard_map.125), calls=%async_computation.2 | async-start | bytes 1048576 | tf_op jit(solution)/shard_map/all_to_all | solution.py:448
  49.7 0.0 copy-start.3
  49.7 0.0 copy-start.4
  49.8 1.5 %shard_map.126 = (bf16[8,128,512]{2,1,0:T(8,128)(2,1)S(1)}, f32[8,64,512]{2,1,0:T(8,128)S(1)}) custom-call(f32[8,2,512]{2,1,0:T(2,128)S(1)} %copy-done.2), custom_call_target="tpu_custom_call" | custom-call | tf_op jit(solution)/shard_map/pallas_call | solution.py:507
  51.2 0.2 convert_reduce_fusion
  51.4 17.7 %all-to-all-done.2.got_ref = bf16[64,32,128]{2,1,0:T(8,128)(2,1)S(1)} async-done(((bf16[64,32,128]{2,1,0:T(8,128)(2,1)}), bf16[64,32,128]{2,1,0:T(8,128)(2,1)S(1)}, u32[]{:S(2)}, u32[]{:S(2)}) %all-to-all-start.2) | async-done | bytes 524320 | tf_op jit(solution)/shard_map/all_to_all | solution.py:448
  69.1 4.9 %shard_map.127 = (f32[8,8,512]{2,1,0:T(8,128)}, f32[512,128]{1,0:T(8,128)}) custom-call(s32[8]{0:T(128)S(1)} %multiply_add_fusion.slot_ref, bf16[64,32,128]{2,1,0:T(8,128)(2,1)S(1)} %all-to-all-done.2.got_ref, bf16[8,128,512]{2,1,0:T(8,128)(2,1)S(1)} %get-tuple-element.6.row_wave_ref, f32[8,64,512]{2,1,0:T(8,128)S(1)} %get-tuple-element.7.column_wave_ref, ...), custom_call_target="tpu_custom_call" | custom-call | tf_op jit(solution)/shard_map/pallas_call | solution.py:454
  74.0 5.4 %all-to-all-start.3 = ((f32[64,8,128]{2,1,0:T(8,128)}), f32[64,8,128]{2,1,0:T(8,128)S(1)}, u32[]{:S(2)}, u32[]{:S(2)}) async-start(f32[64,8,128]{2,1,0:T(8,128)} %bitcast.7), calls=%async_computation.3 | async-start | bytes 524288 | tf_op jit(solution)/shard_map/all_to_all | solution.py:448
  79.4 0.1 broadcast_in_dim_reshape.15.second_row_ref
  79.5 0.1 broadcast_in_dim_reshape.14.first_row_ref
  79.6 13.3 %all-to-all-done.3 = f32[64,8,128]{2,1,0:T(8,128)S(1)} async-done(((f32[64,8,128]{2,1,0:T(8,128)}), f32[64,8,128]{2,1,0:T(8,128)S(1)}, u32[]{:S(2)}, u32[]{:S(2)}) %all-to-all-start.3) | async-done | bytes 262176 | tf_op jit(solution)/shard_map/all_to_all | solution.py:448
  92.9 0.6 shard_map.128
  93.5 9.9 %all_to_all.30.parts_ref = f32[8,64,128]{2,1,0:T(8,128)S(1)} all-to-all(f32[8,64,128]{2,1,0:T(8,128)S(1)} %bitcast.17), channel_id=1, replica_groups=mesh['z'=8,'x'=4,'core'=2,'tile'=8] {'x','core'}, dimensions={0} | all-to-all | bytes 524288 | tf_op jit(solution)/shard_map/all_to_all | solution.py:448
  103.5 18.7 %all_to_all.31.parts_ref = f32[64,8,128]{2,1,0:T(8,128)S(1)} all-to-all(f32[64,8,128]{2,1,0:T(8,128)S(1)} %shard_map.129), channel_id=1, replica_groups=mesh['z'=8,'x'=4,'core'=2,'tile'=8] {'z','tile'}, dimensions={0} | all-to-all | bytes 524288 | tf_op jit(solution)/shard_map/all_to_all | solution.py:448
  122.2 1.0 shard_map.130
  (11 shorter events, 0.1 us)
Async XLA Ops:
  2.2 28.0 %all-to-all-start = ((f32[64,2,128]{2,1,0:T(2,128)}), f32[64,2,128]{2,1,0:T(2,128)S(1)}, u32[]{:S(2)}, u32[]{:S(2)}) async-start(f32[64,2,128]{2,1,0:T(2,128)} %shard_map.122), calls=%async_computation | async-start | bytes 131072 | tf_op jit(solution)/shard_map/all_to_all | solution.py:448
  31.0 11.9 %all-to-all-start.1 = ((f32[8,64,128]{2,1,0:T(8,128)}), f32[8,64,128]{2,1,0:T(8,128)S(1)}, u32[]{:S(2)}, u32[]{:S(2)}) async-start(f32[8,64,128]{2,1,0:T(8,128)} %shard_map.123), calls=%async_computation.1 | async-start | bytes 524288 | tf_op jit(solution)/shard_map/all_to_all | solution.py:448
  35.3 1.0 copy-start
  44.2 5.6 %copy-start.2 = (f32[8,2,512]{2,1,0:T(2,128)S(1)}, f32[8,2,512]{2,1,0:T(2,128)}, u32[]{:S(2)}) copy-start(f32[8,2,512]{2,1,0:T(2,128)} %uv_ref.1) | copy-start | bytes 98308
  44.2 7.0 %copy-start.5 = (s32[8,2]{0,1:T(2,128)S(1)}, s32[8,2]{0,1:T(2,128)}, u32[]{:S(2)}) copy-start(s32[8,2]{0,1:T(2,128)} %param.15) | copy-start | bytes 196
  44.2 24.9 %copy-start.1 = (bf16[384,256]{1,0:T(8,128)(2,1)S(1)}, bf16[384,256]{1,0:T(8,128)(2,1)}, u32[]{:S(2)}) copy-start(bf16[384,256]{1,0:T(8,128)(2,1)} %constant.21.clone.cols_ref) | copy-start | bytes 589828
  44.2 24.9 %all-to-all-start.2 = ((bf16[64,32,128]{2,1,0:T(8,128)(2,1)}), bf16[64,32,128]{2,1,0:T(8,128)(2,1)S(1)}, u32[]{:S(2)}, u32[]{:S(2)}) async-start(bf16[64,32,128]{2,1,0:T(8,128)(2,1)} %shard_map.125), calls=%async_computation.2 | async-start | bytes 1048576 | tf_op jit(solution)/shard_map/all_to_all | solution.py:448
  49.7 19.4 %copy-start.3 = (f32[32,128]{1,0:T(8,128)S(1)}, f32[32,128]{1,0:T(8,128)}, u32[]{:S(2)}) copy-start(f32[32,128]{1,0:T(8,128)} %constant.22.clone.taper_ref) | copy-start | bytes 49156
  49.7 19.4 %copy-start.4 = (bf16[64,96]{1,0:T(8,128)(2,1)S(1)}, bf16[64,96]{1,0:T(8,128)(2,1)}, u32[]{:S(2)}) copy-start(bf16[64,96]{1,0:T(8,128)(2,1)} %constant.20.clone.rows_ref) | copy-start | bytes 36868
  74.0 18.8 %all-to-all-start.3 = ((f32[64,8,128]{2,1,0:T(8,128)}), f32[64,8,128]{2,1,0:T(8,128)S(1)}, u32[]{:S(2)}, u32[]{:S(2)}) async-start(f32[64,8,128]{2,1,0:T(8,128)} %bitcast.7), calls=%async_computation.3 | async-start | bytes 524288 | tf_op jit(solution)/shard_map/all_to_all | solution.py:448

commit v6 on v5

--- a/solution.py
+++ b/solution.py
@@ -176,13 +176,10 @@
     copy.wait()
 
 
-def spread_kernel(got_ref, out_hbm, part_ref, sems):
-    part_ref[...] = got_ref[:, 0:1, :].reshape(ROWS, LANES)
-    copies = [pltpu.make_async_copy(part_ref, out_hbm.at[i], sems.at[i]) for i in range(GROUPS)]
-    for copy in copies:
-        copy.start()
-    for copy in copies:
-        copy.wait()
+def spread_kernel(got_ref, out_ref):
+    part = got_ref[:, 0:1, :].reshape(ROWS, LANES)
+    for i in range(GROUPS):
+        out_ref[i] = part
 
 
 def gather_kernel(table_ref, first_ref, second_ref, patched_hbm, out_hbm, out_ref, sem):
@@ -260,7 +257,7 @@
 
 def main_kernel(
     slot_ref, got_ref, row_wave_ref, column_wave_ref, seen_in, flag_in, rows_ref, cols_ref, taper_ref,
-    res_ref, grad_ref, beam_ref, seen_ref, flag_ref, side_ref, z_ref, dz_ref, held_ref, sems,
+    res_ref, out_ref, grad_ref, beam_ref, seen_ref, flag_ref, side_ref, z_ref, dz_ref, held_ref, sems,
 ):
     copies = [
         pltpu.make_async_copy(a, b, sems.at[i])
@@ -271,7 +268,7 @@
     for copy in copies:
         copy.start()
     got = got_ref[:, 0:ENDS, :].astype(F32)
-    beam_ref[...] = (got[:, :SUBS] + got[:, SUBS:]).reshape(TABLE, LANES)
+    beam_ref[0:TABLE, :] = (got[:, :SUBS] + got[:, SUBS:]).reshape(TABLE, LANES)
     narrow = lax.broadcasted_iota(S32, (SIDE // 2, LANES), 1) // SIDE
     lane = lax.broadcasted_iota(S32, (SIDE, LANES), 1) // SIDE
     taper = taper_ref[...]
@@ -397,6 +394,7 @@
         for half, (dp, dq) in enumerate(((dp_re, dq_re), (dp_im, dq_im))):
             grad = jnp.where(lane == 0, dp, jnp.where(lane == 1, turn(dp, 3), dq))
             grad_ref[pl.ds(k + SUBS * half, SIDE, stride=2 * SUBS), :] = grad
+    out_ref[...] = grad_ref[0:TABLE, :]
 
 
 SMEM = pl.BlockSpec(memory_space=pltpu.SMEM)
@@ -457,7 +455,8 @@
         [SMEM] + [VMEM] * 3 + [HBM] * 2 + [VMEM] * 3,
         (VMEM, VMEM),
         [
-            pltpu.VMEM((TABLE, LANES), F32),
+            pltpu.VMEM((TABLE + 2 * SUBS, LANES), F32),
+            pltpu.VMEM((TABLE + 2 * SUBS, LANES), F32),
             pltpu.VMEM((SUBS, 8, VIS), F32),
             pltpu.VMEM((SUBS, VIS), S32),
             pltpu.VMEM((SUBS, 6, SIDE, LANES), F32),
@@ -490,13 +489,7 @@
         ],
     )(*(in_hbm(x) for x in (stations.T, intervals, offsets, a_terms)))
     got_a = exchange(sent, ACROSS)
-    spread = call(
-        spread_kernel,
-        shape((GROUPS, ROWS, LANES)),
-        [VMEM],
-        HBM,
-        [pltpu.VMEM((ROWS, LANES), F32), pltpu.SemaphoreType.DMA((GROUPS,))],
-    )(got_a)
+    spread = call(spread_kernel, shape((GROUPS, ROWS, LANES)), [VMEM], VMEM)(got_a)
     table = exchange(spread, NEAR).reshape(TABLE, LANES)
 
     wanted = got_a[:, 1, :].astype(S32)

time: 124 us -> 124 us (level)
  no operation moved by 1% of the time
where the time goes in v6:
time: 124 us; the launch traced here: 123 us
  waiting for transfers between devices  45.9 us (37%)
  starting transfers between devices  31.8 us (26%)
  blocking collectives  28.6 us (23%)
  Pallas kernels  14.5 us (12%)
    all_to_all x4, waiting for transfers between devices, exchange(): return lax.all_to_all(x, axes, split_axis=0, concat_axis=0, tiled=True)  45.9 us
    all_to_all x4, starting transfers between devices, exchange(): return lax.all_to_all(x, axes, split_axis=0, concat_axis=0, tiled=True)  31.8 us
    all_to_all x2, blocking collectives, exchange(): return lax.all_to_all(x, axes, split_axis=0, concat_axis=0, tiled=True)  28.6 us
    pallas_call x1, Pallas kernels, main(): call(main_kernel, (shape((SUBS, 8, VIS)), shape((TABLE, LANES))), [SMEM]...  4.92 us
    pallas_call x1, Pallas kernels, cut(): pl.pallas_call(cut_kernel, out_shape=shape((PEERS, 2 * ENDS, LANES), BF16...  2.82 us
  transfers between devices with their start and end apart: 4, of which 4 were waited for; matrix products, arithmetic and copies ran while one was open for 1% of the time, Pallas kernels for 3%

profile of v6, /device:TPU:8, one launch (start us, length us, event | category | flops | bytes accessed | tf_op | source)
XLA Modules:
  0.0 123.1 jit_solution(16101528460534301431)
XLA Ops:
  0.6 1.6 %shard_map.122 = f32[64,2,128]{2,1,0:T(2,128)} custom-call(s32[2,8]{1,0:T(2,128)} %bitcast.19, s32[8]{0:T(128)} %intervals_in.1, s32[2,8]{1,0:T(2,128)} %bitcast.20, f32[8,2,4,1024]{3,2,1,0:T(4,128)} %terms_in.1), custom_call_target="tpu_custom_call" | custom-call | tf_op jit(solution)/shard_map/pallas_call | solution.py:478
  2.2 16.6 %all-to-all-start = ((f32[64,2,128]{2,1,0:T(2,128)}), f32[64,2,128]{2,1,0:T(2,128)S(1)}, u32[]{:S(2)}, u32[]{:S(2)}) async-start(f32[64,2,128]{2,1,0:T(2,128)} %shard_map.122), calls=%async_computation | async-start | bytes 131072 | tf_op jit(solution)/shard_map/all_to_all | solution.py:446
  18.8 0.1 pad_add_fusion.place_ref
  18.9 11.3 %all-to-all-done.got_ref = f32[64,2,128]{2,1,0:T(2,128)S(1)} async-done(((f32[64,2,128]{2,1,0:T(2,128)}), f32[64,2,128]{2,1,0:T(2,128)S(1)}, u32[]{:S(2)}, u32[]{:S(2)}) %all-to-all-start) | async-done | bytes 65568 | tf_op jit(solution)/shard_map/all_to_all | solution.py:446
  30.2 0.7 shard_map.123
  30.9 4.3 %all-to-all-start.1 = ((f32[8,64,128]{2,1,0:T(8,128)}), f32[8,64,128]{2,1,0:T(8,128)S(1)}, u32[]{:S(2)}, u32[]{:S(2)}) async-start(f32[8,64,128]{2,1,0:T(8,128)} %shard_map.123), calls=%async_computation.1 | async-start | bytes 524288 | tf_op jit(solution)/shard_map/all_to_all | solution.py:446
  35.3 0.1 slice.23.wanted_ref
  35.4 0.1 fusion.1
  35.4 0.1 broadcast_in_dim_reshape.16.first_ref
  35.6 0.1 broadcast_in_dim_reshape.17.second_ref
  35.7 0.6 copy-done
  36.3 2.8 %shard_map.124.patched_hbm = bf16[64,32,128]{2,1,0:T(8,128)(2,1)} custom-call(s32[2]{0:T(128)S(1)} %pad_add_fusion.place_ref, s32[64,16]{1,0:T(8,128)S(1)} %slice.23.wanted_ref, bf16[8,256,128]{2,1,0:T(8,128)(2,1)S(1)} %copy-done), custom_call_target="tpu_custom_call" | custom-call | tf_op jit(solution)/shard_map/pallas_call | solution.py:423
  39.1 3.7 %all-to-all-done.1 = f32[8,64,128]{2,1,0:T(8,128)S(1)} async-done(((f32[8,64,128]{2,1,0:T(8,128)}), f32[8,64,128]{2,1,0:T(8,128)S(1)}, u32[]{:S(2)}, u32[]{:S(2)}) %all-to-all-start.1) | async-done | bytes 262176 | tf_op jit(solution)/shard_map/all_to_all | solution.py:446
  42.8 1.3 %shard_map.125 = bf16[64,32,128]{2,1,0:T(8,128)(2,1)} custom-call(f32[512,128]{1,0:T(8,128)S(1)} %bitcast.15, s32[512,1]{1,0:T(8,128)S(1)} %broadcast_in_dim_reshape.16.first_ref, s32[512,1]{1,0:T(8,128)S(1)} %broadcast_in_dim_reshape.17.second_ref, bf16[64,32,128]{2,1,0:T(8,128)(2,1)} %shard_map.124.patched_hbm), custom_call_target="tpu_custom_call", output_to_operand_aliasing={{}: (3, {})} | custom-call | tf_op jit(solution)/shard_map/pallas_call | solution.py:504
  44.1 0.0 copy-start.2
  44.1 0.0 copy-start.5
  44.1 0.0 copy-start.1
  44.1 5.5 %all-to-all-start.2 = ((bf16[64,32,128]{2,1,0:T(8,128)(2,1)}), bf16[64,32,128]{2,1,0:T(8,128)(2,1)S(1)}, u32[]{:S(2)}, u32[]{:S(2)}) async-start(bf16[64,32,128]{2,1,0:T(8,128)(2,1)} %shard_map.125), calls=%async_computation.2 | async-start | bytes 1048576 | tf_op jit(solution)/shard_map/all_to_all | solution.py:446
  49.7 0.0 copy-start.3
  49.7 0.0 copy-start.4
  49.7 1.5 %shard_map.126 = (bf16[8,128,512]{2,1,0:T(8,128)(2,1)S(1)}, f32[8,64,512]{2,1,0:T(8,128)S(1)}) custom-call(f32[8,2,512]{2,1,0:T(2,128)S(1)} %copy-done.2), custom_call_target="tpu_custom_call" | custom-call | tf_op jit(solution)/shard_map/pallas_call | solution.py:500
  51.2 0.2 convert_reduce_fusion
  51.4 17.7 %all-to-all-done.2.got_ref = bf16[64,32,128]{2,1,0:T(8,128)(2,1)S(1)} async-done(((bf16[64,32,128]{2,1,0:T(8,128)(2,1)}), bf16[64,32,128]{2,1,0:T(8,128)(2,1)S(1)}, u32[]{:S(2)}, u32[]{:S(2)}) %all-to-all-start.2) | async-done | bytes 524320 | tf_op jit(solution)/shard_map/all_to_all | solution.py:446
  69.0 4.9 %shard_map.127 = (f32[8,8,512]{2,1,0:T(8,128)}, f32[512,128]{1,0:T(8,128)}) custom-call(s32[8]{0:T(128)S(1)} %multiply_add_fusion.slot_ref, bf16[64,32,128]{2,1,0:T(8,128)(2,1)S(1)} %all-to-all-done.2.got_ref, bf16[8,128,512]{2,1,0:T(8,128)(2,1)S(1)} %get-tuple-element.6.row_wave_ref, f32[8,64,512]{2,1,0:T(8,128)S(1)} %get-tuple-element.7.column_wave_ref, ...), custom_call_target="tpu_custom_call" | custom-call | tf_op jit(solution)/shard_map/pallas_call | solution.py:452
  74.0 5.4 %all-to-all-start.3 = ((f32[64,8,128]{2,1,0:T(8,128)}), f32[64,8,128]{2,1,0:T(8,128)S(1)}, u32[]{:S(2)}, u32[]{:S(2)}) async-start(f32[64,8,128]{2,1,0:T(8,128)} %bitcast.7), calls=%async_computation.3 | async-start | bytes 524288 | tf_op jit(solution)/shard_map/all_to_all | solution.py:446
  79.4 0.1 broadcast_in_dim_reshape.15.second_row_ref
  79.4 0.1 broadcast_in_dim_reshape.14.first_row_ref
  79.5 13.3 %all-to-all-done.3 = f32[64,8,128]{2,1,0:T(8,128)S(1)} async-done(((f32[64,8,128]{2,1,0:T(8,128)}), f32[64,8,128]{2,1,0:T(8,128)S(1)}, u32[]{:S(2)}, u32[]{:S(2)}) %all-to-all-start.3) | async-done | bytes 262176 | tf_op jit(solution)/shard_map/all_to_all | solution.py:446
  92.8 0.6 shard_map.128
  93.5 9.9 %all_to_all.30.parts_ref = f32[8,64,128]{2,1,0:T(8,128)S(1)} all-to-all(f32[8,64,128]{2,1,0:T(8,128)S(1)} %bitcast.17), channel_id=1, replica_groups=mesh['z'=8,'x'=4,'core'=2,'tile'=8] {'x','core'}, dimensions={0} | all-to-all | bytes 524288 | tf_op jit(solution)/shard_map/all_to_all | solution.py:446
  103.4 18.7 %all_to_all.31.parts_ref = f32[64,8,128]{2,1,0:T(8,128)S(1)} all-to-all(f32[64,8,128]{2,1,0:T(8,128)S(1)} %shard_map.129), channel_id=1, replica_groups=mesh['z'=8,'x'=4,'core'=2,'tile'=8] {'z','tile'}, dimensions={0} | all-to-all | bytes 524288 | tf_op jit(solution)/shard_map/all_to_all | solution.py:446
  122.1 1.0 shard_map.130
  (11 shorter events, 0.1 us)
Async XLA Ops:
  2.2 28.0 %all-to-all-start = ((f32[64,2,128]{2,1,0:T(2,128)}), f32[64,2,128]{2,1,0:T(2,128)S(1)}, u32[]{:S(2)}, u32[]{:S(2)}) async-start(f32[64,2,128]{2,1,0:T(2,128)} %shard_map.122), calls=%async_computation | async-start | bytes 131072 | tf_op jit(solution)/shard_map/all_to_all | solution.py:446
  30.9 11.8 %all-to-all-start.1 = ((f32[8,64,128]{2,1,0:T(8,128)}), f32[8,64,128]{2,1,0:T(8,128)S(1)}, u32[]{:S(2)}, u32[]{:S(2)}) async-start(f32[8,64,128]{2,1,0:T(8,128)} %shard_map.123), calls=%async_computation.1 | async-start | bytes 524288 | tf_op jit(solution)/shard_map/all_to_all | solution.py:446
  35.2 1.0 copy-start
  44.1 5.6 %copy-start.2 = (f32[8,2,512]{2,1,0:T(2,128)S(1)}, f32[8,2,512]{2,1,0:T(2,128)}, u32[]{:S(2)}) copy-start(f32[8,2,512]{2,1,0:T(2,128)} %uv_ref.1) | copy-start | bytes 98308
  44.1 7.0 %copy-start.5 = (s32[8,2]{0,1:T(2,128)S(1)}, s32[8,2]{0,1:T(2,128)}, u32[]{:S(2)}) copy-start(s32[8,2]{0,1:T(2,128)} %param.15) | copy-start | bytes 196
  44.1 24.9 %copy-start.1 = (bf16[384,256]{1,0:T(8,128)(2,1)S(1)}, bf16[384,256]{1,0:T(8,128)(2,1)}, u32[]{:S(2)}) copy-start(bf16[384,256]{1,0:T(8,128)(2,1)} %constant.21.clone.cols_ref) | copy-start | bytes 589828
  44.1 24.9 %all-to-all-start.2 = ((bf16[64,32,128]{2,1,0:T(8,128)(2,1)}), bf16[64,32,128]{2,1,0:T(8,128)(2,1)S(1)}, u32[]{:S(2)}, u32[]{:S(2)}) async-start(bf16[64,32,128]{2,1,0:T(8,128)(2,1)} %shard_map.125), calls=%async_computation.2 | async-start | bytes 1048576 | tf_op jit(solution)/shard_map/all_to_all | solution.py:446
  49.7 19.4 %copy-start.3 = (f32[32,128]{1,0:T(8,128)S(1)}, f32[32,128]{1,0:T(8,128)}, u32[]{:S(2)}) copy-start(f32[32,128]{1,0:T(8,128)} %constant.22.clone.taper_ref) | copy-start | bytes 49156
  49.7 19.4 %copy-start.4 = (bf16[64,96]{1,0:T(8,128)(2,1)S(1)}, bf16[64,96]{1,0:T(8,128)(2,1)}, u32[]{:S(2)}) copy-start(bf16[64,96]{1,0:T(8,128)(2,1)} %constant.20.clone.rows_ref) | copy-start | bytes 36868
  74.0 18.9 %all-to-all-start.3 = ((f32[64,8,128]{2,1,0:T(8,128)}), f32[64,8,128]{2,1,0:T(8,128)S(1)}, u32[]{:S(2)}, u32[]{:S(2)}) async-start(f32[64,8,128]{2,1,0:T(8,128)} %bitcast.7), calls=%async_computation.3 | async-start | bytes 524288 | tf_op jit(solution)/shard_map/all_to_all | solution.py:446

commit v7 on v5

--- a/solution.py
+++ b/solution.py
@@ -260,7 +260,7 @@
 
 def main_kernel(
     slot_ref, got_ref, row_wave_ref, column_wave_ref, seen_in, flag_in, rows_ref, cols_ref, taper_ref,
-    res_ref, grad_ref, beam_ref, seen_ref, flag_ref, side_ref, z_ref, dz_ref, held_ref, sems,
+    res_ref, out_ref, grad_ref, beam_ref, seen_ref, flag_ref, side_ref, z_ref, dz_ref, held_ref, sems,
 ):
     copies = [
         pltpu.make_async_copy(a, b, sems.at[i])
@@ -271,7 +271,7 @@
     for copy in copies:
         copy.start()
     got = got_ref[:, 0:ENDS, :].astype(F32)
-    beam_ref[...] = (got[:, :SUBS] + got[:, SUBS:]).reshape(TABLE, LANES)
+    beam_ref[0:TABLE, :] = (got[:, :SUBS] + got[:, SUBS:]).reshape(TABLE, LANES)
     narrow = lax.broadcasted_iota(S32, (SIDE // 2, LANES), 1) // SIDE
     lane = lax.broadcasted_iota(S32, (SIDE, LANES), 1) // SIDE
     taper = taper_ref[...]
@@ -397,6 +397,7 @@
         for half, (dp, dq) in enumerate(((dp_re, dq_re), (dp_im, dq_im))):
             grad = jnp.where(lane == 0, dp, jnp.where(lane == 1, turn(dp, 3), dq))
             grad_ref[pl.ds(k + SUBS * half, SIDE, stride=2 * SUBS), :] = grad
+    out_ref[...] = grad_ref[0:TABLE, :]
 
 
 SMEM = pl.BlockSpec(memory_space=pltpu.SMEM)
@@ -457,7 +458,8 @@
         [SMEM] + [VMEM] * 3 + [HBM] * 2 + [VMEM] * 3,
         (VMEM, VMEM),
         [
-            pltpu.VMEM((TABLE, LANES), F32),
+            pltpu.VMEM((TABLE + 2 * SUBS, LANES), F32),
+            pltpu.VMEM((TABLE + 2 * SUBS, LANES), F32),
             pltpu.VMEM((SUBS, 8, VIS), F32),
             pltpu.VMEM((SUBS, VIS), S32),
             pltpu.VMEM((SUBS, 6, SIDE, LANES), F32),

time: 124 us -> 124 us (level)
  no operation moved by 1% of the time
where the time goes in v7:
time: 124 us; the launch traced here: 123 us
  waiting for transfers between devices  45.9 us (37%)
  starting transfers between devices  31.8 us (26%)
  blocking collectives  28.6 us (23%)
  Pallas kernels  14.5 us (12%)
    all_to_all x4, waiting for transfers between devices, exchange(): return lax.all_to_all(x, axes, split_axis=0, concat_axis=0, tiled=True)  45.9 us
    all_to_all x4, starting transfers between devices, exchange(): return lax.all_to_all(x, axes, split_axis=0, concat_axis=0, tiled=True)  31.8 us
    all_to_all x2, blocking collectives, exchange(): return lax.all_to_all(x, axes, split_axis=0, concat_axis=0, tiled=True)  28.6 us
    pallas_call x1, Pallas kernels, main(): call(main_kernel, (shape((SUBS, 8, VIS)), shape((TABLE, LANES))), [SMEM]...  4.92 us
    pallas_call x1, Pallas kernels, cut(): pl.pallas_call(cut_kernel, out_shape=shape((PEERS, 2 * ENDS, LANES), BF16...  2.82 us
  transfers between devices with their start and end apart: 4, of which 4 were waited for; matrix products, arithmetic and copies ran while one was open for 1% of the time, Pallas kernels for 3%

profile of v7, /device:TPU:8, one launch (start us, length us, event | category | flops | bytes accessed | tf_op | source)
XLA Modules:
  0.0 123.2 jit_solution(7515783032080896874)
XLA Ops:
  0.6 1.6 %shard_map.122 = f32[64,2,128]{2,1,0:T(2,128)} custom-call(s32[2,8]{1,0:T(2,128)} %bitcast.19, s32[8]{0:T(128)} %intervals_in.1, s32[2,8]{1,0:T(2,128)} %bitcast.20, f32[8,2,4,1024]{3,2,1,0:T(4,128)} %terms_in.1), custom_call_target="tpu_custom_call" | custom-call | tf_op jit(solution)/shard_map/pallas_call | solution.py:481
  2.2 16.6 %all-to-all-start = ((f32[64,2,128]{2,1,0:T(2,128)}), f32[64,2,128]{2,1,0:T(2,128)S(1)}, u32[]{:S(2)}, u32[]{:S(2)}) async-start(f32[64,2,128]{2,1,0:T(2,128)} %shard_map.122), calls=%async_computation | async-start | bytes 131072 | tf_op jit(solution)/shard_map/all_to_all | solution.py:449
  18.8 0.1 pad_add_fusion.place_ref
  18.9 11.3 %all-to-all-done.got_ref = f32[64,2,128]{2,1,0:T(2,128)S(1)} async-done(((f32[64,2,128]{2,1,0:T(2,128)}), f32[64,2,128]{2,1,0:T(2,128)S(1)}, u32[]{:S(2)}, u32[]{:S(2)}) %all-to-all-start) | async-done | bytes 65568 | tf_op jit(solution)/shard_map/all_to_all | solution.py:449
  30.2 0.8 shard_map.123
  31.0 4.3 %all-to-all-start.1 = ((f32[8,64,128]{2,1,0:T(8,128)}), f32[8,64,128]{2,1,0:T(8,128)S(1)}, u32[]{:S(2)}, u32[]{:S(2)}) async-start(f32[8,64,128]{2,1,0:T(8,128)} %shard_map.123), calls=%async_computation.1 | async-start | bytes 524288 | tf_op jit(solution)/shard_map/all_to_all | solution.py:449
  35.4 0.1 slice.23.wanted_ref
  35.4 0.1 fusion.1
  35.5 0.1 broadcast_in_dim_reshape.16.first_ref
  35.6 0.1 broadcast_in_dim_reshape.17.second_ref
  35.8 0.6 copy-done
  36.3 2.8 %shard_map.124.patched_hbm = bf16[64,32,128]{2,1,0:T(8,128)(2,1)} custom-call(s32[2]{0:T(128)S(1)} %pad_add_fusion.place_ref, s32[64,16]{1,0:T(8,128)S(1)} %slice.23.wanted_ref, bf16[8,256,128]{2,1,0:T(8,128)(2,1)S(1)} %copy-done), custom_call_target="tpu_custom_call" | custom-call | tf_op jit(solution)/shard_map/pallas_call | solution.py:426
  39.2 3.7 %all-to-all-done.1 = f32[8,64,128]{2,1,0:T(8,128)S(1)} async-done(((f32[8,64,128]{2,1,0:T(8,128)}), f32[8,64,128]{2,1,0:T(8,128)S(1)}, u32[]{:S(2)}, u32[]{:S(2)}) %all-to-all-start.1) | async-done | bytes 262176 | tf_op jit(solution)/shard_map/all_to_all | solution.py:449
  42.8 1.3 %shard_map.125 = bf16[64,32,128]{2,1,0:T(8,128)(2,1)} custom-call(f32[512,128]{1,0:T(8,128)S(1)} %bitcast.15, s32[512,1]{1,0:T(8,128)S(1)} %broadcast_in_dim_reshape.16.first_ref, s32[512,1]{1,0:T(8,128)S(1)} %broadcast_in_dim_reshape.17.second_ref, bf16[64,32,128]{2,1,0:T(8,128)(2,1)} %shard_map.124.patched_hbm), custom_call_target="tpu_custom_call", output_to_operand_aliasing={{}: (3, {})} | custom-call | tf_op jit(solution)/shard_map/pallas_call | solution.py:513
  44.2 0.0 copy-start.2
  44.2 0.0 copy-start.5
  44.2 0.0 copy-start.1
  44.2 5.5 %all-to-all-start.2 = ((bf16[64,32,128]{2,1,0:T(8,128)(2,1)}), bf16[64,32,128]{2,1,0:T(8,128)(2,1)S(1)}, u32[]{:S(2)}, u32[]{:S(2)}) async-start(bf16[64,32,128]{2,1,0:T(8,128)(2,1)} %shard_map.125), calls=%async_computation.2 | async-start | bytes 1048576 | tf_op jit(solution)/shard_map/all_to_all | solution.py:449
  49.7 0.0 copy-start.3
  49.7 0.0 copy-start.4
  49.8 1.5 %shard_map.126 = (bf16[8,128,512]{2,1,0:T(8,128)(2,1)S(1)}, f32[8,64,512]{2,1,0:T(8,128)S(1)}) custom-call(f32[8,2,512]{2,1,0:T(2,128)S(1)} %copy-done.2), custom_call_target="tpu_custom_call" | custom-call | tf_op jit(solution)/shard_map/pallas_call | solution.py:509
  51.2 0.2 convert_reduce_fusion
  51.4 17.7 %all-to-all-done.2.got_ref = bf16[64,32,128]{2,1,0:T(8,128)(2,1)S(1)} async-done(((bf16[64,32,128]{2,1,0:T(8,128)(2,1)}), bf16[64,32,128]{2,1,0:T(8,128)(2,1)S(1)}, u32[]{:S(2)}, u32[]{:S(2)}) %all-to-all-start.2) | async-done | bytes 524320 | tf_op jit(solution)/shard_map/all_to_all | solution.py:449
  69.1 4.9 %shard_map.127 = (f32[8,8,512]{2,1,0:T(8,128)}, f32[512,128]{1,0:T(8,128)}) custom-call(s32[8]{0:T(128)S(1)} %multiply_add_fusion.slot_ref, bf16[64,32,128]{2,1,0:T(8,128)(2,1)S(1)} %all-to-all-done.2.got_ref, bf16[8,128,512]{2,1,0:T(8,128)(2,1)S(1)} %get-tuple-element.6.row_wave_ref, f32[8,64,512]{2,1,0:T(8,128)S(1)} %get-tuple-element.7.column_wave_ref, ...), custom_call_target="tpu_custom_call" | custom-call | tf_op jit(solution)/shard_map/pallas_call | solution.py:455
  74.0 5.4 %all-to-all-start.3 = ((f32[64,8,128]{2,1,0:T(8,128)}), f32[64,8,128]{2,1,0:T(8,128)S(1)}, u32[]{:S(2)}, u32[]{:S(2)}) async-start(f32[64,8,128]{2,1,0:T(8,128)} %bitcast.7), calls=%async_computation.3 | async-start | bytes 524288 | tf_op jit(solution)/shard_map/all_to_all | solution.py:449
  79.4 0.1 broadcast_in_dim_reshape.15.second_row_ref
  79.5 0.1 broadcast_in_dim_reshape.14.first_row_ref
  79.6 13.3 %all-to-all-done.3 = f32[64,8,128]{2,1,0:T(8,128)S(1)} async-done(((f32[64,8,128]{2,1,0:T(8,128)}), f32[64,8,128]{2,1,0:T(8,128)S(1)}, u32[]{:S(2)}, u32[]{:S(2)}) %all-to-all-start.3) | async-done | bytes 262176 | tf_op jit(solution)/shard_map/all_to_all | solution.py:449
  92.9 0.6 shard_map.128
  93.5 9.9 %all_to_all.30.parts_ref = f32[8,64,128]{2,1,0:T(8,128)S(1)} all-to-all(f32[8,64,128]{2,1,0:T(8,128)S(1)} %bitcast.17), channel_id=1, replica_groups=mesh['z'=8,'x'=4,'core'=2,'tile'=8] {'x','core'}, dimensions={0} | all-to-all | bytes 524288 | tf_op jit(solution)/shard_map/all_to_all | solution.py:449
  103.5 18.7 %all_to_all.31.parts_ref = f32[64,8,128]{2,1,0:T(8,128)S(1)} all-to-all(f32[64,8,128]{2,1,0:T(8,128)S(1)} %shard_map.129), channel_id=1, replica_groups=mesh['z'=8,'x'=4,'core'=2,'tile'=8] {'z','tile'}, dimensions={0} | all-to-all | bytes 524288 | tf_op jit(solution)/shard_map/all_to_all | solution.py:449
  122.2 1.0 shard_map.130
  (11 shorter events, 0.1 us)
Async XLA Ops:
  2.2 28.0 %all-to-all-start = ((f32[64,2,128]{2,1,0:T(2,128)}), f32[64,2,128]{2,1,0:T(2,128)S(1)}, u32[]{:S(2)}, u32[]{:S(2)}) async-start(f32[64,2,128]{2,1,0:T(2,128)} %shard_map.122), calls=%async_computation | async-start | bytes 131072 | tf_op jit(solution)/shard_map/all_to_all | solution.py:449
  31.0 11.9 %all-to-all-start.1 = ((f32[8,64,128]{2,1,0:T(8,128)}), f32[8,64,128]{2,1,0:T(8,128)S(1)}, u32[]{:S(2)}, u32[]{:S(2)}) async-start(f32[8,64,128]{2,1,0:T(8,128)} %shard_map.123), calls=%async_computation.1 | async-start | bytes 524288 | tf_op jit(solution)/shard_map/all_to_all | solution.py:449
  35.3 1.0 copy-start
  44.2 5.6 %copy-start.2 = (f32[8,2,512]{2,1,0:T(2,128)S(1)}, f32[8,2,512]{2,1,0:T(2,128)}, u32[]{:S(2)}) copy-start(f32[8,2,512]{2,1,0:T(2,128)} %uv_ref.1) | copy-start | bytes 98308
  44.2 7.0 %copy-start.5 = (s32[8,2]{0,1:T(2,128)S(1)}, s32[8,2]{0,1:T(2,128)}, u32[]{:S(2)}) copy-start(s32[8,2]{0,1:T(2,128)} %param.15) | copy-start | bytes 196
  44.2 24.9 %copy-start.1 = (bf16[384,256]{1,0:T(8,128)(2,1)S(1)}, bf16[384,256]{1,0:T(8,128)(2,1)}, u32[]{:S(2)}) copy-start(bf16[384,256]{1,0:T(8,128)(2,1)} %constant.21.clone.cols_ref) | copy-start | bytes 589828
  44.2 24.9 %all-to-all-start.2 = ((bf16[64,32,128]{2,1,0:T(8,128)(2,1)}), bf16[64,32,128]{2,1,0:T(8,128)(2,1)S(1)}, u32[]{:S(2)}, u32[]{:S(2)}) async-start(bf16[64,32,128]{2,1,0:T(8,128)(2,1)} %shard_map.125), calls=%async_computation.2 | async-start | bytes 1048576 | tf_op jit(solution)/shard_map/all_to_all | solution.py:449
  49.7 19.4 %copy-start.3 = (f32[32,128]{1,0:T(8,128)S(1)}, f32[32,128]{1,0:T(8,128)}, u32[]{:S(2)}) copy-start(f32[32,128]{1,0:T(8,128)} %constant.22.clone.taper_ref) | copy-start | bytes 49156
  49.7 19.4 %copy-start.4 = (bf16[64,96]{1,0:T(8,128)(2,1)S(1)}, bf16[64,96]{1,0:T(8,128)(2,1)}, u32[]{:S(2)}) copy-start(bf16[64,96]{1,0:T(8,128)(2,1)} %constant.20.clone.rows_ref) | copy-start | bytes 36868
  74.0 18.8 %all-to-all-start.3 = ((f32[64,8,128]{2,1,0:T(8,128)}), f32[64,8,128]{2,1,0:T(8,128)S(1)}, u32[]{:S(2)}, u32[]{:S(2)}) async-start(f32[64,8,128]{2,1,0:T(8,128)} %bitcast.7), calls=%async_computation.3 | async-start | bytes 524288 | tf_op jit(solution)/shard_map/all_to_all | solution.py:449

commit v8 on v7

--- a/solution.py
+++ b/solution.py
@@ -260,7 +260,7 @@
 
 def main_kernel(
     slot_ref, got_ref, row_wave_ref, column_wave_ref, seen_in, flag_in, rows_ref, cols_ref, taper_ref,
-    res_ref, out_ref, grad_ref, beam_ref, seen_ref, flag_ref, side_ref, z_ref, dz_ref, held_ref, sems,
+    res_out, out_ref, res_ref, grad_ref, beam_ref, seen_ref, flag_ref, side_ref, z_ref, dz_ref, held_ref, sems,
 ):
     copies = [
         pltpu.make_async_copy(a, b, sems.at[i])
@@ -375,6 +375,8 @@
             one(k, 0)
         if k > 0:
             two(k - 1, 0)
+    sent = pltpu.make_async_copy(res_ref, res_out, sems.at[2])
+    sent.start()
 
     for k in range(SUBS):
         d = dz_ref[k]
@@ -398,6 +400,7 @@
             grad = jnp.where(lane == 0, dp, jnp.where(lane == 1, turn(dp, 3), dq))
             grad_ref[pl.ds(k + SUBS * half, SIDE, stride=2 * SUBS), :] = grad
     out_ref[...] = grad_ref[0:TABLE, :]
+    sent.wait()
 
 
 SMEM = pl.BlockSpec(memory_space=pltpu.SMEM)
@@ -456,8 +459,9 @@
         main_kernel,
         (shape((SUBS, 8, VIS)), shape((TABLE, LANES))),
         [SMEM] + [VMEM] * 3 + [HBM] * 2 + [VMEM] * 3,
-        (VMEM, VMEM),
+        (HBM, VMEM),
         [
+            pltpu.VMEM((SUBS, 8, VIS), F32),
             pltpu.VMEM((TABLE + 2 * SUBS, LANES), F32),
             pltpu.VMEM((TABLE + 2 * SUBS, LANES), F32),
             pltpu.VMEM((SUBS, 8, VIS), F32),

time: 124 us -> 124 us (level)
  no operation moved by 1% of the time
where the time goes in v8:
time: 124 us
  waiting for transfers between devices  45.9 us (37%)
  starting transfers between devices  31.8 us (26%)
  blocking collectives  28.6 us (23%)
  Pallas kernels  15.1 us (12%)
    all_to_all x4, waiting for transfers between devices, exchange(): return lax.all_to_all(x, axes, split_axis=0, concat_axis=0, tiled=True)  45.9 us
    all_to_all x4, starting transfers between devices, exchange(): return lax.all_to_all(x, axes, split_axis=0, concat_axis=0, tiled=True)  31.8 us
    all_to_all x2, blocking collectives, exchange(): return lax.all_to_all(x, axes, split_axis=0, concat_axis=0, tiled=True)  28.6 us
    pallas_call x1, Pallas kernels, main(): call(main_kernel, (shape((SUBS, 8, VIS)), shape((TABLE, LANES))), [SMEM]...  5.49 us
    pallas_call x1, Pallas kernels, cut(): pl.pallas_call(cut_kernel, out_shape=shape((PEERS, 2 * ENDS, LANES), BF16...  2.82 us
  transfers between devices with their start and end apart: 4, of which 4 were waited for; matrix products, arithmetic and copies ran while one was open for 1% of the time, Pallas kernels for 3%

profile of v8, /device:TPU:8, one launch (start us, length us, event | category | flops | bytes accessed | tf_op | source)
XLA Modules:
  0.0 123.7 jit_solution(3177372408804701208)
XLA Ops:
  0.6 1.6 %shard_map.122 = f32[64,2,128]{2,1,0:T(2,128)} custom-call(s32[2,8]{1,0:T(2,128)} %bitcast.19, s32[8]{0:T(128)} %intervals_in.1, s32[2,8]{1,0:T(2,128)} %bitcast.20, f32[8,2,4,1024]{3,2,1,0:T(4,128)} %terms_in.1), custom_call_target="tpu_custom_call" | custom-call | tf_op jit(solution)/shard_map/pallas_call | solution.py:485
  2.2 16.6 %all-to-all-start = ((f32[64,2,128]{2,1,0:T(2,128)}), f32[64,2,128]{2,1,0:T(2,128)S(1)}, u32[]{:S(2)}, u32[]{:S(2)}) async-start(f32[64,2,128]{2,1,0:T(2,128)} %shard_map.122), calls=%async_computation | async-start | bytes 131072 | tf_op jit(solution)/shard_map/all_to_all | solution.py:452
  18.8 0.1 pad_add_fusion.place_ref
  18.9 11.3 %all-to-all-done.got_ref = f32[64,2,128]{2,1,0:T(2,128)S(1)} async-done(((f32[64,2,128]{2,1,0:T(2,128)}), f32[64,2,128]{2,1,0:T(2,128)S(1)}, u32[]{:S(2)}, u32[]{:S(2)}) %all-to-all-start) | async-done | bytes 65568 | tf_op jit(solution)/shard_map/all_to_all | solution.py:452
  30.2 0.8 shard_map.123
  31.0 4.3 %all-to-all-start.1 = ((f32[8,64,128]{2,1,0:T(8,128)}), f32[8,64,128]{2,1,0:T(8,128)S(1)}, u32[]{:S(2)}, u32[]{:S(2)}) async-start(f32[8,64,128]{2,1,0:T(8,128)} %shard_map.123), calls=%async_computation.1 | async-start | bytes 524288 | tf_op jit(solution)/shard_map/all_to_all | solution.py:452
  35.4 0.1 slice.23.wanted_ref
  35.4 0.1 fusion.1
  35.5 0.1 broadcast_in_dim_reshape.16.first_ref
  35.6 0.1 broadcast_in_dim_reshape.17.second_ref
  35.8 0.6 copy-done
  36.3 2.8 %shard_map.124.patched_hbm = bf16[64,32,128]{2,1,0:T(8,128)(2,1)} custom-call(s32[2]{0:T(128)S(1)} %pad_add_fusion.place_ref, s32[64,16]{1,0:T(8,128)S(1)} %slice.23.wanted_ref, bf16[8,256,128]{2,1,0:T(8,128)(2,1)S(1)} %copy-done), custom_call_target="tpu_custom_call" | custom-call | tf_op jit(solution)/shard_map/pallas_call | solution.py:429
  39.2 3.7 %all-to-all-done.1 = f32[8,64,128]{2,1,0:T(8,128)S(1)} async-done(((f32[8,64,128]{2,1,0:T(8,128)}), f32[8,64,128]{2,1,0:T(8,128)S(1)}, u32[]{:S(2)}, u32[]{:S(2)}) %all-to-all-start.1) | async-done | bytes 262176 | tf_op jit(solution)/shard_map/all_to_all | solution.py:452
  42.8 1.3 %shard_map.125 = bf16[64,32,128]{2,1,0:T(8,128)(2,1)} custom-call(f32[512,128]{1,0:T(8,128)S(1)} %bitcast.15, s32[512,1]{1,0:T(8,128)S(1)} %broadcast_in_dim_reshape.16.first_ref, s32[512,1]{1,0:T(8,128)S(1)} %broadcast_in_dim_reshape.17.second_ref, bf16[64,32,128]{2,1,0:T(8,128)(2,1)} %shard_map.124.patched_hbm), custom_call_target="tpu_custom_call", output_to_operand_aliasing={{}: (3, {})} | custom-call | tf_op jit(solution)/shard_map/pallas_call | solution.py:517
  44.2 0.0 copy-start.2
  44.2 0.0 copy-start.5
  44.2 0.0 copy-start.1
  44.2 5.5 %all-to-all-start.2 = ((bf16[64,32,128]{2,1,0:T(8,128)(2,1)}), bf16[64,32,128]{2,1,0:T(8,128)(2,1)S(1)}, u32[]{:S(2)}, u32[]{:S(2)}) async-start(bf16[64,32,128]{2,1,0:T(8,128)(2,1)} %shard_map.125), calls=%async_computation.2 | async-start | bytes 1048576 | tf_op jit(solution)/shard_map/all_to_all | solution.py:452
  49.7 0.0 copy-start.3
  49.7 0.0 copy-start.4
  49.8 1.5 %shard_map.126 = (bf16[8,128,512]{2,1,0:T(8,128)(2,1)S(1)}, f32[8,64,512]{2,1,0:T(8,128)S(1)}) custom-call(f32[8,2,512]{2,1,0:T(2,128)S(1)} %copy-done.2), custom_call_target="tpu_custom_call" | custom-call | tf_op jit(solution)/shard_map/pallas_call | solution.py:513
  51.2 0.2 convert_reduce_fusion
  51.4 17.7 %all-to-all-done.2.got_ref = bf16[64,32,128]{2,1,0:T(8,128)(2,1)S(1)} async-done(((bf16[64,32,128]{2,1,0:T(8,128)(2,1)}), bf16[64,32,128]{2,1,0:T(8,128)(2,1)S(1)}, u32[]{:S(2)}, u32[]{:S(2)}) %all-to-all-start.2) | async-done | bytes 524320 | tf_op jit(solution)/shard_map/all_to_all | solution.py:452
  69.1 5.5 %shard_map.127 = (f32[8,8,512]{2,1,0:T(8,128)}, f32[512,128]{1,0:T(8,128)}) custom-call(s32[8]{0:T(128)S(1)} %multiply_add_fusion.slot_ref, bf16[64,32,128]{2,1,0:T(8,128)(2,1)S(1)} %all-to-all-done.2.got_ref, bf16[8,128,512]{2,1,0:T(8,128)(2,1)S(1)} %get-tuple-element.6.row_wave_ref, f32[8,64,512]{2,1,0:T(8,128)S(1)} %get-tuple-element.7.column_wave_ref, ...), custom_call_target="tpu_custom_call" | custom-call | tf_op jit(solution)/shard_map/pallas_call | solution.py:458
  74.6 5.4 %all-to-all-start.3 = ((f32[64,8,128]{2,1,0:T(8,128)}), f32[64,8,128]{2,1,0:T(8,128)S(1)}, u32[]{:S(2)}, u32[]{:S(2)}) async-start(f32[64,8,128]{2,1,0:T(8,128)} %bitcast.7), calls=%async_computation.3 | async-start | bytes 524288 | tf_op jit(solution)/shard_map/all_to_all | solution.py:452
  80.0 0.1 broadcast_in_dim_reshape.15.second_row_ref
  80.1 0.1 broadcast_in_dim_reshape.14.first_row_ref
  80.2 13.3 %all-to-all-done.3 = f32[64,8,128]{2,1,0:T(8,128)S(1)} async-done(((f32[64,8,128]{2,1,0:T(8,128)}), f32[64,8,128]{2,1,0:T(8,128)S(1)}, u32[]{:S(2)}, u32[]{:S(2)}) %all-to-all-start.3) | async-done | bytes 262176 | tf_op jit(solution)/shard_map/all_to_all | solution.py:452
  93.5 0.6 shard_map.128
  94.1 9.9 %all_to_all.30.parts_ref = f32[8,64,128]{2,1,0:T(8,128)S(1)} all-to-all(f32[8,64,128]{2,1,0:T(8,128)S(1)} %bitcast.17), channel_id=1, replica_groups=mesh['z'=8,'x'=4,'core'=2,'tile'=8] {'x','core'}, dimensions={0} | all-to-all | bytes 524288 | tf_op jit(solution)/shard_map/all_to_all | solution.py:452
  104.1 18.7 %all_to_all.31.parts_ref = f32[64,8,128]{2,1,0:T(8,128)S(1)} all-to-all(f32[64,8,128]{2,1,0:T(8,128)S(1)} %shard_map.129), channel_id=1, replica_groups=mesh['z'=8,'x'=4,'core'=2,'tile'=8] {'z','tile'}, dimensions={0} | all-to-all | bytes 524288 | tf_op jit(solution)/shard_map/all_to_all | solution.py:452
  122.8 1.0 shard_map.130
  (11 shorter events, 0.1 us)
Async XLA Ops:
  2.2 28.0 %all-to-all-start = ((f32[64,2,128]{2,1,0:T(2,128)}), f32[64,2,128]{2,1,0:T(2,128)S(1)}, u32[]{:S(2)}, u32[]{:S(2)}) async-start(f32[64,2,128]{2,1,0:T(2,128)} %shard_map.122), calls=%async_computation | async-start | bytes 131072 | tf_op jit(solution)/shard_map/all_to_all | solution.py:452
  31.0 11.9 %all-to-all-start.1 = ((f32[8,64,128]{2,1,0:T(8,128)}), f32[8,64,128]{2,1,0:T(8,128)S(1)}, u32[]{:S(2)}, u32[]{:S(2)}) async-start(f32[8,64,128]{2,1,0:T(8,128)} %shard_map.123), calls=%async_computation.1 | async-start | bytes 524288 | tf_op jit(solution)/shard_map/all_to_all | solution.py:452
  35.3 1.0 copy-start
  44.2 5.6 %copy-start.2 = (f32[8,2,512]{2,1,0:T(2,128)S(1)}, f32[8,2,512]{2,1,0:T(2,128)}, u32[]{:S(2)}) copy-start(f32[8,2,512]{2,1,0:T(2,128)} %uv_ref.1) | copy-start | bytes 98308
  44.2 7.0 %copy-start.5 = (s32[8,2]{0,1:T(2,128)S(1)}, s32[8,2]{0,1:T(2,128)}, u32[]{:S(2)}) copy-start(s32[8,2]{0,1:T(2,128)} %param.15) | copy-start | bytes 196
  44.2 24.9 %copy-start.1 = (bf16[384,256]{1,0:T(8,128)(2,1)S(1)}, bf16[384,256]{1,0:T(8,128)(2,1)}, u32[]{:S(2)}) copy-start(bf16[384,256]{1,0:T(8,128)(2,1)} %constant.21.clone.cols_ref) | copy-start | bytes 589828
  44.2 24.9 %all-to-all-start.2 = ((bf16[64,32,128]{2,1,0:T(8,128)(2,1)}), bf16[64,32,128]{2,1,0:T(8,128)(2,1)S(1)}, u32[]{:S(2)}, u32[]{:S(2)}) async-start(bf16[64,32,128]{2,1,0:T(8,128)(2,1)} %shard_map.125), calls=%async_computation.2 | async-start | bytes 1048576 | tf_op jit(solution)/shard_map/all_to_all | solution.py:452
  49.7 19.4 %copy-start.3 = (f32[32,128]{1,0:T(8,128)S(1)}, f32[32,128]{1,0:T(8,128)}, u32[]{:S(2)}) copy-start(f32[32,128]{1,0:T(8,128)} %constant.22.clone.taper_ref) | copy-start | bytes 49156
  49.7 19.4 %copy-start.4 = (bf16[64,96]{1,0:T(8,128)(2,1)S(1)}, bf16[64,96]{1,0:T(8,128)(2,1)}, u32[]{:S(2)}) copy-start(bf16[64,96]{1,0:T(8,128)(2,1)} %constant.20.clone.rows_ref) | copy-start | bytes 36868
  74.6 18.8 %all-to-all-start.3 = ((f32[64,8,128]{2,1,0:T(8,128)}), f32[64,8,128]{2,1,0:T(8,128)S(1)}, u32[]{:S(2)}, u32[]{:S(2)}) async-start(f32[64,8,128]{2,1,0:T(8,128)} %bitcast.7), calls=%async_computation.3 | async-start | bytes 524288 | tf_op jit(solution)/shard_map/all_to_all | solution.py:452

commit v9 on v7

--- a/solution.py
+++ b/solution.py
@@ -249,7 +249,9 @@
                     for i in range(1, 4):
                         total = jnp.where(lane == i, turned[i][(i - at) % 4], total)
                     out_ref[:, interval, 2 * half + part, block * LANES : (block + 1) * LANES] = total
-        lanes = pl.ds(block * LANES, LANES)
+        if block % 2 == 0:
+            continue
+        lanes = pl.ds((block - 1) * LANES, 2 * LANES)
         copies.append(
             pltpu.make_async_copy(out_ref.at[:, :, :, lanes], out_hbm.at[:, :, :, lanes], sems.at[block])
         )

time: 124 us -> 124 us (level)
  no operation moved by 1% of the time
where the time goes in v9:
time: 124 us; the launch traced here: 123 us
  waiting for transfers between devices  45.9 us (37%)
  starting transfers between devices  31.8 us (26%)
  blocking collectives  28.6 us (23%)
  Pallas kernels  14.6 us (12%)
    all_to_all x4, waiting for transfers between devices, exchange(): return lax.all_to_all(x, axes, split_axis=0, concat_axis=0, tiled=True)  45.9 us
    all_to_all x4, starting transfers between devices, exchange(): return lax.all_to_all(x, axes, split_axis=0, concat_axis=0, tiled=True)  31.8 us
    all_to_all x2, blocking collectives, exchange(): return lax.all_to_all(x, axes, split_axis=0, concat_axis=0, tiled=True)  28.6 us
    pallas_call x1, Pallas kernels, main(): call(main_kernel, (shape((SUBS, 8, VIS)), shape((TABLE, LANES))), [SMEM]...  4.92 us
    pallas_call x1, Pallas kernels, cut(): pl.pallas_call(cut_kernel, out_shape=shape((PEERS, 2 * ENDS, LANES), BF16...  2.82 us
  transfers between devices with their start and end apart: 4, of which 4 were waited for; matrix products, arithmetic and copies ran while one was open for 1% of the time, Pallas kernels for 3%

profile of v9, /device:TPU:8, one launch (start us, length us, event | category | flops | bytes accessed | tf_op | source)
XLA Modules:
  0.0 123.2 jit_solution(12315087626581403428)
XLA Ops:
  0.6 1.6 %shard_map.122 = f32[64,2,128]{2,1,0:T(2,128)} custom-call(s32[2,8]{1,0:T(2,128)} %bitcast.19, s32[8]{0:T(128)} %intervals_in.1, s32[2,8]{1,0:T(2,128)} %bitcast.20, f32[8,2,4,1024]{3,2,1,0:T(4,128)} %terms_in.1), custom_call_target="tpu_custom_call" | custom-call | tf_op jit(solution)/shard_map/pallas_call | solution.py:483
  2.2 16.6 %all-to-all-start = ((f32[64,2,128]{2,1,0:T(2,128)}), f32[64,2,128]{2,1,0:T(2,128)S(1)}, u32[]{:S(2)}, u32[]{:S(2)}) async-start(f32[64,2,128]{2,1,0:T(2,128)} %shard_map.122), calls=%async_computation | async-start | bytes 131072 | tf_op jit(solution)/shard_map/all_to_all | solution.py:451
  18.8 0.1 pad_add_fusion.place_ref
  18.9 11.3 %all-to-all-done.got_ref = f32[64,2,128]{2,1,0:T(2,128)S(1)} async-done(((f32[64,2,128]{2,1,0:T(2,128)}), f32[64,2,128]{2,1,0:T(2,128)S(1)}, u32[]{:S(2)}, u32[]{:S(2)}) %all-to-all-start) | async-done | bytes 65568 | tf_op jit(solution)/shard_map/all_to_all | solution.py:451
  30.2 0.8 shard_map.123
  31.0 4.3 %all-to-all-start.1 = ((f32[8,64,128]{2,1,0:T(8,128)}), f32[8,64,128]{2,1,0:T(8,128)S(1)}, u32[]{:S(2)}, u32[]{:S(2)}) async-start(f32[8,64,128]{2,1,0:T(8,128)} %shard_map.123), calls=%async_computation.1 | async-start | bytes 524288 | tf_op jit(solution)/shard_map/all_to_all | solution.py:451
  35.4 0.1 slice.23.wanted_ref
  35.4 0.1 fusion.1
  35.5 0.1 broadcast_in_dim_reshape.16.first_ref
  35.6 0.1 broadcast_in_dim_reshape.17.second_ref
  35.8 0.6 copy-done
  36.3 2.8 %shard_map.124.patched_hbm = bf16[64,32,128]{2,1,0:T(8,128)(2,1)} custom-call(s32[2]{0:T(128)S(1)} %pad_add_fusion.place_ref, s32[64,16]{1,0:T(8,128)S(1)} %slice.23.wanted_ref, bf16[8,256,128]{2,1,0:T(8,128)(2,1)S(1)} %copy-done), custom_call_target="tpu_custom_call" | custom-call | tf_op jit(solution)/shard_map/pallas_call | solution.py:428
  39.2 3.7 %all-to-all-done.1 = f32[8,64,128]{2,1,0:T(8,128)S(1)} async-done(((f32[8,64,128]{2,1,0:T(8,128)}), f32[8,64,128]{2,1,0:T(8,128)S(1)}, u32[]{:S(2)}, u32[]{:S(2)}) %all-to-all-start.1) | async-done | bytes 262176 | tf_op jit(solution)/shard_map/all_to_all | solution.py:451
  42.8 1.3 %shard_map.125 = bf16[64,32,128]{2,1,0:T(8,128)(2,1)} custom-call(f32[512,128]{1,0:T(8,128)S(1)} %bitcast.15, s32[512,1]{1,0:T(8,128)S(1)} %broadcast_in_dim_reshape.16.first_ref, s32[512,1]{1,0:T(8,128)S(1)} %broadcast_in_dim_reshape.17.second_ref, bf16[64,32,128]{2,1,0:T(8,128)(2,1)} %shard_map.124.patched_hbm), custom_call_target="tpu_custom_call", output_to_operand_aliasing={{}: (3, {})} | custom-call | tf_op jit(solution)/shard_map/pallas_call | solution.py:515
  44.2 0.0 copy-start.2
  44.2 0.0 copy-start.5
  44.2 0.0 copy-start.1
  44.2 5.5 %all-to-all-start.2 = ((bf16[64,32,128]{2,1,0:T(8,128)(2,1)}), bf16[64,32,128]{2,1,0:T(8,128)(2,1)S(1)}, u32[]{:S(2)}, u32[]{:S(2)}) async-start(bf16[64,32,128]{2,1,0:T(8,128)(2,1)} %shard_map.125), calls=%async_computation.2 | async-start | bytes 1048576 | tf_op jit(solution)/shard_map/all_to_all | solution.py:451
  49.7 0.0 copy-start.3
  49.7 0.0 copy-start.4
  49.8 1.5 %shard_map.126 = (bf16[8,128,512]{2,1,0:T(8,128)(2,1)S(1)}, f32[8,64,512]{2,1,0:T(8,128)S(1)}) custom-call(f32[8,2,512]{2,1,0:T(2,128)S(1)} %copy-done.2), custom_call_target="tpu_custom_call" | custom-call | tf_op jit(solution)/shard_map/pallas_call | solution.py:511
  51.2 0.2 convert_reduce_fusion
  51.4 17.7 %all-to-all-done.2.got_ref = bf16[64,32,128]{2,1,0:T(8,128)(2,1)S(1)} async-done(((bf16[64,32,128]{2,1,0:T(8,128)(2,1)}), bf16[64,32,128]{2,1,0:T(8,128)(2,1)S(1)}, u32[]{:S(2)}, u32[]{:S(2)}) %all-to-all-start.2) | async-done | bytes 524320 | tf_op jit(solution)/shard_map/all_to_all | solution.py:451
  69.1 4.9 %shard_map.127 = (f32[8,8,512]{2,1,0:T(8,128)}, f32[512,128]{1,0:T(8,128)}) custom-call(s32[8]{0:T(128)S(1)} %multiply_add_fusion.slot_ref, bf16[64,32,128]{2,1,0:T(8,128)(2,1)S(1)} %all-to-all-done.2.got_ref, bf16[8,128,512]{2,1,0:T(8,128)(2,1)S(1)} %get-tuple-element.6.row_wave_ref, f32[8,64,512]{2,1,0:T(8,128)S(1)} %get-tuple-element.7.column_wave_ref, ...), custom_call_target="tpu_custom_call" | custom-call | tf_op jit(solution)/shard_map/pallas_call | solution.py:457
  74.0 5.4 %all-to-all-start.3 = ((f32[64,8,128]{2,1,0:T(8,128)}), f32[64,8,128]{2,1,0:T(8,128)S(1)}, u32[]{:S(2)}, u32[]{:S(2)}) async-start(f32[64,8,128]{2,1,0:T(8,128)} %bitcast.7), calls=%async_computation.3 | async-start | bytes 524288 | tf_op jit(solution)/shard_map/all_to_all | solution.py:451
  79.4 0.1 broadcast_in_dim_reshape.15.second_row_ref
  79.5 0.1 broadcast_in_dim_reshape.14.first_row_ref
  79.6 13.3 %all-to-all-done.3 = f32[64,8,128]{2,1,0:T(8,128)S(1)} async-done(((f32[64,8,128]{2,1,0:T(8,128)}), f32[64,8,128]{2,1,0:T(8,128)S(1)}, u32[]{:S(2)}, u32[]{:S(2)}) %all-to-all-start.3) | async-done | bytes 262176 | tf_op jit(solution)/shard_map/all_to_all | solution.py:451
  92.9 0.6 shard_map.128
  93.5 9.9 %all_to_all.30.parts_ref = f32[8,64,128]{2,1,0:T(8,128)S(1)} all-to-all(f32[8,64,128]{2,1,0:T(8,128)S(1)} %bitcast.17), channel_id=1, replica_groups=mesh['z'=8,'x'=4,'core'=2,'tile'=8] {'x','core'}, dimensions={0} | all-to-all | bytes 524288 | tf_op jit(solution)/shard_map/all_to_all | solution.py:451
  103.5 18.7 %all_to_all.31.parts_ref = f32[64,8,128]{2,1,0:T(8,128)S(1)} all-to-all(f32[64,8,128]{2,1,0:T(8,128)S(1)} %shard_map.129), channel_id=1, replica_groups=mesh['z'=8,'x'=4,'core'=2,'tile'=8] {'z','tile'}, dimensions={0} | all-to-all | bytes 524288 | tf_op jit(solution)/shard_map/all_to_all | solution.py:451
  122.2 1.0 shard_map.130
  (11 shorter events, 0.1 us)
Async XLA Ops:
  2.2 28.0 %all-to-all-start = ((f32[64,2,128]{2,1,0:T(2,128)}), f32[64,2,128]{2,1,0:T(2,128)S(1)}, u32[]{:S(2)}, u32[]{:S(2)}) async-start(f32[64,2,128]{2,1,0:T(2,128)} %shard_map.122), calls=%async_computation | async-start | bytes 131072 | tf_op jit(solution)/shard_map/all_to_all | solution.py:451
  31.0 11.9 %all-to-all-start.1 = ((f32[8,64,128]{2,1,0:T(8,128)}), f32[8,64,128]{2,1,0:T(8,128)S(1)}, u32[]{:S(2)}, u32[]{:S(2)}) async-start(f32[8,64,128]{2,1,0:T(8,128)} %shard_map.123), calls=%async_computation.1 | async-start | bytes 524288 | tf_op jit(solution)/shard_map/all_to_all | solution.py:451
  35.3 1.0 copy-start
  44.2 5.6 %copy-start.2 = (f32[8,2,512]{2,1,0:T(2,128)S(1)}, f32[8,2,512]{2,1,0:T(2,128)}, u32[]{:S(2)}) copy-start(f32[8,2,512]{2,1,0:T(2,128)} %uv_ref.1) | copy-start | bytes 98308
  44.2 7.0 %copy-start.5 = (s32[8,2]{0,1:T(2,128)S(1)}, s32[8,2]{0,1:T(2,128)}, u32[]{:S(2)}) copy-start(s32[8,2]{0,1:T(2,128)} %param.15) | copy-start | bytes 196
  44.2 24.9 %copy-start.1 = (bf16[384,256]{1,0:T(8,128)(2,1)S(1)}, bf16[384,256]{1,0:T(8,128)(2,1)}, u32[]{:S(2)}) copy-start(bf16[384,256]{1,0:T(8,128)(2,1)} %constant.21.clone.cols_ref) | copy-start | bytes 589828
  44.2 24.9 %all-to-all-start.2 = ((bf16[64,32,128]{2,1,0:T(8,128)(2,1)}), bf16[64,32,128]{2,1,0:T(8,128)(2,1)S(1)}, u32[]{:S(2)}, u32[]{:S(2)}) async-start(bf16[64,32,128]{2,1,0:T(8,128)(2,1)} %shard_map.125), calls=%async_computation.2 | async-start | bytes 1048576 | tf_op jit(solution)/shard_map/all_to_all | solution.py:451
  49.7 19.4 %copy-start.3 = (f32[32,128]{1,0:T(8,128)S(1)}, f32[32,128]{1,0:T(8,128)}, u32[]{:S(2)}) copy-start(f32[32,128]{1,0:T(8,128)} %constant.22.clone.taper_ref) | copy-start | bytes 49156
  49.7 19.4 %copy-start.4 = (bf16[64,96]{1,0:T(8,128)(2,1)S(1)}, bf16[64,96]{1,0:T(8,128)(2,1)}, u32[]{:S(2)}) copy-start(bf16[64,96]{1,0:T(8,128)(2,1)} %constant.20.clone.rows_ref) | copy-start | bytes 36868
  74.0 18.8 %all-to-all-start.3 = ((f32[64,8,128]{2,1,0:T(8,128)}), f32[64,8,128]{2,1,0:T(8,128)S(1)}, u32[]{:S(2)}, u32[]{:S(2)}) async-start(f32[64,8,128]{2,1,0:T(8,128)} %bitcast.7), calls=%async_computation.3 | async-start | bytes 524288 | tf_op jit(solution)/shard_map/all_to_all | solution.py:451
